TPU v7x, 32 devices: a whole 2x2x4 slice. The times are simulated.
32 devices in a mesh: groups: 2 (over y), ctx: 4 (over x, core), head: 4 (over z).
Axes of the slice: x: 2, y: 2, z: 4, core: 2. Of those that a mesh axis runs over, the one named last changes fastest.
Arguments:
- queries: bfloat16 [1024, 12288], P(('groups', 'ctx'), 'head'), parts along dimension 0, may hold values from -8 to 8
- latent: bfloat16 [65536, 576], P(('groups', 'ctx')), parts along dimension 0, may hold values from -8 to 8
- selection: int32 [8, 64], P(('groups', 'ctx')), parts along dimension 0, may hold values from 0 to 511, as said below
- span_offset: int32 [2], P('groups'), parts along dimension 0, may hold values from 24576 to 32256, as said below
- w_absorb: bfloat16 [64, 128, 512], P('head'), may hold values from -0.5 to 0.5
- w_value: bfloat16 [64, 512, 128], P('head'), may hold values from -4 to 4
- w_out: bfloat16 [8192, 7168], P('head', 'ctx'), may hold values from -0.0625 to 0.0625
Outputs:
- attention_out: bfloat16 [1024, 7168], P(('groups', 'head'), 'ctx'), parts along dimension 0
There are 2 independent parts, one for each index of `groups`. A program takes and returns all parts, laid end to end along the dimension named above; an argument that names none is the same for every part. Nothing has to cross between parts.
Inputs may be any that keep to these rules, and one draw needn't show every extreme that they name: `selection`: row q lists 64 distinct latent blocks, among them block 0. Blocks j * 128 to (j + 1) * 128 - 1 lie on index j of ctx; at most 24 blocks of a row lie on one index, and some index holds exactly 24 blocks of every row. `span_offset`: A multiple of 64.
All inputs are finite; a program needn't handle non-finite values.
Results may differ from a plain program's by a relative error of at most 0.015.
Values may be sent and summed in bfloat16 or wider, within the bound.
No kernel may reach another device: no remote copies, remote signals or barrier semaphores. Data moves between devices by JAX's collectives and lax.ppermute only.
A program may use at most 192 MiB of HBM per device.

v0:
```python
import jax
import jax.numpy as jnp
from jax import lax
from jax.sharding import PartitionSpec as P

NOPE = 128
ROPE = 64
BT = 64
TOPK = 64


def slot_table(blocks, owners, slot_depth, blocks_held):
    owner = blocks // blocks_held
    local_index = blocks % blocks_held
    marks = (owner[:, None] == jnp.arange(owners)[None, :]).astype(jnp.int32)
    before = jnp.cumsum(marks, axis=0) - marks
    standing = jnp.sum(before * marks, axis=1)
    slot_index = owner * slot_depth + standing
    slot_cells = jnp.arange(owners * slot_depth)
    matches = (slot_index[None, :] == slot_cells[:, None]).astype(jnp.int32)
    slot_rows = jnp.sum(matches * (local_index[None, :] + 1), axis=1) - 1
    return (slot_rows.reshape(owners, slot_depth), slot_index)


def body(queries, latent, selection, span_offset, w_absorb, w_value, w_out):
    owners = lax.axis_size("ctx")
    my_index = lax.axis_index("ctx")
    slot_depth = 3 * TOPK // (2 * owners)
    blocks_held = latent.shape[0] // BT
    row_width = latent.shape[1]
    blocks = selection[0]
    slot_rows, slot_index = slot_table(blocks, owners, slot_depth, blocks_held)
    wanted = lax.all_to_all(slot_rows, "ctx", split_axis=0, concat_axis=0, tiled=True)
    filled = wanted >= 0
    local_index = jnp.maximum(wanted, 0)
    stored = latent.reshape(blocks_held, BT, row_width)
    packed = jnp.where(filled[:, :, None, None], stored[local_index], jnp.zeros((), latent.dtype))
    arrived = lax.all_to_all(packed, "ctx", split_axis=0, concat_axis=0, tiled=True)
    arrived_pool = arrived.reshape(owners * slot_depth, BT, row_width)
    key_rows = arrived_pool[slot_index].reshape(TOPK * BT, row_width)
    key_position = (blocks[:, None] * BT + jnp.arange(BT, dtype=jnp.int32)[None, :]).reshape(-1)
    query_rows = queries.shape[0]
    query_position = (
        span_offset[0] + my_index * query_rows + jnp.arange(query_rows, dtype=jnp.int32)
    )
    visible = key_position[None, :] <= query_position[:, None]
    local_heads = w_absorb.shape[0]
    nope_width = w_absorb.shape[1]
    latent_width = w_absorb.shape[2]
    grouped = queries.reshape(query_rows, local_heads, -1)
    q_latent = jnp.einsum(
        "qhd,hdl->hql", grouped[:, :, :nope_width], w_absorb, preferred_element_type=jnp.float32
    ).astype(jnp.bfloat16)
    q_full = jnp.concatenate(
        [q_latent, jnp.transpose(grouped[:, :, nope_width:], (1, 0, 2))], axis=2
    )
    q_full = q_full.reshape(local_heads * query_rows, row_width)
    softmax_scale = (NOPE + ROPE) ** (-0.5)
    scores = (
        lax.dot_general(
            q_full, key_rows, (((1,), (1,)), ((), ())), preferred_element_type=jnp.float32
        )
        * softmax_scale
    )
    scores = scores.reshape(local_heads, query_rows, -1)
    scores = jnp.where(visible[None, :, :], scores, -jnp.inf)
    row_peak = jnp.max(scores, axis=-1, keepdims=True)
    shifted = jnp.exp(scores - row_peak)
    weights = (shifted / jnp.sum(shifted, axis=-1, keepdims=True)).astype(jnp.bfloat16)
    mixed_latent = jnp.dot(
        weights.reshape(local_heads * query_rows, -1),
        key_rows[:, :latent_width],
        preferred_element_type=jnp.float32,
    ).astype(jnp.bfloat16)
    head_out = jnp.einsum(
        "hql,hlv->qhv",
        mixed_latent.reshape(local_heads, query_rows, latent_width),
        w_value,
        preferred_element_type=jnp.float32,
    ).astype(jnp.bfloat16)
    head_out = head_out.reshape(query_rows, -1)
    gathered = lax.all_gather(head_out, "ctx", axis=0, tiled=True)
    return lax.psum_scatter(
        jnp.dot(gathered, w_out, preferred_element_type=jnp.float32).astype(jnp.bfloat16),
        "head",
        scatter_dimension=0,
        tiled=True,
    )


def solution(mesh):
    placed = (
        P(("groups", "ctx"), "head"),
        P(("groups", "ctx"), None),
        P(("groups", "ctx"), None),
        P("groups"),
        P("head", None, None),
        P("head", None, None),
        P("head", "ctx"),
    )
    return jax.shard_map(
        body, mesh=mesh, in_specs=placed, out_specs=P(("groups", "head"), "ctx"), check_vma=False
    )
```

profile of v0, /device:TPU:0, one launch (start us, length us, event | category | flops | bytes accessed | tf_op | source)
XLA Modules:
  0.0 296.4 jit_solution(5574957410722731380)
XLA Ops:
  6.5 0.0 copy-start
  6.5 0.8 bitcast_multiply_fusion
  7.3 0.1 fusion.8
  7.4 0.1 reduce_window_sum.11
  7.5 0.2 select_reduce_fusion.1
  7.7 0.7 fusion.12
  8.4 0.1 select_reduce_fusion
  8.5 0.7 sub.33
  9.2 4.2 %all-to-all-start = ((s32[4,1,24]{2,1,0:T(1,128)}), s32[4,1,24]{2,1,0:T(1,128)S(1)}, u32[]{:S(2)}, u32[]{:S(2)}) async-start(s32[4,1,24]{2,1,0:T(1,128)} %bitcast.9), calls=%async_computation | async-start | bytes 4096 | tf_op jit(solution)/shard_map/all_to_all | solution.py:33
  13.4 14.1 %copy.30 = bf16[8192,576]{1,0:T(8,128)(2,1)} copy(bf16[8192,576]{0,1:T(8,128)(2,1)} %param.8) | data formatting | bytes 18874368 | tf_op args[1]
  27.5 0.0 all-to-all-done
  27.5 0.1 reshape.234
  27.6 11.0 %gather_fusion = bf16[96,64,576]{2,1,0:T(8,128)(2,1)} fusion(bf16[128,64,576]{2,1,0:T(8,128)(2,1)} %bitcast.68, s32[1024]{0:T(1024)S(1)} %pad_clamp_fusion.1), kind=kCustom, calls=%fused_computation | custom fusion | bytes 14156160 | tf_op jit(solution)/shard_map/gather | solution.py:37
  38.5 7.2 %broadcast_select_fusion = bf16[4,24,64,576]{3,2,1,0:T(8,128)(2,1)} fusion(bf16[4,24,64,576]{3,2,1,0:T(8,128)(2,1)} %bitcast.69, pred[4,24]{1,0:T(4,128)(4,1)S(1)} %bitcast.78), kind=kLoop, calls=%fused_computation.7 | loop fusion | flops 3538944 | bytes 14155872 | tf_op jit(solution)/shard_map/jit(_where)/select_n | solution.py:37
  45.7 0.0 copy-start.4
  45.7 5.7 %all-to-all-start.1 = ((bf16[4,24,64,576]{3,2,1,0:T(8,128)(2,1)}), bf16[4,24,64,576]{3,2,1,0:T(8,128)(2,1)}, u32[]{:S(2)}, u32[]{:S(2)}) async-start(bf16[4,24,64,576]{3,2,1,0:T(8,128)(2,1)} %broadcast_select_fusion), calls=%async_computation.1 | async-start | bytes 15728640 | tf_op jit(solution)/shard_map/all_to_all | solution.py:38
  51.4 0.0 all-gather.2.cloned.1.call-start
  52.1 0.1 iota_add_fusion
  52.2 0.1 add.101
  52.2 1.5 copy.26
  53.7 0.7 slice.17
  54.5 1.2 copy.35
  55.7 0.0 copy-done.4
  55.8 0.0 copy-done
  55.8 0.8 convolution_convert_fusion.1
  56.5 1.8 pad_maximum_fusion
  58.3 0.4 broadcast_compare_fusion
  58.7 80.3 %all-to-all-done.1 = bf16[4,24,64,576]{3,2,1,0:T(8,128)(2,1)} async-done(((bf16[4,24,64,576]{3,2,1,0:T(8,128)(2,1)}), bf16[4,24,64,576]{3,2,1,0:T(8,128)(2,1)}, u32[]{:S(2)}, u32[]{:S(2)}) %all-to-all-start.1) | async-done | bytes 7077920 | tf_op jit(solution)/shard_map/all_to_all | solution.py:38
  138.9 6.8 %gather_fusion.1 = bf16[64,64,576]{2,1,0:T(8,128)(2,1)} fusion(bf16[96,64,576]{2,1,0:T(8,128)(2,1)} %bitcast.12, s32[1024]{0:T(1024)S(1)} %pad_clamp_fusion), kind=kCustom, calls=%fused_computation.1 | custom fusion | bytes 9437440 | tf_op jit(solution)/shard_map/gather | solution.py:40
  145.7 23.0 %fusion = (f32[2048]{0:T(1024)S(1)}, f32[2048,4096]{1,0:T(8,128)}) fusion(pred[128,4096]{1,0:T(8,128)(4,1)S(1)} %broadcast_compare_fusion, bf16[2048,576]{1,0:T(8,128)(2,1)} %bitcast.72, bf16[4096,576]{1,0:T(8,128)(2,1)} %bitcast.70), kind=kOutput, calls=%fused_computation.5 | convolution fusion | flops 9688840192 | bytes 41164800 | tf_op jit(solution)/shard_map/dot_general | solution.py:60
  168.7 0.0 copy-start.2
  168.7 17.2 %fusion.1 = f32[2048]{0:T(1024)S(1)} fusion(f32[2048,4096]{1,0:T(8,128)} %get-tuple-element.10, f32[2048]{0:T(1024)S(1)} %get-tuple-element.9, pred[128,4096]{1,0:T(8,128)(4,1)S(1)} %broadcast_compare_fusion), kind=kLoop, calls=%fused_computation.6 | loop fusion | flops 33552384 | bytes 34095104 | tf_op jit(solution)/shard_map/reduce_sum | solution.py:69
  185.9 3.0 %copy-done.2 = f32[2048,4096]{1,0:T(8,128)S(1)} copy-done((f32[2048,4096]{1,0:T(8,128)S(1)}, f32[2048,4096]{1,0:T(8,128)}, u32[]{:S(2)}) %copy-start.2) | copy-done | bytes 33554456
  189.0 12.7 %divide_convert_fusion = bf16[2048,4096]{1,0:T(8,128)(2,1)} fusion(f32[2048,4096]{1,0:T(8,128)S(1)} %copy-done.2, f32[2048]{0:T(1024)S(1)} %fusion.1, f32[2048]{0:T(1024)S(1)} %get-tuple-element.9, pred[128,4096]{1,0:T(8,128)(4,1)S(1)} %broadcast_compare_fusion), kind=kLoop, calls=%fused_computation.2 | loop fusion | flops 41943040 | bytes 50872320 | tf_op jit(solution)/shard_map/convert_element_type | solution.py:69
  201.7 0.0 copy-start.3
  201.7 13.9 %fusion.4 = bf16[2048,512]{1,0:T(8,128)(2,1)S(1)} fusion(bf16[2048,4096]{1,0:T(8,128)(2,1)} %divide_convert_fusion, bf16[4096,576]{1,0:T(8,128)(2,1)} %bitcast.71), kind=kOutput, calls=%fused_computation.11 | convolution fusion | flops 8590983168 | bytes 23068672 | tf_op jit(solution)/shard_map/dot_general | solution.py:70
  215.6 0.0 copy-done.3
  215.6 1.6 convolution_convert_fusion.2
  217.2 0.0 all-gather.2.cloned.1.call-update
  217.2 0.0 copy-start.1
  217.2 0.0 reduce-scatter.2.cloned.1.call-start
  217.3 23.7 %all-gather.2.cloned.1.call-done = bf16[512,2048]{0,1:T(8,128)(2,1)} async-done(((bf16[128,2048]{0,1:T(8,128)(2,1)}), bf16[512,2048]{0,1:T(8,128)(2,1)}) %all-gather.2.cloned.1.call-update) | async-done | bytes 2097168 | tf_op jit(solution)/shard_map/all_gather | solution.py:82
  241.0 9.0 %convolution_convert_fusion = bf16[512,1792]{1,0:T(8,128)(2,1)} fusion(bf16[512,2048]{0,1:T(8,128)(2,1)} %all-gather.2.cloned.1.call-done, bf16[2048,1792]{1,0:T(8,128)(2,1)} %param.13), kind=kOutput, calls=%fused_computation.10 | convolution fusion | flops 3759013888 | bytes 11272192 | tf_op jit(solution)/shard_map/dot_general | solution.py:84
  250.0 0.0 reduce-scatter.2.cloned.1.call-update
  250.0 39.6 %reduce-scatter.2.cloned.1.call-done = bf16[128,1792]{1,0:T(8,128)(2,1)} async-done(((bf16[512,1792]{1,0:T(8,128)(2,1)}), bf16[128,1792]{1,0:T(8,128)(2,1)}) %reduce-scatter.2.cloned.1.call-update) | async-done | bytes 458768 | tf_op jit(solution)/shard_map/reduce_scatter | solution.py:83
  289.6 0.0 copy-done.1
  (8 shorter events, 0.1 us)
Async XLA Ops:
  6.5 49.2 %copy-start = (bf16[16,128,512]{2,1,0:T(8,128)(2,1)S(1)}, bf16[16,128,512]{2,1,0:T(8,128)(2,1)}, u32[]{:S(2)}) copy-start(bf16[16,128,512]{2,1,0:T(8,128)(2,1)} %param.11) | copy-start | bytes 6291460
  9.2 18.3 %all-to-all-start = ((s32[4,1,24]{2,1,0:T(1,128)}), s32[4,1,24]{2,1,0:T(1,128)S(1)}, u32[]{:S(2)}, u32[]{:S(2)}) async-start(s32[4,1,24]{2,1,0:T(1,128)} %bitcast.9), calls=%async_computation | async-start | bytes 4096 | tf_op jit(solution)/shard_map/all_to_all | solution.py:33
  45.7 10.0 %copy-start.4 = (s32[1,64]{1,0:T(1,128)S(1)}, s32[1,64]{1,0:T(1,128)}, u32[]{:S(2)}) copy-start(s32[1,64]{1,0:T(1,128)} %param.9) | copy-start | bytes 772
  45.7 93.2 %all-to-all-start.1 = ((bf16[4,24,64,576]{3,2,1,0:T(8,128)(2,1)}), bf16[4,24,64,576]{3,2,1,0:T(8,128)(2,1)}, u32[]{:S(2)}, u32[]{:S(2)}) async-start(bf16[4,24,64,576]{3,2,1,0:T(8,128)(2,1)} %broadcast_select_fusion), calls=%async_computation.1 | async-start | bytes 15728640 | tf_op jit(solution)/shard_map/all_to_all | solution.py:38
  51.4 189.6 %all-gather.2.cloned.1.call-start = ((), (), s32[]{:S(2)}) async-start(), calls=%async_computation.3 | async-start | bytes 2621440 | tf_op jit(solution)/shard_map/all_gather | solution.py:82
  168.7 20.2 %copy-start.2 = (f32[2048,4096]{1,0:T(8,128)S(1)}, f32[2048,4096]{1,0:T(8,128)}, u32[]{:S(2)}) copy-start(f32[2048,4096]{1,0:T(8,128)} %get-tuple-element.10) | copy-start | bytes 100663296
  201.7 13.9 %copy-start.3 = (bf16[16,512,128]{2,1,0:T(8,128)(2,1)S(1)}, bf16[16,512,128]{2,1,0:T(8,128)(2,1)}, u32[]{:S(2)}) copy-start(bf16[16,512,128]{2,1,0:T(8,128)(2,1)} %param.12) | copy-start | bytes 6291460
  217.2 72.4 %copy-start.1 = (bf16[16,128,512]{2,1,0:T(8,128)(2,1)S(1)}, bf16[16,128,512]{2,1,0:T(8,128)(2,1)}, u32[]{:S(2)}) copy-start(bf16[16,128,512]{2,1,0:T(8,128)(2,1)} %param.11) | copy-start | bytes 6291460
  217.2 72.4 %reduce-scatter.2.cloned.1.call-start = ((), (), s32[]{:S(2)}) async-start(), calls=%async_computation.4 | async-start | bytes 2293760 | tf_op jit(solution)/shard_map/reduce_scatter | solution.py:83
Sparse Core Ops, SparseCore 0:
  217.3 23.6 all-gather.1
  250.2 39.4 reduce-scatter.1
where the time goes:
time: 297 us; the launch traced here: 296 us
  waiting for transfers between devices  144 us (48%)
  matrix products  48.2 us (16%)
  other arithmetic  41.3 us (14%)
  local copies, waits for them, and re-layouts  39.2 us (13%)
  between operations  14.2 us (5%)
  starting transfers between devices  9.95 us (3%)
    all_to_all x1, waiting for transfers between devices, body(): lax.all_to_all(packed, 'ctx', split_axis=0, concat_axis=0, tiled=True)  80.3 us
    reduce_scatter x1, waiting for transfers between devices, body(): lax.psum_scatter(jnp.dot(gathered, w_out, preferred_element_type=jnp.floa...  39.6 us
    all_gather x1, waiting for transfers between devices, body(): gathered = lax.all_gather(head_out, 'ctx', axis=0, tiled=True)  23.7 us
    dot_general x1, matrix products, body(): lax.dot_general(q_full, key_rows, (((1,), (1,)), ((), ())), preferred_ele...  23 us
    unnamed x14, local copies, waits for them, and re-layouts  19.9 us
    reduce_sum x1, other arithmetic, body(): jnp.sum(shifted, axis=-1, keepdims=True)  17.2 us
    dot_general x1, matrix products, body(): jnp.dot(weights.reshape(local_heads * query_rows, -1), key_rows[:, :laten...  13.9 us
    convert_element_type x1, other arithmetic, body(): (shifted / jnp.sum(shifted, axis=-1, keepdims=True)).astype(jnp.bfloat16)  12.7 us
  transfers between devices with their start and end apart: 4, of which 3 were waited for; matrix products, arithmetic and copies ran while one was open for 7% of the time, Pallas kernels for 0%

commit v1 on v0

v1 whole, which is shorter than its diff:
```python
import functools
import math

import jax
import jax.numpy as jnp
from jax import lax
from jax.experimental import pallas as pl
from jax.experimental.pallas import tpu as pltpu
from jax.sharding import PartitionSpec as P

BT = 64
CHUNK = 8
ROW_TILE = 512
NEVER = -1e30
FAR = 1 << 30


def attend_kernel(
    blocks_held, depth, sources, offset,
    meta, q_ref, wa_hbm, own_hbm, sib_hbm, wv_hbm, o_ref,
    kv, q_full, wa, wv, acc, place, edge, kv_sem, wa_sem, wv_sem,
):
    tokens = q_ref.shape[0]
    heads, nope, lat = wa.shape
    width = kv.shape[1]
    vd = wv.shape[2]
    head_width = nope + width - lat
    slots = kv.shape[0] // BT
    step = CHUNK * BT
    fold = head_width ** -0.5 * math.log2(math.e)
    first = meta[64] + offset
    mine = meta[65]
    other = meta[66]

    wa_copy = pltpu.make_async_copy(wa_hbm, wa, wa_sem)
    wv_copy = pltpu.make_async_copy(wv_hbm, wv, wv_sem)
    wa_copy.start()

    def fetch(block, slot):
        owner = block // blocks_held
        row = pl.multiple_of((block % blocks_held) * BT, BT)
        target = kv.at[pl.ds(pl.multiple_of(slot * BT, BT), BT), :]
        if "own" in sources:
            @pl.when(owner == mine)
            def _():
                pltpu.make_async_copy(own_hbm.at[pl.ds(row, BT), :], target, kv_sem).start()
        if "sib" in sources:
            @pl.when(owner == other)
            def _():
                pltpu.make_async_copy(sib_hbm.at[pl.ds(row, BT), :], target, kv_sem).start()

    def scan(j, carry):
        full, part = carry
        block = meta[j]
        owner = block // blocks_held
        here = jnp.bool_(False)
        if "own" in sources:
            here = here | (owner == mine)
        if "sib" in sources:
            here = here | (owner == other)
        whole = here & (block * BT + BT - 1 <= first)
        some = here & (block * BT + BT - 1 > first) & (block * BT <= first + tokens - 1)

        @pl.when(whole)
        def _():
            fetch(block, full)

        @pl.when(some)
        def _():
            edge[part] = block

        return full + whole.astype(jnp.int32), part + some.astype(jnp.int32)

    full, part = lax.fori_loop(0, 64, scan, (jnp.int32(0), jnp.int32(0)))

    def fetch_edge(i, _):
        fetch(edge[i], full + i)
        place[full + i] = edge[i] * BT
        return 0

    lax.fori_loop(0, part, fetch_edge, 0)
    count = full + part
    chunks = jnp.maximum((count + CHUNK - 1) // CHUNK, 1)

    def fill(i, _):
        target = kv.at[pl.ds(pl.multiple_of(i * BT, BT), BT), :]
        pltpu.make_async_copy(own_hbm.at[pl.ds(0, BT), :], target, kv_sem).start()
        place[i] = FAR
        return 0

    lax.fori_loop(count, chunks * CHUNK, fill, 0)
    plain = full // CHUNK

    def clear(i, _):
        place[i] = 0
        return 0

    lax.fori_loop(plain * CHUNK, full, clear, 0)
    wv_copy.start()

    wa_copy.wait()
    for h in range(heads):
        base = h * head_width
        latent_part = jnp.dot(
            q_ref[:, base : base + nope], wa[h], preferred_element_type=jnp.float32
        )
        rows = slice(h * tokens, (h + 1) * tokens)
        q_full[rows, 0:lat] = (latent_part * fold).astype(jnp.bfloat16)
        turned = q_ref[:, base + nope : base + head_width].astype(jnp.float32)
        q_full[rows, lat:width] = (turned * fold).astype(jnp.bfloat16)

    def land(i, _):
        pltpu.make_async_copy(own_hbm.at[pl.ds(0, BT), :], kv.at[pl.ds(0, BT), :], kv_sem).wait()
        return 0

    lax.fori_loop(0, chunks * CHUNK, land, 0)
    wv_copy.wait()

    tile = min(ROW_TILE, heads * tokens)
    tile_heads = tile // tokens
    lane = lax.broadcasted_iota(jnp.int32, (tokens, 128), 1)

    def row_tile(r, lse_tile):
        row0 = pl.multiple_of(r * tile, tile)
        acc[...] = jnp.zeros_like(acc)

        def chunk(masked, c, carry):
            peak, total = carry
            keys = pl.ds(pl.multiple_of(c * step, step), step)
            scores = lax.dot_general(
                q_full[pl.ds(row0, tile), :], kv[keys, :], (((1,), (1,)), ((), ())),
                preferred_element_type=jnp.float32,
            )
            if masked:
                column = lax.broadcasted_iota(jnp.int32, (tokens, step), 1)
                position = jnp.zeros((tokens, step), jnp.int32)
                for b in range(CHUNK):
                    position = jnp.where(
                        column // BT == b, place[c * CHUNK + b] + column % BT, position
                    )
                query = first + lax.broadcasted_iota(jnp.int32, (tokens, step), 0)
                visible = position <= query
                scores = jnp.where(
                    visible[None], scores.reshape(tile_heads, tokens, step), NEVER
                ).reshape(tile, step)
            new_peak = jnp.maximum(peak, jnp.max(scores, axis=1, keepdims=True))
            raised = jnp.exp2(scores - new_peak)
            keep = jnp.exp2(peak - new_peak)
            total = total * keep
            for n in range(step // 128):
                total = total + raised[:, n * 128 : (n + 1) * 128]
            acc[...] = acc[...] * keep + jnp.dot(
                raised.astype(jnp.bfloat16), kv[keys, 0:lat], preferred_element_type=jnp.float32
            )
            return new_peak, total

        carry = (jnp.full((tile, 1), NEVER, jnp.float32), jnp.zeros((tile, 128), jnp.float32))
        carry = lax.fori_loop(0, plain, functools.partial(chunk, False), carry)
        peak, total = lax.fori_loop(plain, chunks, functools.partial(chunk, True), carry)
        total = jnp.sum(total, axis=1, keepdims=True)
        lse = peak + jnp.log2(total)
        scale = 1.0 / total
        for i in range(tile_heads):
            h = r * tile_heads + i
            rows = slice(i * tokens, (i + 1) * tokens)
            mixed = (acc[rows, :] * scale[rows, :]).astype(jnp.bfloat16)
            out = jnp.dot(mixed, wv[h], preferred_element_type=jnp.float32)
            o_ref[:, pl.ds(pl.multiple_of(h * vd, vd), vd)] = out.astype(jnp.bfloat16)
            value = lse[rows, :]
            high = value.astype(jnp.bfloat16).astype(jnp.float32)
            middle = (value - high).astype(jnp.bfloat16).astype(jnp.float32)
            low = value - high - middle
            lse_tile = jnp.where(lane == h, high, lse_tile)
            lse_tile = jnp.where(lane == h + 32, middle, lse_tile)
            lse_tile = jnp.where(lane == h + 64, low, lse_tile)
        return lse_tile

    lse_tile = lax.fori_loop(
        0, heads * tokens // tile, row_tile, jnp.zeros((tokens, 128), jnp.float32)
    )
    o_ref[:, heads * vd :] = lse_tile.astype(jnp.bfloat16)


def attend(meta, queries, own, sib, w_absorb, w_value, depth, sources, offset=0):
    tokens = queries.shape[0]
    heads, nope, lat = w_absorb.shape
    vd = w_value.shape[2]
    width = own.shape[1]
    slots = -(-depth * len(sources) // CHUNK) * CHUNK
    rows = heads * tokens
    tile = min(ROW_TILE, rows)
    keys = depth * len(sources) * BT * 2 // 3
    any_space = pl.BlockSpec(memory_space=pl.ANY)
    vmem = pl.BlockSpec(memory_space=pltpu.VMEM)
    return pl.pallas_call(
        functools.partial(attend_kernel, own.shape[0] // BT, depth, sources, offset),
        out_shape=jax.ShapeDtypeStruct((tokens, heads * vd + 128), jnp.bfloat16),
        in_specs=[
            pl.BlockSpec(memory_space=pltpu.SMEM), vmem, any_space, any_space, any_space, any_space,
        ],
        out_specs=vmem,
        scratch_shapes=[
            pltpu.VMEM((slots * BT, width), jnp.bfloat16),
            pltpu.VMEM((rows, width), jnp.bfloat16),
            pltpu.VMEM(w_absorb.shape, jnp.bfloat16),
            pltpu.VMEM(w_value.shape, jnp.bfloat16),
            pltpu.VMEM((tile, lat), jnp.float32),
            pltpu.SMEM((slots,), jnp.int32),
            pltpu.SMEM((64,), jnp.int32),
            pltpu.SemaphoreType.DMA,
            pltpu.SemaphoreType.DMA,
            pltpu.SemaphoreType.DMA,
        ],
        compiler_params=pltpu.CompilerParams(vmem_limit_bytes=40 * 1024 * 1024),
        cost_estimate=pl.CostEstimate(
            flops=2 * rows * keys * (width + lat),
            bytes_accessed=2 * keys * width * 2,
            transcendentals=rows * keys,
        ),
    )(meta, queries, w_absorb, own, sib, w_value)


def split_partial(partial, heads):
    values = partial[:, :-128].astype(jnp.float32).reshape(partial.shape[0], heads, -1)
    tail = partial[:, -128:].astype(jnp.float32)
    lse = tail[:, 0:heads] + tail[:, 32 : 32 + heads] + tail[:, 64 : 64 + heads]
    return values, lse


def combine(partials, heads):
    parts = [split_partial(p, heads) for p in partials]
    peak = functools.reduce(jnp.maximum, [lse for _, lse in parts])
    shares = [jnp.exp2(lse - peak) for _, lse in parts]
    norm = 1.0 / functools.reduce(jnp.add, shares)
    mixed = sum(v * (s * norm)[:, :, None] for (v, _), s in zip(parts, shares))
    return mixed.reshape(mixed.shape[0], -1).astype(jnp.bfloat16)


def body(queries, latent, selection, span_offset, w_absorb, w_value, w_out):
    owners = lax.axis_size("ctx")
    me = lax.axis_index("ctx")
    chips = owners // 2
    depth = 3 * selection.shape[1] // (2 * owners)
    heads = w_absorb.shape[0]
    tokens = queries.shape[0]
    sibling = [(i, i ^ 1) for i in range(owners)]
    sib_latent = lax.ppermute(latent, "ctx", sibling)

    def meta_of(row, index):
        return jnp.concatenate(
            [row[0], jnp.stack([span_offset[0] + index * tokens, me, me ^ 1])]
        ).astype(jnp.int32)

    own_partials = [
        attend(meta_of(selection, me), queries, latent, latent, w_absorb, w_value, depth, ("own",)),
        attend(meta_of(selection, me), queries, latent, sib_latent, w_absorb, w_value, depth, ("sib",)),
    ]
    for turn in range(1, chips):
        ahead = [(i, (i + 2 * turn) % owners) for i in range(owners)]
        back = [(i, (i - 2 * turn) % owners) for i in range(owners)]
        far_queries = lax.ppermute(queries, "ctx", ahead)
        far_rows = lax.ppermute(selection, "ctx", ahead)
        index = (me - 2 * turn) % owners
        partial = attend(
            meta_of(far_rows, index), far_queries, latent, sib_latent, w_absorb, w_value, depth, ("own", "sib")
        )
        own_partials.append(lax.ppermute(partial, "ctx", back))
    head_out = combine(own_partials, heads)
    gathered = lax.all_gather(head_out, "ctx", axis=0, tiled=True)
    return lax.psum_scatter(
        jnp.dot(gathered, w_out, preferred_element_type=jnp.float32).astype(jnp.bfloat16),
        "head",
        scatter_dimension=0,
        tiled=True,
    )


def solution(mesh):
    placed = (
        P(("groups", "ctx"), "head"),
        P(("groups", "ctx"), None),
        P(("groups", "ctx"), None),
        P("groups"),
        P("head", None, None),
        P("head", None, None),
        P("head", "ctx"),
    )
    return jax.shard_map(
        body, mesh=mesh, in_specs=placed, out_specs=P(("groups", "head"), "ctx"), check_vma=False
    )
```

time: 297 us -> 190 us (0.64)
  waiting for transfers between devices: 144 us -> 67.2 us
  Pallas kernels: 0 us -> 60.6 us
  matrix products: 48.2 us -> 8.9 us
  other arithmetic: 41.3 us -> 2.41 us
  starting transfers between devices: 9.95 us -> 3.12 us
  local copies, waits for them, and re-layouts: 39.2 us -> 32.6 us
    all_to_all x2 -> x0, waiting for transfers between devices: 80.3 us -> none  [the longest x1 80.3 us: body(): lax.all_to_all(packed, 'ctx', split_axis=0, concat_axis=0, tiled=True)]
    pallas_call x0 -> x3, Pallas kernels: none -> 60.6 us  [attend(): pl.pallas_call(functools.partial(attend_kernel, own.shape[0] // BT, depth...]
    dot_general x4 -> x0, matrix products: 39.2 us -> none  [the longest x1 23 us: body(): lax.dot_general(q_full, key_rows, (((1,), (1,)), ((), ())), preferred_ele...]
    gather x2 -> x0, local copies, waits for them, and re-layouts: 17.8 us -> none  [the longest x1 11 us: body(): stored[local_index]]
    reduce_sum x3 -> x0, other arithmetic: 17.5 us -> none  [the longest x1 17.2 us: body(): jnp.sum(shifted, axis=-1, keepdims=True)]
    ppermute x0 -> x1, local copies, waits for them, and re-layouts: none -> 14.1 us  [body(): sib_latent = lax.ppermute(latent, 'ctx', sibling)]
    convert_element_type x2 -> x3, other arithmetic: 12.8 us -> 2 us  [the longest x1 1.98 us: combine(): return mixed.reshape(mixed.shape[0], -1).astype(jnp.bfloat16)]
    all_to_all x2 -> x0, starting transfers between devices: 9.87 us -> none  [the longest x1 5.66 us: body(): lax.all_to_all(packed, 'ctx', split_axis=0, concat_axis=0, tiled=True)]
  transfers between devices with their start and end apart: 4 -> 6, of which waited for: 3 -> 3; matrix products, arithmetic and copies ran while one was open for 7% -> 15% of each run, Pallas kernels for 0% -> 17%
where the time goes in v1:
time: 190 us; the launch traced here: 189 us
  waiting for transfers between devices  67.2 us (35%)
  Pallas kernels  60.6 us (32%)
  local copies, waits for them, and re-layouts  32.6 us (17%)
  between operations  14.2 us (7%)
  matrix products  8.9 us (5%)
  starting transfers between devices  3.12 us (2%)
  other arithmetic  2.41 us (1%)
    pallas_call x3, Pallas kernels, attend(): pl.pallas_call(functools.partial(attend_kernel, own.shape[0] // BT, depth...  60.6 us
    reduce_scatter x1, waiting for transfers between devices, body(): lax.psum_scatter(jnp.dot(gathered, w_out, preferred_element_type=jnp.floa...  39.6 us
    all_gather x1, waiting for transfers between devices, body(): gathered = lax.all_gather(head_out, 'ctx', axis=0, tiled=True)  27 us
    unnamed x13, local copies, waits for them, and re-layouts  17.5 us
    ppermute x1, local copies, waits for them, and re-layouts, body(): sib_latent = lax.ppermute(latent, 'ctx', sibling)  14.1 us
    dot_general x1, matrix products, body(): jnp.dot(gathered, w_out, preferred_element_type=jnp.float32)  8.9 us
  transfers between devices with their start and end apart: 6, of which 3 were waited for; matrix products, arithmetic and copies ran while one was open for 15% of the time, Pallas kernels for 17%

profile of v1, /device:TPU:0, one launch (start us, length us, event | category | flops | bytes accessed | tf_op | source)
XLA Modules:
  0.0 189.0 jit_solution(12880916686807597484)
XLA Ops:
  6.5 0.0 all-gather.2.cloned.1.call-start
  6.5 0.5 collective-permute-start
  7.0 2.5 %collective-permute-start.2 = (bf16[128,3072]{1,0:T(8,128)(2,1)}, bf16[128,3072]{1,0:T(8,128)(2,1)}, u32[]{:S(2)}, u32[]{:S(2)}) collective-permute-start(bf16[128,3072]{1,0:T(8,128)(2,1)} %q_ref.3), channel_id=1, source_target_pairs={{0,8},{4,12},{8,0},{12,4},{1,9},{5,13},{9,1},{13,5},{2,10},{6,14},... | collective-permute-start | bytes 2359304 | tf_op jit(solution)/shard_map/ppermute | solution.py:261
  9.5 0.1 collective-permute-start.1
  9.5 0.0 copy-start.5
  9.5 0.0 copy-start
  9.5 0.0 copy-start.4
  9.5 14.3 %copy.19.own_hbm.sib_hbm = bf16[8192,576]{1,0:T(8,128)(2,1)} copy(bf16[8192,576]{0,1:T(8,128)(2,1)} %param.8) | data formatting | bytes 18874368 | tf_op args[1]
  24.5 0.0 copy-done.5
  24.5 0.1 add_add_fusion.meta
  24.6 0.0 copy-done
  24.6 0.0 copy-done.4
  24.6 0.0 copy-start.1
  24.6 1.6 copy-done.1
  26.2 18.5 %shard_map.73 = bf16[128,2176]{1,0:T(8,128)(2,1)S(1)} custom-call(s32[67]{0:T(128)S(1)} %add_add_fusion.meta, bf16[128,3072]{1,0:T(8,128)(2,1)S(1)} %copy-done.4, bf16[16,128,512]{2,1,0:T(8,128)(2,1)S(1)} %copy-done, bf16[8192,576]{1,0:T(8,128)(2,1)} %copy.19.own_hbm.sib_hbm, bf16[8192,576]{1,0:T(8,128)(2,1)} %copy.19.own_hbm.sib_hbm, ...), custom_call_target="tpu_custom_call" | custom-call | flops 4563402752 | bytes 2359296 | tf_op jit(solution)/shard_map/pallas_call | solution.py:195
  44.7 0.0 collective-permute-done.1
  44.8 0.1 add_add_fusion.1.meta
  44.8 0.0 collective-permute-done
  44.8 14.1 %copy.22.sib_hbm = bf16[8192,576]{1,0:T(8,128)(2,1)} copy(bf16[8192,576]{0,1:T(8,128)(2,1)} %collective-permute-done) | data formatting | bytes 18874368 | tf_op jit(solution)/shard_map/ppermute | solution.py:247
  59.0 0.0 collective-permute-done.2.q_ref
  59.0 0.0 copy-start.2
  59.0 1.6 copy-done.2
  60.6 0.0 copy-start.3
  60.6 28.0 %shard_map.75 = bf16[128,2176]{1,0:T(8,128)(2,1)S(1)} custom-call(s32[67]{0:T(128)S(1)} %add_add_fusion.1.meta, bf16[128,3072]{1,0:T(8,128)(2,1)} %collective-permute-done.2.q_ref, bf16[16,128,512]{2,1,0:T(8,128)(2,1)S(1)} %copy-done, bf16[8192,576]{1,0:T(8,128)(2,1)} %copy.19.own_hbm.sib_hbm, bf16[8192,576]{1,0:T(8,128)(2,1)} %copy.22.sib_hbm, ...), custom_call_target="tpu_custom_call" | custom-call | flops 9126805504 | bytes 4718592 | tf_op jit(solution)/shard_map/pallas_call | solution.py:195
  88.6 0.1 collective-permute-start.3
  88.6 0.0 copy-done.3
  88.6 14.1 %shard_map.74 = bf16[128,2176]{1,0:T(8,128)(2,1)S(1)} custom-call(s32[67]{0:T(128)S(1)} %add_add_fusion.meta, bf16[128,3072]{1,0:T(8,128)(2,1)S(1)} %copy-done.4, bf16[16,128,512]{2,1,0:T(8,128)(2,1)S(1)} %copy-done, bf16[8192,576]{1,0:T(8,128)(2,1)} %copy.19.own_hbm.sib_hbm, bf16[8192,576]{1,0:T(8,128)(2,1)} %copy.22.sib_hbm, ...), custom_call_target="tpu_custom_call" | custom-call | flops 4563402752 | bytes 2359296 | tf_op jit(solution)/shard_map/pallas_call | solution.py:195
  102.7 0.7 collective-permute-done.3
  103.4 0.2 fusion.3
  103.6 0.1 fusion.4
  103.7 0.3 mul.56
  104.0 0.3 mul.52
  104.3 0.3 mul.60
  104.7 2.0 %fusion.1 = bf16[128,2048]{1,0:T(8,128)(2,1)} fusion(f32[16,8,16,128]{3,2,1,0:T(8,128)S(1)} %bitcast.32, f32[16,8,16,128]{3,2,1,0:T(8,128)S(1)} %bitcast.30, f32[16,8,16,128]{3,2,1,0:T(8,128)S(1)} %bitcast.31, bf16[128,2176]{1,0:T(8,128)(2,1)S(1)} %collective-permute-done.3, bf16[128,2176]{1,0:T(8,128)(2,1)S(1)} %shard_map.74, bf16[128,2176]{1,0:T(8,128)(2,1)S(1)} %shard_map.73), kind=kLoop, calls=%fused_computation.3 | loop fusion | flops 2359296 | bytes 5242880 | tf_op jit(solution)/shard_map/convert_element_type | solution.py:236
  106.6 0.0 all-gather.2.cloned.1.call-update
  106.7 0.0 reduce-scatter.2.cloned.1.call-start
  106.7 27.0 %all-gather.2.cloned.1.call-done = bf16[512,2048]{1,0:T(8,128)(2,1)} async-done(((bf16[128,2048]{1,0:T(8,128)(2,1)}), bf16[512,2048]{1,0:T(8,128)(2,1)}) %all-gather.2.cloned.1.call-update) | async-done | bytes 2097168 | tf_op jit(solution)/shard_map/all_gather | solution.py:269
  133.7 8.9 %convolution_convert_fusion = bf16[512,1792]{1,0:T(8,128)(2,1)} fusion(bf16[512,2048]{1,0:T(8,128)(2,1)} %all-gather.2.cloned.1.call-done, bf16[2048,1792]{1,0:T(8,128)(2,1)} %param.13), kind=kOutput, calls=%fused_computation | convolution fusion | flops 3759013888 | bytes 11272192 | tf_op jit(solution)/shard_map/dot_general | solution.py:271
  142.6 0.0 reduce-scatter.2.cloned.1.call-update
  142.6 39.6 %reduce-scatter.2.cloned.1.call-done = bf16[128,1792]{1,0:T(8,128)(2,1)} async-done(((bf16[512,1792]{1,0:T(8,128)(2,1)}), bf16[128,1792]{1,0:T(8,128)(2,1)}) %reduce-scatter.2.cloned.1.call-update) | async-done | bytes 458768 | tf_op jit(solution)/shard_map/reduce_scatter | solution.py:270
  (2 shorter events, 0.0 us)
Async XLA Ops:
  6.5 127.1 %all-gather.2.cloned.1.call-start = ((), (), s32[]{:S(2)}) async-start(), calls=%async_computation.1 | async-start | bytes 2621440 | tf_op jit(solution)/shard_map/all_gather | solution.py:269
  6.5 38.3 %collective-permute-start = (bf16[8192,576]{0,1:T(8,128)(2,1)}, bf16[8192,576]{0,1:T(8,128)(2,1)}, u32[]{:S(2)}, u32[]{:S(2)}) collective-permute-start(bf16[8192,576]{0,1:T(8,128)(2,1)} %param.8), channel_id=1, source_target_pairs={{0,4},{4,0},{8,12},{12,8},{1,5},{5,1},{9,13},{13,9},{2,6},{6,2},{1... | collective-permute-start | bytes 28311560 | tf_op jit(solution)/shard_map/ppermute | solution.py:247
  7.0 52.0 %collective-permute-start.2 = (bf16[128,3072]{1,0:T(8,128)(2,1)}, bf16[128,3072]{1,0:T(8,128)(2,1)}, u32[]{:S(2)}, u32[]{:S(2)}) collective-permute-start(bf16[128,3072]{1,0:T(8,128)(2,1)} %q_ref.3), channel_id=1, source_target_pairs={{0,8},{4,12},{8,0},{12,4},{1,9},{5,13},{9,1},{13,5},{2,10},{6,14},... | collective-permute-start | bytes 2359304 | tf_op jit(solution)/shard_map/ppermute | solution.py:261
  9.5 35.3 %collective-permute-start.1 = (s32[1,64]{1,0:T(1,128)}, s32[1,64]{1,0:T(1,128)S(1)}, u32[]{:S(2)}, u32[]{:S(2)}) collective-permute-start(s32[1,64]{1,0:T(1,128)} %param.9), channel_id=1, source_target_pairs={{0,8},{4,12},{8,0},{12,4},{1,9},{5,13},{9,1},{13,5},{2,10},{6,14},... | collective-permute-start | bytes 776 | tf_op jit(solution)/shard_map/ppermute | solution.py:262
  9.5 14.9 %copy-start.5 = (s32[1,64]{1,0:T(1,128)S(1)}, s32[1,64]{1,0:T(1,128)}, u32[]{:S(2)}) copy-start(s32[1,64]{1,0:T(1,128)} %param.9) | copy-start | bytes 772
  9.5 15.0 %copy-start = (bf16[16,128,512]{2,1,0:T(8,128)(2,1)S(1)}, bf16[16,128,512]{2,1,0:T(8,128)(2,1)}, u32[]{:S(2)}) copy-start(bf16[16,128,512]{2,1,0:T(8,128)(2,1)} %wa_hbm.5) | copy-start | bytes 6291460
  9.5 15.0 %copy-start.4 = (bf16[128,3072]{1,0:T(8,128)(2,1)S(1)}, bf16[128,3072]{1,0:T(8,128)(2,1)}, u32[]{:S(2)}) copy-start(bf16[128,3072]{1,0:T(8,128)(2,1)} %q_ref.3) | copy-start | bytes 2359300
  24.6 1.6 copy-start.1
  59.0 1.6 copy-start.2
  60.6 28.1 %copy-start.3 = (bf16[16,512,128]{2,1,0:T(8,128)(2,1)S(1)}, bf16[16,512,128]{2,1,0:T(8,128)(2,1)}, u32[]{:S(2)}) copy-start(bf16[16,512,128]{2,1,0:T(8,128)(2,1)} %wv_hbm.5) | copy-start | bytes 6291460
  88.6 14.8 %collective-permute-start.3 = (bf16[128,2176]{1,0:T(8,128)(2,1)S(1)}, bf16[128,2176]{1,0:T(8,128)(2,1)S(1)}, u32[]{:S(2)}, u32[]{:S(2)}) collective-permute-start(bf16[128,2176]{1,0:T(8,128)(2,1)S(1)} %shard_map.75), channel_id=1, source_target_pairs={{0,8},{4,12},{8,0},{12,4},{1,9},{5,13},{9,1},{13,5},{2,10},{6,14},... | collective-permute-start | bytes 1671176 | tf_op jit(solution)/shard_map/ppermute | solution.py:267
  106.7 75.5 %reduce-scatter.2.cloned.1.call-start = ((), (), s32[]{:S(2)}) async-start(), calls=%async_computation.2 | async-start | bytes 2293760 | tf_op jit(solution)/shard_map/reduce_scatter | solution.py:270
Sparse Core Ops, SparseCore 0:
  106.8 26.8 all-gather.1
  142.7 39.4 reduce-scatter.1

commit v2 on v1

v2 whole, which is shorter than its diff:
```python
import functools
import math

import jax
import jax.numpy as jnp
from jax import lax
from jax.experimental import pallas as pl
from jax.experimental.pallas import tpu as pltpu
from jax.sharding import PartitionSpec as P

BT = 64
WIDE = 128
CHUNK = 8
SMALL = 4
PIECES = 2
NEVER = -1e30
FAR = 1 << 30
MIB = 1024 * 1024


def attend_kernel(
    blocks_held, sources, offset,
    meta, q_ref, wa_hbm, own_hbm, sib_hbm, wv_hbm, o_ref,
    raw, kt, q_full, wa, wv, acc0, acc1, s0, s1, p0, p1, t0, t1, listed, edge, kv_sem, wa_sem, wv_sem,
):
    accs, stores, peaks, totals = (acc0, acc1), (s0, s1), (p0, p1), (t0, t1)
    tokens = q_ref.shape[0]
    heads, nope, lat = wa.shape
    width = kt.shape[0]
    vd = wv.shape[2]
    head_width = nope + width - lat
    fold = head_width ** -0.5 * math.log2(math.e)
    first = meta[64] + offset
    mine = meta[65]
    other = meta[66]

    wa_copy = pltpu.make_async_copy(wa_hbm, wa, wa_sem)
    wv_copy = pltpu.make_async_copy(wv_hbm, wv, wv_sem)
    wa_copy.start()

    def fetch(block, slot):
        owner = block // blocks_held
        col = pl.multiple_of((block % blocks_held) // 2 * WIDE, WIDE)
        for name, holder, source in (("own", mine, own_hbm), ("sib", other, sib_hbm)):
            if name in sources:
                @pl.when(owner == holder)
                def _(source=source):
                    pltpu.make_async_copy(source.at[:, pl.ds(col, WIDE)], raw.at[slot], kv_sem).start()

    def scan(j, carry):
        full, part = carry
        block = meta[j]
        owner = block // blocks_held
        here = jnp.bool_(False)
        for name, holder in (("own", mine), ("sib", other)):
            if name in sources:
                here = here | (owner == holder)
        whole = here & (block * BT + BT - 1 <= first)
        some = here & (block * BT + BT - 1 > first) & (block * BT <= first + tokens - 1)

        @pl.when(whole)
        def _():
            fetch(block, full)
            listed[full] = block

        @pl.when(some)
        def _():
            edge[part] = block

        return full + whole.astype(jnp.int32), part + some.astype(jnp.int32)

    full, part = lax.fori_loop(0, 64, scan, (jnp.int32(0), jnp.int32(0)))

    def fetch_edge(i, _):
        fetch(edge[i], full + i)
        listed[full + i] = edge[i]
        return 0

    lax.fori_loop(0, part, fetch_edge, 0)
    count = full + part
    plain_chunks = full // CHUNK
    done = plain_chunks * CHUNK
    small_chunks = (count - done + SMALL - 1) // SMALL
    slots = done + small_chunks * SMALL

    def fill(i, _):
        pltpu.make_async_copy(own_hbm.at[:, pl.ds(0, WIDE)], raw.at[i], kv_sem).start()
        listed[i] = 0
        return 0

    lax.fori_loop(count, slots, fill, 0)
    wv_copy.start()

    wa_copy.wait()
    for h in range(heads):
        base = h * head_width
        latent_part = jnp.dot(
            q_ref[:, base : base + nope], wa[h], preferred_element_type=jnp.float32
        )
        rows = slice(h * tokens, (h + 1) * tokens)
        q_full[rows, 0:lat] = (latent_part * fold).astype(jnp.bfloat16)
        turned = q_ref[:, base + nope : base + head_width].astype(jnp.float32)
        q_full[rows, lat:width] = (turned * fold).astype(jnp.bfloat16)

    def land(i, _):
        pltpu.make_async_copy(own_hbm.at[:, pl.ds(0, WIDE)], raw.at[0], kv_sem).wait()
        return 0

    lax.fori_loop(0, slots, land, 0)

    def join(i, _):
        left = raw[2 * i]
        right = raw[2 * i + 1]
        left_swapped = jnp.concatenate([left[:, BT:], left[:, :BT]], axis=1)
        right_swapped = jnp.concatenate([right[:, BT:], right[:, :BT]], axis=1)
        low = jnp.where(listed[2 * i] % 2 == 1, left_swapped, left)
        high = jnp.where(listed[2 * i + 1] % 2 == 1, right, right_swapped)
        lane = lax.broadcasted_iota(jnp.int32, (width, WIDE), 1)
        kt[:, pl.ds(pl.multiple_of(i * WIDE, WIDE), WIDE)] = jnp.where(lane < BT, low, high)
        return 0

    lax.fori_loop(0, slots // 2, join, 0)
    wv_copy.wait()

    tile = acc0.shape[0]
    tile_heads = tile // tokens
    lane = lax.broadcasted_iota(jnp.int32, (tokens, 128), 1)

    def row_pair(r, lse_tile):
        bases = [pl.multiple_of(r * 2 * tile, tile), pl.multiple_of(r * 2 * tile + tile, tile)]
        for i in range(2):
            accs[i][...] = jnp.zeros_like(accs[i])
            peaks[i][...] = jnp.full(peaks[i].shape, NEVER, jnp.float32)
            totals[i][...] = jnp.zeros_like(totals[i])

        def score(i, key0, n):
            stores[i][:, 0 : n * BT] = jnp.dot(
                q_full[pl.ds(bases[i], tile), :], kt[:, pl.ds(key0, n * BT)],
                preferred_element_type=jnp.float32,
            )

        def soften(i, n, visible):
            scores = stores[i][:, 0 : n * BT]
            if visible is not None:
                scores = jnp.where(
                    visible[None], scores.reshape(tile_heads, tokens, n * BT), NEVER
                ).reshape(tile, n * BT)
            peak = peaks[i][...]
            new_peak = jnp.maximum(peak, jnp.max(scores, axis=1, keepdims=True))
            peaks[i][...] = new_peak
            raised = jnp.exp2(scores - new_peak[:, 0:1])
            keep = jnp.exp2(peak - new_peak)
            total = totals[i][...] * keep
            for k in range(n * BT // 128):
                total = total + raised[:, k * 128 : (k + 1) * 128]
            totals[i][...] = total
            return raised.astype(jnp.bfloat16), keep[:, 0:1]

        def mix(i, key0, n, raised, keep):
            accs[i][...] = accs[i][...] * keep + lax.dot_general(
                raised, kt[0:lat, pl.ds(key0, n * BT)], (((1,), (1,)), ((), ())),
                preferred_element_type=jnp.float32,
            )

        def chunk(n, total_chunks, start, masked, c, _):
            key0 = pl.multiple_of(start + c * n * BT, 128)
            last = start + (total_chunks - 1) * n * BT
            key1 = pl.multiple_of(jnp.minimum(key0 + n * BT, last), 128)
            visible = None
            if masked:
                block0 = key0 // BT
                column = lax.broadcasted_iota(jnp.int32, (tokens, n * BT), 1)
                position = jnp.zeros((tokens, n * BT), jnp.int32)
                for b in range(n):
                    at = jnp.where(
                        block0 + b < full, 0,
                        jnp.where(block0 + b < count, listed[block0 + b] * BT, FAR),
                    )
                    position = jnp.where(column // BT == b, at + column % BT, position)
                query = first + lax.broadcasted_iota(jnp.int32, (tokens, n * BT), 0)
                visible = position <= query
            score(1, key0, n)
            raised, keep = soften(0, n, visible)
            mix(0, key0, n, raised, keep)
            score(0, key1, n)
            raised, keep = soften(1, n, visible)
            mix(1, key0, n, raised, keep)
            return 0

        @pl.when(plain_chunks > 0)
        def _():
            score(0, 0, CHUNK)
            lax.fori_loop(
                0, plain_chunks, functools.partial(chunk, CHUNK, plain_chunks, 0, False), 0
            )

        @pl.when(small_chunks > 0)
        def _():
            score(0, pl.multiple_of(done * BT, 128), SMALL)
            lax.fori_loop(
                0, small_chunks, functools.partial(chunk, SMALL, small_chunks, done * BT, True), 0
            )

        for i in range(2):
            total = jnp.maximum(jnp.sum(totals[i][...], axis=1, keepdims=True), 1e-30)
            lse = peaks[i][:, 0:1] + jnp.log2(total)
            scale = 1.0 / total
            for j in range(tile_heads):
                h = (r * 2 + i) * tile_heads + j
                rows = slice(j * tokens, (j + 1) * tokens)
                mixed = (accs[i][rows, :] * scale[rows, :]).astype(jnp.bfloat16)
                out = jnp.dot(mixed, wv[h], preferred_element_type=jnp.float32)
                o_ref[:, pl.ds(pl.multiple_of(h * vd, vd), vd)] = out.astype(jnp.bfloat16)
                value = lse[rows, :]
                high = value.astype(jnp.bfloat16).astype(jnp.float32)
                middle = (value - high).astype(jnp.bfloat16).astype(jnp.float32)
                low = value - high - middle
                lse_tile = jnp.where(lane == h, high, lse_tile)
                lse_tile = jnp.where(lane == h + 32, middle, lse_tile)
                lse_tile = jnp.where(lane == h + 64, low, lse_tile)
        return lse_tile

    lse_tile = lax.fori_loop(
        0, heads * tokens // (2 * tile), row_pair, jnp.zeros((tokens, 128), jnp.float32)
    )
    o_ref[:, heads * vd :] = lse_tile.astype(jnp.bfloat16)


def attend(meta, queries, own, sib, w_absorb, w_value, depth, sources, offset, row_tile):
    tokens = queries.shape[0]
    heads, nope, lat = w_absorb.shape
    vd = w_value.shape[2]
    width = own.shape[0]
    slots = -(-depth * len(sources) // SMALL) * SMALL
    rows = heads * tokens
    tile = min(row_tile, rows // 2)
    keys = depth * len(sources) * BT * 2 // 3
    any_space = pl.BlockSpec(memory_space=pl.ANY)
    vmem = pl.BlockSpec(memory_space=pltpu.VMEM)
    return pl.pallas_call(
        functools.partial(attend_kernel, own.shape[1] // BT, sources, offset),
        out_shape=jax.ShapeDtypeStruct((tokens, heads * vd + 128), jnp.bfloat16),
        in_specs=[
            pl.BlockSpec(memory_space=pltpu.SMEM), vmem, any_space, any_space, any_space, any_space,
        ],
        out_specs=vmem,
        scratch_shapes=[
            pltpu.VMEM((slots, width, WIDE), jnp.bfloat16),
            pltpu.VMEM((width, slots * BT), jnp.bfloat16),
            pltpu.VMEM((rows, width), jnp.bfloat16),
            pltpu.VMEM(w_absorb.shape, jnp.bfloat16),
            pltpu.VMEM(w_value.shape, jnp.bfloat16),
            *[pltpu.VMEM((tile, lat), jnp.float32)] * 2,
            *[pltpu.VMEM((tile, CHUNK * BT), jnp.float32)] * 2,
            *[pltpu.VMEM((tile, 128), jnp.float32)] * 4,
            pltpu.SMEM((slots,), jnp.int32),
            pltpu.SMEM((64,), jnp.int32),
            pltpu.SemaphoreType.DMA,
            pltpu.SemaphoreType.DMA,
            pltpu.SemaphoreType.DMA,
        ],
        compiler_params=pltpu.CompilerParams(vmem_limit_bytes=52 * MIB),
        cost_estimate=pl.CostEstimate(
            flops=2 * rows * keys * (width + lat),
            bytes_accessed=2 * keys * width * 2,
            transcendentals=rows * keys,
        ),
    )(meta, queries, w_absorb, own, sib, w_value)


def combine_kernel(heads, *refs):
    partials, out = refs[:-1], refs[-1]
    vd = out.shape[1] // heads
    logs = []
    for ref in partials:
        tail = ref[:, heads * vd :].astype(jnp.float32)
        logs.append(tail[:, 0:heads] + tail[:, 32 : 32 + heads] + tail[:, 64 : 64 + heads])
    peak = functools.reduce(jnp.maximum, logs)
    shares = [jnp.exp2(value - peak) for value in logs]
    norm = 1.0 / functools.reduce(jnp.add, shares)
    for h in range(heads):
        columns = slice(h * vd, (h + 1) * vd)
        mixed = sum(
            ref[:, columns].astype(jnp.float32) * (share * norm)[:, h : h + 1]
            for ref, share in zip(partials, shares)
        )
        out[:, columns] = mixed.astype(jnp.bfloat16)


def combine(partials, heads):
    tokens, columns = partials[0].shape
    vmem = pl.BlockSpec(memory_space=pltpu.VMEM)
    return pl.pallas_call(
        functools.partial(combine_kernel, heads),
        out_shape=jax.ShapeDtypeStruct((tokens, columns - 128), jnp.bfloat16),
        in_specs=[vmem] * len(partials),
        out_specs=vmem,
        compiler_params=pltpu.CompilerParams(vmem_limit_bytes=16 * MIB),
        cost_estimate=pl.CostEstimate(
            flops=4 * tokens * columns, bytes_accessed=8 * tokens * columns, transcendentals=0
        ),
    )(*partials)


def project_kernel(x_ref, w_ref, o_ref):
    o_ref[...] = jnp.dot(x_ref[...], w_ref[...], preferred_element_type=jnp.float32).astype(jnp.bfloat16)


def project(x, w):
    rows, depth = x.shape
    columns = w.shape[1]
    wide = 256 if columns % 256 == 0 else columns
    return pl.pallas_call(
        project_kernel,
        out_shape=jax.ShapeDtypeStruct((rows, columns), jnp.bfloat16),
        grid=(columns // wide,),
        in_specs=[
            pl.BlockSpec((rows, depth), lambda j: (0, 0)),
            pl.BlockSpec((depth, wide), lambda j: (0, j)),
        ],
        out_specs=pl.BlockSpec((rows, wide), lambda j: (0, j)),
        compiler_params=pltpu.CompilerParams(vmem_limit_bytes=32 * MIB),
        cost_estimate=pl.CostEstimate(
            flops=2 * rows * depth * columns,
            bytes_accessed=2 * (rows * depth + depth * columns + rows * columns),
            transcendentals=0,
        ),
    )(x, w)


def body(queries, latent, selection, span_offset, w_absorb, w_value, w_out):
    owners = lax.axis_size("ctx")
    groups = lax.axis_size("head")
    me = lax.axis_index("ctx")
    column = lax.axis_index("head")
    chips = owners // 2
    depth = 3 * selection.shape[1] // (2 * owners)
    heads = w_absorb.shape[0]
    tokens = queries.shape[0]
    piece = tokens // PIECES
    sibling = [(i, i ^ 1) for i in range(owners)]
    ahead = {t: [(i, (i + 2 * t) % owners) for i in range(owners)] for t in range(1, chips)}
    back = {t: [(i, (i - 2 * t) % owners) for i in range(owners)] for t in range(1, chips)}
    own = latent.T

    def meta_of(row, index):
        return jnp.concatenate(
            [row[0], jnp.stack([span_offset[0] + index * tokens, me, me ^ 1])]
        ).astype(jnp.int32)

    cuts = [slice(c * piece, (c + 1) * piece) for c in range(PIECES)]
    far_rows = {t: lax.ppermute(selection, "ctx", ahead[t]) for t in ahead}
    far_queries = [
        {t: lax.ppermute(queries[cut], "ctx", ahead[t]) for t in ahead} for cut in cuts
    ]
    sib = lax.ppermute(own, "ctx", sibling)
    my_meta = meta_of(selection, me)
    near = attend(my_meta, queries, own, own, w_absorb, w_value, depth, ("own",), 0, 1024)
    outputs = []
    for c, cut in enumerate(cuts):
        partials = []
        for t in ahead:
            partial = attend(
                meta_of(far_rows[t], (me - 2 * t) % owners), far_queries[c][t], own, sib,
                w_absorb, w_value, depth, ("own", "sib"), c * piece, 512,
            )
            partials.append(lax.ppermute(partial, "ctx", back[t]))
        partials.append(
            attend(my_meta, queries[cut], own, sib, w_absorb, w_value, depth, ("sib",), c * piece, 512)
        )
        partials.append(near[cut])
        mine = combine(partials, heads)
        gathered = [mine] + [lax.ppermute(mine, "ctx", ahead[t]) for t in ahead]
        pairs = [x for g in gathered for x in (g, lax.ppermute(g, "ctx", sibling))]
        shares = project(jnp.concatenate(pairs, axis=0), w_out)

        def share_of(block):
            turn = (me // 2 - block // 2) % chips
            place = turn * 2 + (me + block) % 2
            return lax.dynamic_slice_in_dim(shares, place * piece, piece, 0)

        arrived = [share_of(column)]
        order = sorted(range(1, groups), key=lambda s: -min(s, groups - s))
        for s in order:
            shift = [(i, (i + s) % groups) for i in range(groups)]
            arrived.append(lax.ppermute(share_of((column + s) % groups), "head", shift))
        outputs.append(sum(a.astype(jnp.float32) for a in arrived).astype(jnp.bfloat16))
    return jnp.concatenate(outputs, axis=0)


def solution(mesh):
    placed = (
        P(("groups", "ctx"), "head"),
        P(("groups", "ctx"), None),
        P(("groups", "ctx"), None),
        P("groups"),
        P("head", None, None),
        P("head", None, None),
        P("head", "ctx"),
    )
    return jax.shard_map(
        body, mesh=mesh, in_specs=placed, out_specs=P(("groups", "head"), "ctx"), check_vma=False
    )
```

time: 190 us -> 148 us (0.78)
  the two profiles are of different devices: /device:TPU:0 before, /device:TPU:17 now
where the time goes in v2:
time: 148 us; the launch traced here: 146 us
  Pallas kernels  77 us (52%)
  starting transfers between devices  31.9 us (22%)
  waiting for transfers between devices  27.1 us (18%)
  local copies, waits for them, and re-layouts  7.47 us (5%)
  other arithmetic  2 us (1%)
    pallas_call x5, Pallas kernels, attend(): pl.pallas_call(functools.partial(attend_kernel, own.shape[1] // BT, sourc...  68.3 us
    ppermute x6, waiting for transfers between devices, body(): arrived.append(lax.ppermute(share_of((column + s) % groups), 'head', shift))  26.9 us
    ppermute x6, starting transfers between devices, body(): arrived.append(lax.ppermute(share_of((column + s) % groups), 'head', shift))  15.9 us
    ppermute x4, starting transfers between devices, body(): pairs = [x for g in gathered for x in (g, lax.ppermute(g, 'ctx', sibling))]  7.44 us
    pallas_call x2, Pallas kernels, project(): pl.pallas_call(project_kernel, out_shape=jax.ShapeDtypeStruct((rows, colu...  7.44 us
    unnamed x6, local copies, waits for them, and re-layouts  6.16 us
  transfers between devices with their start and end apart: 18, of which 7 were waited for; matrix products, arithmetic and copies ran while one was open for 2% of the time, Pallas kernels for 50%

profile of v2, /device:TPU:17, one launch (start us, length us, event | category | flops | bytes accessed | tf_op | source)
XLA Modules:
  0.0 146.3 jit_solution(1836117234625645507)
XLA Ops:
  0.0 0.0 copy-start.2
  0.0 0.7 collective-permute-start.2
  0.7 1.2 collective-permute-start
  1.9 1.2 fusion
  3.1 0.3 collective-permute-start.1
  3.4 1.2 collective-permute-start.10
  5.2 0.7 add_add_fusion.1.meta
  6.0 0.0 copy-done.2
  6.0 16.1 %shard_map.75 = bf16[128,2176]{1,0:T(8,128)(2,1)S(1)} custom-call(s32[67]{0:T(128)S(1)} %add_add_fusion.1.meta, bf16[128,3072]{1,0:T(8,128)(2,1)S(1)} %copy-done.2, bf16[16,128,512]{2,1,0:T(8,128)(2,1)} %wa_hbm.9, bf16[576,8192]{1,0:T(8,128)(2,1)} %bitcast.11, bf16[576,8192]{1,0:T(8,128)(2,1)} %bitcast.12, bf16[16,512,128]{2,1,0:T(8,128)(2,1)} %wv_hbm.9), custom_call_target="tpu_custom_call" | custom-call | flops 4563402752 | bytes 2359296 | tf_op jit(solution)/shard_map/pallas_call | solution.py:240
  22.2 0.0 collective-permute-done
  22.2 0.1 add_add_fusion.meta
  22.3 0.0 collective-permute-done.1.q_ref
  22.3 0.0 collective-permute-done.2.sib_hbm
  22.3 15.7 %shard_map.73 = bf16[64,2176]{1,0:T(8,128)(2,1)S(1)} custom-call(s32[67]{0:T(128)S(1)} %add_add_fusion.meta, bf16[64,3072]{1,0:T(8,128)(2,1)S(1)} %collective-permute-done.1.q_ref, bf16[16,128,512]{2,1,0:T(8,128)(2,1)} %wa_hbm.9, bf16[576,8192]{1,0:T(8,128)(2,1)} %bitcast.13, bf16[576,8192]{1,0:T(8,128)(2,1)} %collective-permute-done.2.sib_hbm, ...), custom_call_target="tpu_custom_call" | custom-call | flops 4563402752 | bytes 4718592 | tf_op jit(solution)/shard_map/pallas_call | solution.py:240
  38.0 0.1 collective-permute-start.3
  38.1 0.0 collective-permute-done.10.q_ref
  38.1 15.6 %shard_map.78 = bf16[64,2176]{1,0:T(8,128)(2,1)S(1)} custom-call(s32[67]{0:T(128)S(1)} %add_add_fusion.meta, bf16[64,3072]{1,0:T(8,128)(2,1)S(1)} %collective-permute-done.10.q_ref, bf16[16,128,512]{2,1,0:T(8,128)(2,1)} %wa_hbm.9, bf16[576,8192]{1,0:T(8,128)(2,1)} %bitcast.14, bf16[576,8192]{1,0:T(8,128)(2,1)} %collective-permute-done.2.sib_hbm, ...), custom_call_target="tpu_custom_call" | custom-call | flops 4563402752 | bytes 4718592 | tf_op jit(solution)/shard_map/pallas_call | solution.py:240
  53.7 2.4 %collective-permute-start.11 = (bf16[64,2176]{1,0:T(8,128)(2,1)S(1)}, bf16[64,2176]{1,0:T(8,128)(2,1)S(1)}, u32[]{:S(2)}, u32[]{:S(2)}) collective-permute-start(bf16[64,2176]{1,0:T(8,128)(2,1)S(1)} %shard_map.78), channel_id=1, source_target_pairs={{0,8},{4,12},{8,0},{12,4},{1,9},{5,13},{9,1},{13,5},{2,10},{6,14},... | collective-permute-start | bytes 835592 | tf_op jit(solution)/shard_map/ppermute | solution.py:367
  56.1 10.3 %shard_map.74.refs_1_ = bf16[64,2176]{1,0:T(8,128)(2,1)S(1)} custom-call(s32[67]{0:T(128)S(1)} %add_add_fusion.1.meta, bf16[64,3072]{1,0:T(8,128)(2,1)S(1)} %get-tuple-element.11.q_ref, bf16[16,128,512]{2,1,0:T(8,128)(2,1)} %wa_hbm.9, bf16[576,8192]{1,0:T(8,128)(2,1)} %bitcast.15, bf16[576,8192]{1,0:T(8,128)(2,1)} %collective-permute-done.2.sib_hbm, ...), custom_call_target="tpu_custom_call" | custom-call | flops 2281701376 | bytes 2359296 | tf_op jit(solution)/shard_map/pallas_call | solution.py:240
  66.4 0.0 collective-permute-done.3.refs_0_
  66.4 0.6 shard_map.76
  67.0 1.3 collective-permute-start.5
  68.3 10.6 %shard_map.79.refs_1_ = bf16[64,2176]{1,0:T(8,128)(2,1)S(1)} custom-call(s32[67]{0:T(128)S(1)} %add_add_fusion.1.meta, bf16[64,3072]{1,0:T(8,128)(2,1)S(1)} %get-tuple-element.12.q_ref, bf16[16,128,512]{2,1,0:T(8,128)(2,1)} %wa_hbm.9, bf16[576,8192]{1,0:T(8,128)(2,1)} %bitcast.16, bf16[576,8192]{1,0:T(8,128)(2,1)} %collective-permute-done.2.sib_hbm, ...), custom_call_target="tpu_custom_call" | custom-call | flops 2281701376 | bytes 2359296 | tf_op jit(solution)/shard_map/pallas_call | solution.py:240
  78.9 0.0 collective-permute-done.11.refs_0_
  78.9 0.6 shard_map.80
  79.5 1.5 %collective-permute-start.13 = (bf16[64,2048]{1,0:T(8,128)(2,1)S(1)}, bf16[64,2048]{1,0:T(8,128)(2,1)S(1)}, u32[]{:S(2)}, u32[]{:S(2)}) collective-permute-start(bf16[64,2048]{1,0:T(8,128)(2,1)S(1)} %shard_map.80), channel_id=1, source_target_pairs={{0,8},{4,12},{8,0},{12,4},{1,9},{5,13},{9,1},{13,5},{2,10},{6,14},... | collective-permute-start | bytes 786440 | tf_op jit(solution)/shard_map/ppermute | solution.py:373
  81.0 3.2 %collective-permute-start.4 = (bf16[64,2048]{1,0:T(8,128)(2,1)S(1)}, bf16[64,2048]{1,0:T(8,128)(2,1)S(1)}, u32[]{:S(2)}, u32[]{:S(2)}) collective-permute-start(bf16[64,2048]{1,0:T(8,128)(2,1)S(1)} %shard_map.76), channel_id=1, source_target_pairs={{0,4},{4,0},{8,12},{12,8},{1,5},{5,1},{9,13},{13,9},{2,6},{6,2},{1... | collective-permute-start | bytes 786440 | tf_op jit(solution)/shard_map/ppermute | solution.py:374
  84.2 0.0 collective-permute-done.5
  84.2 0.0 collective-permute-start.6
  84.2 0.5 collective-permute-start.12
  84.7 0.1 collective-permute-done.13
  84.8 3.7 %collective-permute-start.14 = (bf16[64,2048]{1,0:T(8,128)(2,1)S(1)}, bf16[64,2048]{1,0:T(8,128)(2,1)S(1)}, u32[]{:S(2)}, u32[]{:S(2)}) collective-permute-start(bf16[64,2048]{1,0:T(8,128)(2,1)S(1)} %collective-permute-done.13), channel_id=1, source_target_pairs={{0,4},{4,0},{8,12},{12,8},{1,5},{5,1},{9,13},{13,9},{2,6},{6,2},{1... | collective-permute-start | bytes 786440 | tf_op jit(solution)/shard_map/ppermute | solution.py:374
  88.5 0.0 collective-permute-done.4
  88.5 0.0 collective-permute-done.6
  88.5 0.1 pad_maximum_fusion.x_ref
  88.6 0.0 copy-start
  88.6 3.1 %copy-done = bf16[2048,1792]{1,0:T(8,128)(2,1)S(1)} copy-done((bf16[2048,1792]{1,0:T(8,128)(2,1)S(1)}, bf16[2048,1792]{1,0:T(8,128)(2,1)}, u32[]{:S(2)}) %copy-start) | copy-done | bytes 7340056
  91.7 3.7 %shard_map.77 = bf16[256,1792]{1,0:T(8,128)(2,1)S(1)} custom-call(bf16[256,2048]{1,0:T(8,128)(2,1)S(1)} %pad_maximum_fusion.x_ref, bf16[2048,1792]{1,0:T(8,128)(2,1)S(1)} %copy-done), custom_call_target="tpu_custom_call" | custom-call | flops 1879048192 | bytes 9306112 | tf_op jit(solution)/shard_map/pallas_call | solution.py:313
  95.4 0.0 collective-permute-done.12
  95.4 0.0 collective-permute-done.14
  95.5 0.1 pad_maximum_fusion.1.x_ref
  95.6 0.0 copy-start.1
  95.6 3.1 %copy-done.1 = bf16[2048,1792]{1,0:T(8,128)(2,1)S(1)} copy-done((bf16[2048,1792]{1,0:T(8,128)(2,1)S(1)}, bf16[2048,1792]{1,0:T(8,128)(2,1)}, u32[]{:S(2)}) %copy-start.1) | copy-done | bytes 7340056
  98.6 3.7 %shard_map.81 = bf16[256,1792]{1,0:T(8,128)(2,1)S(1)} custom-call(bf16[256,2048]{1,0:T(8,128)(2,1)S(1)} %pad_maximum_fusion.1.x_ref, bf16[2048,1792]{1,0:T(8,128)(2,1)S(1)} %copy-done.1), custom_call_target="tpu_custom_call" | custom-call | flops 1879048192 | bytes 9306112 | tf_op jit(solution)/shard_map/pallas_call | solution.py:313
  102.4 0.1 constant_dynamic-slice_fusion.2
  102.4 0.1 collective-permute-start.15
  102.5 2.5 %collective-permute-start.17 = (bf16[64,1792]{1,0:T(8,128)(2,1)S(1)}, bf16[64,1792]{1,0:T(8,128)(2,1)S(1)}, u32[]{:S(2)}, u32[]{:S(2)}) collective-permute-start(bf16[64,1792]{1,0:T(8,128)(2,1)S(1)} %get-tuple-element.9), channel_id=1, source_target_pairs={{0,3},{1,0},{2,1},{3,2},{4,7},{5,4},{6,5},{7,6},{8,11},{9,8},{10,9... | collective-permute-start | bytes 688136 | tf_op jit(solution)/shard_map/ppermute | solution.py:386
  105.0 0.0 collective-permute-start.16
  105.0 1.4 collective-permute-start.7
  106.4 2.0 %collective-permute-start.9 = (bf16[64,1792]{1,0:T(8,128)(2,1)S(1)}, bf16[64,1792]{1,0:T(8,128)(2,1)S(1)}, u32[]{:S(2)}, u32[]{:S(2)}) collective-permute-start(bf16[64,1792]{1,0:T(8,128)(2,1)S(1)} %get-tuple-element.6), channel_id=1, source_target_pairs={{0,3},{1,0},{2,1},{3,2},{4,7},{5,4},{6,5},{7,6},{8,11},{9,8},{10,9... | collective-permute-start | bytes 688136 | tf_op jit(solution)/shard_map/ppermute | solution.py:386
  108.4 4.1 %collective-permute-done.15 = bf16[64,1792]{1,0:T(8,128)(2,1)S(1)} collective-permute-done((bf16[64,1792]{1,0:T(8,128)(2,1)S(1)}, bf16[64,1792]{1,0:T(8,128)(2,1)S(1)}, u32[]{:S(2)}, u32[]{:S(2)}) %collective-permute-start.15) | collective-permute-done | bytes 229408 | tf_op jit(solution)/shard_map/ppermute | solution.py:386
  112.6 9.9 %collective-permute-start.8 = (bf16[64,1792]{1,0:T(8,128)(2,1)S(1)}, bf16[64,1792]{1,0:T(8,128)(2,1)S(1)}, u32[]{:S(2)}, u32[]{:S(2)}) collective-permute-start(bf16[64,1792]{1,0:T(8,128)(2,1)S(1)} %get-tuple-element.7), channel_id=1, source_target_pairs={{0,1},{1,2},{2,3},{3,0},{4,5},{5,6},{6,7},{7,4},{8,9},{9,10},{10,1... | collective-permute-start | bytes 688136 | tf_op jit(solution)/shard_map/ppermute | solution.py:386
  122.5 4.8 %collective-permute-done.17 = bf16[64,1792]{1,0:T(8,128)(2,1)S(1)} collective-permute-done((bf16[64,1792]{1,0:T(8,128)(2,1)S(1)}, bf16[64,1792]{1,0:T(8,128)(2,1)S(1)}, u32[]{:S(2)}, u32[]{:S(2)}) %collective-permute-start.17) | collective-permute-done | bytes 229408 | tf_op jit(solution)/shard_map/ppermute | solution.py:386
  127.3 8.3 %collective-permute-done.16 = bf16[64,1792]{1,0:T(8,128)(2,1)S(1)} collective-permute-done((bf16[64,1792]{1,0:T(8,128)(2,1)S(1)}, bf16[64,1792]{1,0:T(8,128)(2,1)S(1)}, u32[]{:S(2)}, u32[]{:S(2)}) %collective-permute-start.16) | collective-permute-done | bytes 229408 | tf_op jit(solution)/shard_map/ppermute | solution.py:386
  135.6 0.1 add_convert_fusion
  135.7 1.4 collective-permute-done.7
  137.1 4.9 %collective-permute-done.9 = bf16[64,1792]{1,0:T(8,128)(2,1)S(1)} collective-permute-done((bf16[64,1792]{1,0:T(8,128)(2,1)S(1)}, bf16[64,1792]{1,0:T(8,128)(2,1)S(1)}, u32[]{:S(2)}, u32[]{:S(2)}) %collective-permute-start.9) | collective-permute-done | bytes 229408 | tf_op jit(solution)/shard_map/ppermute | solution.py:386
  142.0 3.4 %collective-permute-done.8 = bf16[64,1792]{1,0:T(8,128)(2,1)S(1)} collective-permute-done((bf16[64,1792]{1,0:T(8,128)(2,1)S(1)}, bf16[64,1792]{1,0:T(8,128)(2,1)S(1)}, u32[]{:S(2)}, u32[]{:S(2)}) %collective-permute-start.8) | collective-permute-done | bytes 229408 | tf_op jit(solution)/shard_map/ppermute | solution.py:386
  145.4 0.1 add_convert_fusion.1
  145.5 0.8 pad_maximum_fusion.2
  (2 shorter events, 0.1 us)
Async XLA Ops:
  0.0 6.0 %copy-start.2 = (bf16[128,3072]{1,0:T(8,128)(2,1)S(1)}, bf16[128,3072]{1,0:T(8,128)(2,1)}, u32[]{:S(2)}) copy-start(bf16[128,3072]{1,0:T(8,128)(2,1)} %q_ref.1) | copy-start | bytes 2359300
  0.0 22.3 %collective-permute-start.2 = (bf16[576,8192]{1,0:T(8,128)(2,1)}, bf16[576,8192]{1,0:T(8,128)(2,1)}, u32[]{:S(2)}, u32[]{:S(2)}) collective-permute-start(bf16[576,8192]{1,0:T(8,128)(2,1)} %bitcast.10), channel_id=1, source_target_pairs={{0,4},{4,0},{8,12},{12,8},{1,5},{5,1},{9,13},{13,9},{2,6},{6,2},{1... | collective-permute-start | bytes 28311560 | tf_op jit(solution)/shard_map/ppermute | solution.py:356
  0.7 21.5 %collective-permute-start = (s32[1,64]{1,0:T(1,128)}, s32[1,64]{1,0:T(1,128)S(1)}, u32[]{:S(2)}, u32[]{:S(2)}) collective-permute-start(s32[1,64]{1,0:T(1,128)} %param.9), channel_id=1, source_target_pairs={{0,8},{4,12},{8,0},{12,4},{1,9},{5,13},{9,1},{13,5},{2,10},{6,14},... | collective-permute-start | bytes 776 | tf_op jit(solution)/shard_map/ppermute | solution.py:352
  3.1 19.2 %collective-permute-start.1 = (bf16[64,3072]{1,0:T(8,128)(2,1)S(1)}, bf16[64,3072]{1,0:T(8,128)(2,1)S(1)}, u32[]{:S(2)}, u32[]{:S(2)}) collective-permute-start(bf16[64,3072]{1,0:T(8,128)(2,1)S(1)} %get-tuple-element.11.q_ref), channel_id=1, source_target_pairs={{0,8},{4,12},{8,0},{12,4},{1,9},{5,13},{9,1},{13,5},{2,10},{6,14},... | collective-permute-start | bytes 1179656 | tf_op jit(solution)/shard_map/ppermute | solution.py:354
  3.4 34.7 %collective-permute-start.10 = (bf16[64,3072]{1,0:T(8,128)(2,1)S(1)}, bf16[64,3072]{1,0:T(8,128)(2,1)S(1)}, u32[]{:S(2)}, u32[]{:S(2)}) collective-permute-start(bf16[64,3072]{1,0:T(8,128)(2,1)S(1)} %get-tuple-element.12.q_ref), channel_id=1, source_target_pairs={{0,8},{4,12},{8,0},{12,4},{1,9},{5,13},{9,1},{13,5},{2,10},{6,14},... | collective-permute-start | bytes 1179656 | tf_op jit(solution)/shard_map/ppermute | solution.py:354
  38.0 28.4 %collective-permute-start.3 = (bf16[64,2176]{1,0:T(8,128)(2,1)S(1)}, bf16[64,2176]{1,0:T(8,128)(2,1)S(1)}, u32[]{:S(2)}, u32[]{:S(2)}) collective-permute-start(bf16[64,2176]{1,0:T(8,128)(2,1)S(1)} %shard_map.73), channel_id=1, source_target_pairs={{0,8},{4,12},{8,0},{12,4},{1,9},{5,13},{9,1},{13,5},{2,10},{6,14},... | collective-permute-start | bytes 835592 | tf_op jit(solution)/shard_map/ppermute | solution.py:367
  53.7 25.2 %collective-permute-start.11 = (bf16[64,2176]{1,0:T(8,128)(2,1)S(1)}, bf16[64,2176]{1,0:T(8,128)(2,1)S(1)}, u32[]{:S(2)}, u32[]{:S(2)}) collective-permute-start(bf16[64,2176]{1,0:T(8,128)(2,1)S(1)} %shard_map.78), channel_id=1, source_target_pairs={{0,8},{4,12},{8,0},{12,4},{1,9},{5,13},{9,1},{13,5},{2,10},{6,14},... | collective-permute-start | bytes 835592 | tf_op jit(solution)/shard_map/ppermute | solution.py:367
  67.0 17.2 %collective-permute-start.5 = (bf16[64,2048]{1,0:T(8,128)(2,1)S(1)}, bf16[64,2048]{1,0:T(8,128)(2,1)S(1)}, u32[]{:S(2)}, u32[]{:S(2)}) collective-permute-start(bf16[64,2048]{1,0:T(8,128)(2,1)S(1)} %shard_map.76), channel_id=1, source_target_pairs={{0,8},{4,12},{8,0},{12,4},{1,9},{5,13},{9,1},{13,5},{2,10},{6,14},... | collective-permute-start | bytes 786440 | tf_op jit(solution)/shard_map/ppermute | solution.py:373
  79.5 5.3 %collective-permute-start.13 = (bf16[64,2048]{1,0:T(8,128)(2,1)S(1)}, bf16[64,2048]{1,0:T(8,128)(2,1)S(1)}, u32[]{:S(2)}, u32[]{:S(2)}) collective-permute-start(bf16[64,2048]{1,0:T(8,128)(2,1)S(1)} %shard_map.80), channel_id=1, source_target_pairs={{0,8},{4,12},{8,0},{12,4},{1,9},{5,13},{9,1},{13,5},{2,10},{6,14},... | collective-permute-start | bytes 786440 | tf_op jit(solution)/shard_map/ppermute | solution.py:373
  81.0 7.5 %collective-permute-start.4 = (bf16[64,2048]{1,0:T(8,128)(2,1)S(1)}, bf16[64,2048]{1,0:T(8,128)(2,1)S(1)}, u32[]{:S(2)}, u32[]{:S(2)}) collective-permute-start(bf16[64,2048]{1,0:T(8,128)(2,1)S(1)} %shard_map.76), channel_id=1, source_target_pairs={{0,4},{4,0},{8,12},{12,8},{1,5},{5,1},{9,13},{13,9},{2,6},{6,2},{1... | collective-permute-start | bytes 786440 | tf_op jit(solution)/shard_map/ppermute | solution.py:374
  84.2 4.4 %collective-permute-start.6 = (bf16[64,2048]{1,0:T(8,128)(2,1)S(1)}, bf16[64,2048]{1,0:T(8,128)(2,1)S(1)}, u32[]{:S(2)}, u32[]{:S(2)}) collective-permute-start(bf16[64,2048]{1,0:T(8,128)(2,1)S(1)} %collective-permute-done.5), channel_id=1, source_target_pairs={{0,4},{4,0},{8,12},{12,8},{1,5},{5,1},{9,13},{13,9},{2,6},{6,2},{1... | collective-permute-start | bytes 786440 | tf_op jit(solution)/shard_map/ppermute | solution.py:374
  84.2 11.2 %collective-permute-start.12 = (bf16[64,2048]{1,0:T(8,128)(2,1)S(1)}, bf16[64,2048]{1,0:T(8,128)(2,1)S(1)}, u32[]{:S(2)}, u32[]{:S(2)}) collective-permute-start(bf16[64,2048]{1,0:T(8,128)(2,1)S(1)} %shard_map.80), channel_id=1, source_target_pairs={{0,4},{4,0},{8,12},{12,8},{1,5},{5,1},{9,13},{13,9},{2,6},{6,2},{1... | collective-permute-start | bytes 786440 | tf_op jit(solution)/shard_map/ppermute | solution.py:374
  84.8 10.7 %collective-permute-start.14 = (bf16[64,2048]{1,0:T(8,128)(2,1)S(1)}, bf16[64,2048]{1,0:T(8,128)(2,1)S(1)}, u32[]{:S(2)}, u32[]{:S(2)}) collective-permute-start(bf16[64,2048]{1,0:T(8,128)(2,1)S(1)} %collective-permute-done.13), channel_id=1, source_target_pairs={{0,4},{4,0},{8,12},{12,8},{1,5},{5,1},{9,13},{13,9},{2,6},{6,2},{1... | collective-permute-start | bytes 786440 | tf_op jit(solution)/shard_map/ppermute | solution.py:374
  88.6 3.1 %copy-start = (bf16[2048,1792]{1,0:T(8,128)(2,1)S(1)}, bf16[2048,1792]{1,0:T(8,128)(2,1)}, u32[]{:S(2)}) copy-start(bf16[2048,1792]{1,0:T(8,128)(2,1)} %w_ref.3) | copy-start | bytes 22020100
  95.6 3.1 %copy-start.1 = (bf16[2048,1792]{1,0:T(8,128)(2,1)S(1)}, bf16[2048,1792]{1,0:T(8,128)(2,1)}, u32[]{:S(2)}) copy-start(bf16[2048,1792]{1,0:T(8,128)(2,1)} %w_ref.3) | copy-start | bytes 22020100
  102.4 10.1 %collective-permute-start.15 = (bf16[64,1792]{1,0:T(8,128)(2,1)S(1)}, bf16[64,1792]{1,0:T(8,128)(2,1)S(1)}, u32[]{:S(2)}, u32[]{:S(2)}) collective-permute-start(bf16[64,1792]{1,0:T(8,128)(2,1)S(1)} %get-tuple-element.8), channel_id=1, source_target_pairs={{0,2},{1,3},{2,0},{3,1},{4,6},{5,7},{6,4},{7,5},{8,10},{9,11},{10,... | collective-permute-start | bytes 688136 | tf_op jit(solution)/shard_map/ppermute | solution.py:386
  102.5 24.8 %collective-permute-start.17 = (bf16[64,1792]{1,0:T(8,128)(2,1)S(1)}, bf16[64,1792]{1,0:T(8,128)(2,1)S(1)}, u32[]{:S(2)}, u32[]{:S(2)}) collective-permute-start(bf16[64,1792]{1,0:T(8,128)(2,1)S(1)} %get-tuple-element.9), channel_id=1, source_target_pairs={{0,3},{1,0},{2,1},{3,2},{4,7},{5,4},{6,5},{7,6},{8,11},{9,8},{10,9... | collective-permute-start | bytes 688136 | tf_op jit(solution)/shard_map/ppermute | solution.py:386
  105.0 30.6 %collective-permute-start.16 = (bf16[64,1792]{1,0:T(8,128)(2,1)S(1)}, bf16[64,1792]{1,0:T(8,128)(2,1)S(1)}, u32[]{:S(2)}, u32[]{:S(2)}) collective-permute-start(bf16[64,1792]{1,0:T(8,128)(2,1)S(1)} %get-tuple-element.10), channel_id=1, source_target_pairs={{0,1},{1,2},{2,3},{3,0},{4,5},{5,6},{6,7},{7,4},{8,9},{9,10},{10,1... | collective-permute-start | bytes 688136 | tf_op jit(solution)/shard_map/ppermute | solution.py:386
  105.0 32.1 %collective-permute-start.7 = (bf16[64,1792]{1,0:T(8,128)(2,1)S(1)}, bf16[64,1792]{1,0:T(8,128)(2,1)S(1)}, u32[]{:S(2)}, u32[]{:S(2)}) collective-permute-start(bf16[64,1792]{1,0:T(8,128)(2,1)S(1)} %get-tuple-element.5), channel_id=1, source_target_pairs={{0,2},{1,3},{2,0},{3,1},{4,6},{5,7},{6,4},{7,5},{8,10},{9,11},{10,... | collective-permute-start | bytes 688136 | tf_op jit(solution)/shard_map/ppermute | solution.py:386
  106.4 35.6 %collective-permute-start.9 = (bf16[64,1792]{1,0:T(8,128)(2,1)S(1)}, bf16[64,1792]{1,0:T(8,128)(2,1)S(1)}, u32[]{:S(2)}, u32[]{:S(2)}) collective-permute-start(bf16[64,1792]{1,0:T(8,128)(2,1)S(1)} %get-tuple-element.6), channel_id=1, source_target_pairs={{0,3},{1,0},{2,1},{3,2},{4,7},{5,4},{6,5},{7,6},{8,11},{9,8},{10,9... | collective-permute-start | bytes 688136 | tf_op jit(solution)/shard_map/ppermute | solution.py:386
  112.6 32.9 %collective-permute-start.8 = (bf16[64,1792]{1,0:T(8,128)(2,1)S(1)}, bf16[64,1792]{1,0:T(8,128)(2,1)S(1)}, u32[]{:S(2)}, u32[]{:S(2)}) collective-permute-start(bf16[64,1792]{1,0:T(8,128)(2,1)S(1)} %get-tuple-element.7), channel_id=1, source_target_pairs={{0,1},{1,2},{2,3},{3,0},{4,5},{5,6},{6,7},{7,4},{8,9},{9,10},{10,1... | collective-permute-start | bytes 688136 | tf_op jit(solution)/shard_map/ppermute | solution.py:386

commit v3 on v0

v3 whole, which is shorter than its diff:
```python
import functools
import math

import jax
import jax.numpy as jnp
from jax import lax
from jax.experimental import pallas as pl
from jax.experimental.pallas import tpu as pltpu
from jax.sharding import PartitionSpec as P

BT = 64
WIDE = 128
CHUNK = 8
SMALL = 4
PIECES = 2
NEVER = -1e30
FAR = 1 << 30
MIB = 1024 * 1024
META = 67


def attend_kernel(blocks_held, jobs, fresh, keep, *refs):
    refs = list(refs)
    n = len(jobs)

    def take(k):
        out = refs[:k]
        del refs[:k]
        return out

    (meta,) = take(1)
    queries = take(n)
    wa_hbm, own_hbm, sib_hbm, wv_hbm = take(4)
    saved, listed = ([], None) if fresh else (take(n), take(1)[0])
    outs = take(n)
    kept = take(n) if keep else []
    if keep:
        (listed,) = take(1)
    raws = take(n) if fresh else []
    kts = take(n)
    q_full, wa, wv = take(3)
    accs, stores, peaks, totals = take(2), take(2), take(2), take(2)
    if fresh and not keep:
        (listed,) = take(1)
    edge, wa_sem, wv_sem, kv_sems, keep_sems = take(5)

    tokens = queries[0].shape[0]
    heads, nope, lat = wa.shape
    width = kts[0].shape[0]
    vd = wv.shape[2]
    head_width = nope + width - lat
    fold = head_width ** -0.5 * math.log2(math.e)
    strides = [0]
    for kt in kts:
        strides.append(strides[-1] + kt.shape[1] // BT + 2)

    wa_copy = pltpu.make_async_copy(wa_hbm, wa, wa_sem)
    wv_copy = pltpu.make_async_copy(wv_hbm, wv, wv_sem)
    wa_copy.start()

    def gather(j):
        row0, list0 = META * j, strides[j]
        room = kts[j].shape[1] // BT
        start, mine, other = meta[row0 + 64], meta[row0 + 65], meta[row0 + 66]
        raw, sem = raws[j], kv_sems.at[j]
        holders = [
            h for h in (("own", mine, own_hbm), ("sib", other, sib_hbm)) if h[0] in jobs[j][0]
        ]

        def fetch(block, slot):
            owner = block // blocks_held
            col = pl.multiple_of((block % blocks_held) // 2 * WIDE, WIDE)
            for _, holder, source in holders:
                @pl.when(owner == holder)
                def _(source=source):
                    pltpu.make_async_copy(source.at[:, pl.ds(col, WIDE)], raw.at[slot], sem).start()

        def scan(i, carry):
            full, part = carry
            block = meta[row0 + i]
            owner = block // blocks_held
            here = jnp.bool_(False)
            for _, holder, _ in holders:
                here = here | (owner == holder)
            whole = here & (block * BT + BT - 1 <= start)
            some = here & (block * BT + BT - 1 > start) & (block * BT <= start + jobs[j][1] - 1)

            @pl.when(whole)
            def _():
                fetch(block, full)
                listed[list0 + full] = block

            @pl.when(some)
            def _():
                edge[part] = block

            return full + whole.astype(jnp.int32), part + some.astype(jnp.int32)

        full, part = lax.fori_loop(0, 64, scan, (jnp.int32(0), jnp.int32(0)))

        def fetch_edge(i, _):
            fetch(edge[i], full + i)
            listed[list0 + full + i] = edge[i]
            return 0

        lax.fori_loop(0, part, fetch_edge, 0)
        count = full + part

        def fill(i, _):
            pltpu.make_async_copy(own_hbm.at[:, pl.ds(0, WIDE)], raw.at[i], sem).start()
            listed[list0 + i] = 0
            return 0

        lax.fori_loop(count, (count + SMALL - 1) // SMALL * SMALL, fill, 0)
        listed[list0 + room] = full
        listed[list0 + room + 1] = count

    def join(j):
        raw, kt, list0 = raws[j], kts[j], strides[j]
        count = listed[list0 + kt.shape[1] // BT + 1]
        slots = (count + SMALL - 1) // SMALL * SMALL

        def land(i, _):
            pltpu.make_async_copy(own_hbm.at[:, pl.ds(0, WIDE)], raw.at[0], kv_sems.at[j]).wait()
            return 0

        lax.fori_loop(0, slots, land, 0)

        def pair(i, _):
            left = raw[2 * i]
            right = raw[2 * i + 1]
            left_swapped = jnp.concatenate([left[:, BT:], left[:, :BT]], axis=1)
            right_swapped = jnp.concatenate([right[:, BT:], right[:, :BT]], axis=1)
            low = jnp.where(listed[list0 + 2 * i] % 2 == 1, left_swapped, left)
            high = jnp.where(listed[list0 + 2 * i + 1] % 2 == 1, right, right_swapped)
            lane = lax.broadcasted_iota(jnp.int32, (width, WIDE), 1)
            kt[:, pl.ds(pl.multiple_of(i * WIDE, WIDE), WIDE)] = jnp.where(lane < BT, low, high)
            return 0

        lax.fori_loop(0, slots // 2, pair, 0)

    if fresh:
        for j in range(n):
            gather(j)
    else:
        for j in range(n):
            pltpu.make_async_copy(saved[j], kts[j], kv_sems.at[j]).start()
    wv_copy.start()
    wa_copy.wait()
    rows_each = heads * tokens
    for j in range(n):
        for h in range(heads):
            base = h * head_width
            latent_part = jnp.dot(
                queries[j][:, base : base + nope], wa[h], preferred_element_type=jnp.float32
            )
            rows = slice(j * rows_each + h * tokens, j * rows_each + (h + 1) * tokens)
            q_full[rows, 0:lat] = (latent_part * fold).astype(jnp.bfloat16)
            turned = queries[j][:, base + nope : base + head_width].astype(jnp.float32)
            q_full[rows, lat:width] = (turned * fold).astype(jnp.bfloat16)
    for j in range(n):
        if fresh:
            join(j)
        else:
            pltpu.make_async_copy(saved[j], kts[j], kv_sems.at[j]).wait()
        if keep:
            pltpu.make_async_copy(kts[j], kept[j], keep_sems.at[j]).start()
    wv_copy.wait()

    tile = accs[0].shape[0]
    tile_heads = tile // tokens
    lane = lax.broadcasted_iota(jnp.int32, (tokens, 128), 1)

    def work(j):
        kt, list0, o_ref = kts[j], strides[j], outs[j]
        room = kt.shape[1] // BT
        first = meta[META * j + 64] + jobs[j][2]
        full = listed[list0 + room]
        count = listed[list0 + room + 1]
        plain_chunks = full // CHUNK
        done = plain_chunks * CHUNK
        small_chunks = (count - done + SMALL - 1) // SMALL

        def row_pair(r, lse_tile):
            row0 = j * rows_each + r * 2 * tile
            bases = [pl.multiple_of(row0, tile), pl.multiple_of(row0 + tile, tile)]
            for i in range(2):
                accs[i][...] = jnp.zeros_like(accs[i])
                peaks[i][...] = jnp.full(peaks[i].shape, NEVER, jnp.float32)
                totals[i][...] = jnp.zeros_like(totals[i])

            def score(i, key0, n):
                stores[i][:, 0 : n * BT] = jnp.dot(
                    q_full[pl.ds(bases[i], tile), :], kt[:, pl.ds(key0, n * BT)],
                    preferred_element_type=jnp.float32,
                )

            def soften(i, n, visible):
                scores = stores[i][:, 0 : n * BT]
                if visible is not None:
                    scores = jnp.where(
                        visible[None], scores.reshape(tile_heads, tokens, n * BT), NEVER
                    ).reshape(tile, n * BT)
                peak = peaks[i][...]
                new_peak = jnp.maximum(peak, jnp.max(scores, axis=1, keepdims=True))
                peaks[i][...] = new_peak
                raised = jnp.exp2(scores - new_peak[:, 0:1])
                keep_share = jnp.exp2(peak - new_peak)
                total = totals[i][...] * keep_share
                for k in range(n * BT // 128):
                    total = total + raised[:, k * 128 : (k + 1) * 128]
                totals[i][...] = total
                return raised.astype(jnp.bfloat16), keep_share[:, 0:1]

            def mix(i, key0, n, raised, keep_share):
                accs[i][...] = accs[i][...] * keep_share + lax.dot_general(
                    raised, kt[0:lat, pl.ds(key0, n * BT)], (((1,), (1,)), ((), ())),
                    preferred_element_type=jnp.float32,
                )

            def chunk(n, total_chunks, start, masked, c, _):
                key0 = pl.multiple_of(start + c * n * BT, 128)
                last = start + (total_chunks - 1) * n * BT
                key1 = pl.multiple_of(jnp.minimum(key0 + n * BT, last), 128)
                visible = None
                if masked:
                    block0 = key0 // BT
                    column = lax.broadcasted_iota(jnp.int32, (tokens, n * BT), 1)
                    position = jnp.zeros((tokens, n * BT), jnp.int32)
                    for b in range(n):
                        at = jnp.where(
                            block0 + b < full, 0,
                            jnp.where(block0 + b < count, listed[list0 + block0 + b] * BT, FAR),
                        )
                        position = jnp.where(column // BT == b, at + column % BT, position)
                    query = first + lax.broadcasted_iota(jnp.int32, (tokens, n * BT), 0)
                    visible = position <= query
                score(1, key0, n)
                raised, share = soften(0, n, visible)
                mix(0, key0, n, raised, share)
                score(0, key1, n)
                raised, share = soften(1, n, visible)
                mix(1, key0, n, raised, share)
                return 0

            @pl.when(plain_chunks > 0)
            def _():
                score(0, 0, CHUNK)
                lax.fori_loop(
                    0, plain_chunks, functools.partial(chunk, CHUNK, plain_chunks, 0, False), 0
                )

            @pl.when(small_chunks > 0)
            def _():
                score(0, pl.multiple_of(done * BT, 128), SMALL)
                lax.fori_loop(
                    0, small_chunks, functools.partial(chunk, SMALL, small_chunks, done * BT, True), 0
                )

            for i in range(2):
                total = jnp.maximum(jnp.sum(totals[i][...], axis=1, keepdims=True), 1e-30)
                lse = peaks[i][:, 0:1] + jnp.log2(total)
                scale = 1.0 / total
                for k in range(tile_heads):
                    h = (r * 2 + i) * tile_heads + k
                    rows = slice(k * tokens, (k + 1) * tokens)
                    mixed = (accs[i][rows, :] * scale[rows, :]).astype(jnp.bfloat16)
                    out = jnp.dot(mixed, wv[h], preferred_element_type=jnp.float32)
                    o_ref[:, pl.ds(pl.multiple_of(h * vd, vd), vd)] = out.astype(jnp.bfloat16)
                    lse_tile = place_log(lse_tile, lane, h, lse[rows, :])
            return lse_tile

        lse_tile = lax.fori_loop(
            0, rows_each // (2 * tile), row_pair, jnp.zeros((tokens, 128), jnp.float32)
        )
        o_ref[:, heads * vd :] = lse_tile.astype(jnp.bfloat16)

    for j in range(n):
        work(j)
    if keep:
        for j in range(n):
            pltpu.make_async_copy(kts[j], kept[j], keep_sems.at[j]).wait()


def place_log(tile, lane, h, value):
    high = value.astype(jnp.bfloat16).astype(jnp.float32)
    middle = (value - high).astype(jnp.bfloat16).astype(jnp.float32)
    low = value - high - middle
    tile = jnp.where(lane == h, high, tile)
    tile = jnp.where(lane == h + 32, middle, tile)
    return jnp.where(lane == h + 64, low, tile)


def attend(metas, queries, jobs, own, sib, w_absorb, w_value, depth, row_tile, saved=None, keep=False):
    fresh = saved is None
    tokens = queries[0].shape[0]
    heads, nope, lat = w_absorb.shape
    vd = w_value.shape[2]
    width = own.shape[0]
    slots = [-(-depth * len(job[0]) // SMALL) * SMALL for job in jobs]
    rows = heads * tokens
    tile = min(row_tile, rows // 2)
    keys = sum(slots) * BT * 2 // 3
    any_space = pl.BlockSpec(memory_space=pl.ANY)
    vmem = pl.BlockSpec(memory_space=pltpu.VMEM)
    smem = pl.BlockSpec(memory_space=pltpu.SMEM)
    lists = sum(slots) + 2 * len(jobs)
    kt_shapes = [(width, s * BT) for s in slots]
    out_shape = [jax.ShapeDtypeStruct((tokens, heads * vd + 128), jnp.bfloat16) for _ in jobs]
    out_specs = [vmem for _ in jobs]
    if keep:
        out_shape += [jax.ShapeDtypeStruct(s, jnp.bfloat16) for s in kt_shapes]
        out_shape += [jax.ShapeDtypeStruct((lists,), jnp.int32)]
        out_specs += [any_space] * len(jobs) + [smem]
    in_specs = [smem] + [vmem] * len(jobs) + [any_space] * 4
    operands = [jnp.concatenate(metas), *queries, w_absorb, own, sib, w_value]
    if not fresh:
        in_specs += [any_space] * len(jobs) + [smem]
        operands += saved
    scratch = []
    if fresh:
        scratch += [pltpu.VMEM((s, width, WIDE), jnp.bfloat16) for s in slots]
    scratch += [pltpu.VMEM(s, jnp.bfloat16) for s in kt_shapes]
    scratch += [
        pltpu.VMEM((len(jobs) * rows, width), jnp.bfloat16),
        pltpu.VMEM(w_absorb.shape, jnp.bfloat16),
        pltpu.VMEM(w_value.shape, jnp.bfloat16),
        *[pltpu.VMEM((tile, lat), jnp.float32)] * 2,
        *[pltpu.VMEM((tile, CHUNK * BT), jnp.float32)] * 2,
        *[pltpu.VMEM((tile, 128), jnp.float32)] * 4,
    ]
    if fresh and not keep:
        scratch += [pltpu.SMEM((lists,), jnp.int32)]
    scratch += [
        pltpu.SMEM((64,), jnp.int32),
        pltpu.SemaphoreType.DMA,
        pltpu.SemaphoreType.DMA,
        pltpu.SemaphoreType.DMA((len(jobs),)),
        pltpu.SemaphoreType.DMA((len(jobs),)),
    ]
    return pl.pallas_call(
        functools.partial(attend_kernel, own.shape[1] // BT, jobs, fresh, keep),
        out_shape=out_shape,
        in_specs=in_specs,
        out_specs=out_specs,
        scratch_shapes=scratch,
        compiler_params=pltpu.CompilerParams(vmem_limit_bytes=56 * MIB),
        cost_estimate=pl.CostEstimate(
            flops=2 * rows * keys * (width + lat),
            bytes_accessed=2 * keys * width * 2,
            transcendentals=rows * keys,
        ),
    )(*operands)


def read_log(ref, rows, heads):
    tail = ref[rows, ref.shape[1] - 128 :].astype(jnp.float32)
    return tail[:, 0:heads] + tail[:, 32 : 32 + heads] + tail[:, 64 : 64 + heads]


def merge(parts, heads, out, out_rows, with_log):
    vd = (parts[0][0].shape[1] - 128) // heads
    logs = [read_log(ref, rows, heads) for ref, rows in parts]
    peak = functools.reduce(jnp.maximum, logs)
    shares = [jnp.exp2(value - peak) for value in logs]
    total = functools.reduce(jnp.add, shares)
    norm = 1.0 / total
    for h in range(heads):
        columns = slice(h * vd, (h + 1) * vd)
        mixed = sum(
            ref[rows, columns].astype(jnp.float32) * (share * norm)[:, h : h + 1]
            for (ref, rows), share in zip(parts, shares)
        )
        out[out_rows, columns] = mixed.astype(jnp.bfloat16)
    if with_log:
        log = peak + jnp.log2(total)
        tokens = log.shape[0]
        lane = lax.broadcasted_iota(jnp.int32, (tokens, 128), 1)
        tile = jnp.zeros((tokens, 128), jnp.float32)
        for h in range(heads):
            tile = place_log(tile, lane, h, log[:, h : h + 1])
        out[out_rows, heads * vd :] = tile.astype(jnp.bfloat16)


def small_call(kernel, shape, operands):
    vmem = pl.BlockSpec(memory_space=pltpu.VMEM)
    return pl.pallas_call(
        kernel,
        out_shape=jax.ShapeDtypeStruct(shape, jnp.bfloat16),
        in_specs=[vmem] * len(operands),
        out_specs=vmem,
        compiler_params=pltpu.CompilerParams(vmem_limit_bytes=16 * MIB),
        cost_estimate=pl.CostEstimate(
            flops=4 * shape[0] * shape[1], bytes_accessed=8 * shape[0] * shape[1], transcendentals=0
        ),
    )(*operands)


def combine(partials, heads):
    tokens = min(p.shape[0] for p, _ in partials)
    columns = partials[0][0].shape[1]

    def kernel(*refs):
        parts = [(ref, slice(r, r + tokens)) for ref, (_, r) in zip(refs, partials)]
        merge(parts, heads, refs[-1], slice(0, tokens), False)

    return small_call(kernel, (tokens, columns - 128), [p for p, _ in partials])


def pack_for_other(far, near, near_row, side, heads):
    tokens, columns = far.shape

    def kernel(far_ref, near_ref, side_ref, out):
        out[0:tokens, :] = far_ref[...]
        parts = [(near_ref, slice(near_row, near_row + tokens)), (side_ref, slice(0, tokens))]
        merge(parts, heads, out, slice(tokens, 2 * tokens), True)

    return small_call(kernel, (2 * tokens, columns), [far, near, side])


def settle(sent, got, heads):
    rows, columns = sent.shape
    half = rows // 2
    low, high = slice(0, half), slice(half, rows)

    def kernel(sent_ref, got_ref, out):
        merge([(sent_ref, high), (got_ref, low)], heads, out, low, False)
        merge([(sent_ref, low), (got_ref, high)], heads, out, high, False)

    return small_call(kernel, (rows, columns - 128), [sent, got])


def project_kernel(x_ref, w_ref, o_ref):
    o_ref[...] = jnp.dot(x_ref[...], w_ref[...], preferred_element_type=jnp.float32).astype(jnp.bfloat16)


def project(x, w):
    rows, depth = x.shape
    columns = w.shape[1]
    wide = 256 if columns % 256 == 0 else columns
    return pl.pallas_call(
        project_kernel,
        out_shape=jax.ShapeDtypeStruct((rows, columns), jnp.bfloat16),
        grid=(columns // wide,),
        in_specs=[
            pl.BlockSpec((rows, depth), lambda j: (0, 0)),
            pl.BlockSpec((depth, wide), lambda j: (0, j)),
        ],
        out_specs=pl.BlockSpec((rows, wide), lambda j: (0, j)),
        compiler_params=pltpu.CompilerParams(vmem_limit_bytes=60 * MIB),
        cost_estimate=pl.CostEstimate(
            flops=2 * rows * depth * columns,
            bytes_accessed=2 * (rows * depth + depth * columns + rows * columns),
            transcendentals=0,
        ),
    )(x, w)


def body(queries, latent, selection, span_offset, w_absorb, w_value, w_out):
    owners = lax.axis_size("ctx")
    groups = lax.axis_size("head")
    me = lax.axis_index("ctx")
    column = lax.axis_index("head")
    chips = owners // 2
    depth = 3 * selection.shape[1] // (2 * owners)
    heads = w_absorb.shape[0]
    tokens = queries.shape[0]
    piece = tokens // PIECES
    sibling = [(i, i ^ 1) for i in range(owners)]
    turns = range(1, chips)
    ahead = {t: [(i, (i + 2 * t) % owners) for i in range(owners)] for t in turns}
    back = {t: [(i, (i - 2 * t) % owners) for i in range(owners)] for t in turns}
    own = latent.T

    def meta_of(row, index):
        return jnp.concatenate(
            [row[0], jnp.stack([span_offset[0] + index * tokens, me, me ^ 1])]
        ).astype(jnp.int32)

    far_queries = {t: lax.ppermute(queries, "ctx", ahead[t]) for t in turns}
    sib = lax.ppermute(own, "ctx", sibling)
    far_rows = {t: lax.ppermute(selection, "ctx", ahead[t]) for t in turns}
    my_meta = meta_of(selection, me)
    metas = [meta_of(far_rows[t], (me - 2 * t) % owners) for t in turns] + [my_meta]
    (near,) = attend(
        [my_meta], [queries], [(("own",), tokens, 0)], own, own, w_absorb, w_value, depth, 1024
    )
    outputs = []
    saved = None
    pieces = []
    last = near
    for c in range(PIECES):
        rows = slice(c * piece, (c + 1) * piece)
        jobs = [(("own", "sib"), tokens, c * piece) for _ in turns] + [(("sib",), tokens, c * piece)]
        cuts = [far_queries[t][rows] for t in turns] + [queries[rows]]
        *cuts, last = lax.optimization_barrier((*cuts, last))
        results = attend(
            metas, cuts, jobs, own, sib, w_absorb, w_value, depth, 512, saved, saved is None
        )
        if saved is None:
            saved = list(results[len(jobs) :])
        fars, side = results[: len(jobs) - 1], results[len(jobs) - 1]
        if chips == 2:
            sent = pack_for_other(fars[0], near, c * piece, side, heads)
            last = sent
            pieces.append((sent, lax.ppermute(sent, "ctx", ahead[1])))
        else:
            arrived = [lax.ppermute(far, "ctx", back[t]) for t, far in zip(turns, fars)]
            pieces.append(combine([(a, 0) for a in arrived] + [(side, 0), (near, c * piece)], heads))
    for c in range(PIECES):
        if chips == 2:
            sent, got = pieces[c]
            mine = settle(sent, got, heads)
        else:
            mine = pieces[c]
            mine = jnp.concatenate([mine] + [lax.ppermute(mine, "ctx", ahead[t]) for t in turns], axis=0)
        pair = jnp.concatenate([mine, lax.ppermute(mine, "ctx", sibling)], axis=0)
        shares = project(pair, w_out)

        def share_of(block):
            turn = (me // 2 - block // 2) % chips
            place = (me + block) % 2 * chips + turn
            return lax.dynamic_slice_in_dim(shares, place * piece, piece, 0)

        arrived = [share_of(column)]
        for s in sorted(range(1, groups), key=lambda s: -min(s, groups - s)):
            shift = [(i, (i + s) % groups) for i in range(groups)]
            arrived.append(lax.ppermute(share_of((column + s) % groups), "head", shift))
        outputs.append(sum(a.astype(jnp.float32) for a in arrived).astype(jnp.bfloat16))
    return jnp.concatenate(outputs, axis=0)


def solution(mesh):
    placed = (
        P(("groups", "ctx"), "head"),
        P(("groups", "ctx"), None),
        P(("groups", "ctx"), None),
        P("groups"),
        P("head", None, None),
        P("head", None, None),
        P("head", "ctx"),
    )
    return jax.shard_map(
        body, mesh=mesh, in_specs=placed, out_specs=P(("groups", "head"), "ctx"), check_vma=False
    )
```

time: 297 us -> 164 us (0.55)
  waiting for transfers between devices: 144 us -> 45.9 us
  Pallas kernels: 0 us -> 88.4 us
  matrix products: 48.2 us -> 0 us
  other arithmetic: 41.3 us -> 6.37 us
  local copies, waits for them, and re-layouts: 39.2 us -> 8.75 us
  between operations: 14.2 us -> 1.06 us
  starting transfers between devices: 9.95 us -> 15 us
    pallas_call x0 -> x9, Pallas kernels: none -> 88.4 us  [the longest x3 69 us: attend(): pl.pallas_call(functools.partial(attend_kernel, own.shape[1] // BT, jobs,...]
    all_to_all x2 -> x0, waiting for transfers between devices: 80.3 us -> none  [the longest x1 80.3 us: body(): lax.all_to_all(packed, 'ctx', split_axis=0, concat_axis=0, tiled=True)]
    dot_general x5 -> x0, matrix products: 48.2 us -> none  [the longest x1 23 us: body(): lax.dot_general(q_full, key_rows, (((1,), (1,)), ((), ())), preferred_ele...]
    ppermute x0 -> x13, waiting for transfers between devices: none -> 45.9 us  [the longest x2 23.3 us: body(): pieces.append((sent, lax.ppermute(sent, 'ctx', ahead[1])))]
    reduce_scatter x1 -> x0, waiting for transfers between devices: 39.6 us -> none  [body(): lax.psum_scatter(jnp.dot(gathered, w_out, preferred_element_type=jnp.floa...]
    all_gather x1 -> x0, waiting for transfers between devices: 23.7 us -> none  [body(): gathered = lax.all_gather(head_out, 'ctx', axis=0, tiled=True)]
    gather x2 -> x0, local copies, waits for them, and re-layouts: 17.8 us -> none  [the longest x1 11 us: body(): stored[local_index]]
    reduce_sum x3 -> x0, other arithmetic: 17.5 us -> none  [the longest x1 17.2 us: body(): jnp.sum(shifted, axis=-1, keepdims=True)]
  transfers between devices with their start and end apart: 4 -> 13, of which waited for: 3 -> 5; matrix products, arithmetic and copies ran while one was open for 7% -> 6% of each run, Pallas kernels for 0% -> 21%
where the time goes in v3:
time: 164 us; the launch traced here: 166 us
  Pallas kernels  88.4 us (54%)
  waiting for transfers between devices  45.9 us (28%)
  starting transfers between devices  15 us (9%)
  local copies, waits for them, and re-layouts  8.75 us (5%)
  other arithmetic  6.37 us (4%)
    pallas_call x3, Pallas kernels, attend(): pl.pallas_call(functools.partial(attend_kernel, own.shape[1] // BT, jobs,...  69 us
    ppermute x2, waiting for transfers between devices, body(): pieces.append((sent, lax.ppermute(sent, 'ctx', ahead[1])))  23.3 us
    ppermute x6, waiting for transfers between devices, body(): arrived.append(lax.ppermute(share_of((column + s) % groups), 'head', shift))  22.6 us
    pallas_call x2, Pallas kernels, project(): pl.pallas_call(project_kernel, out_shape=jax.ShapeDtypeStruct((rows, colu...  15.9 us
    ppermute x6, starting transfers between devices, body(): arrived.append(lax.ppermute(share_of((column + s) % groups), 'head', shift))  9.79 us
    unnamed x14, local copies, waits for them, and re-layouts  3.82 us
    pallas_call x4, Pallas kernels, small_call(): pl.pallas_call(kernel, out_shape=jax.ShapeDtypeStruct(shape, jnp.bfloat16...  3.48 us
  transfers between devices with their start and end apart: 13, of which 5 were waited for; matrix products, arithmetic and copies ran while one was open for 6% of the time, Pallas kernels for 21%

profile of v3, /device:TPU:0, one launch (start us, length us, event | category | flops | bytes accessed | tf_op | source)
XLA Modules:
  0.0 165.6 jit_solution(4690625379170895975)
XLA Ops:
  0.0 0.5 collective-permute-start.2
  0.5 2.5 %collective-permute-start = (s32[1,64]{1,0:T(1,128)}, s32[1,64]{1,0:T(1,128)S(1)}, u32[]{:S(2)}, u32[]{:S(2)}) collective-permute-start(s32[1,64]{1,0:T(1,128)} %param.9), channel_id=1, source_target_pairs={{0,8},{4,12},{8,0},{12,4},{1,9},{5,13},{9,1},{13,5},{2,10},{6,14},... | collective-permute-start | bytes 776 | tf_op jit(solution)/shard_map/ppermute | solution.py:482
  2.9 0.1 collective-permute-start.1
  3.7 1.3 pad_add_fusion.refs_0_
  4.9 0.0 copy-start.5
  4.9 0.0 copy-start.6
  4.9 17.6 %shard_map.73.near_ref = bf16[128,2176]{1,0:T(8,128)(2,1)} custom-call(s32[67]{0:T(128)} %pad_add_fusion.refs_0_, bf16[128,3072]{1,0:T(8,128)(2,1)} %refs_1_.1, bf16[16,128,512]{2,1,0:T(8,128)(2,1)} %refs_3_.3, bf16[576,8192]{1,0:T(8,128)(2,1)} %bitcast.11, bf16[576,8192]{1,0:T(8,128)(2,1)} %bitcast.12, bf16[16,512,128]{2,1,0:T(8,128)(2,1)} %refs_6_.3), custom_call_target="tpu_custom_call" | custom-call | flops 4563402752 | bytes 2359296 | tf_op jit(solution)/shard_map/pallas_call | solution.py:341
  22.5 0.0 copy-done.5
  22.5 0.9 fusion
  23.5 0.0 collective-permute-done
  23.5 0.0 copy-done.6
  23.5 0.6 concatenate.19.refs_0_
  24.1 0.0 collective-permute-done.1
  24.1 0.9 fusion.1
  25.1 0.0 copy-start
  25.1 0.0 collective-permute-done.2.refs_5_
  25.1 28.6 %shard_map.74 = (bf16[64,2176]{1,0:T(8,128)(2,1)}, bf16[64,2176]{1,0:T(8,128)(2,1)}, bf16[576,3072]{1,0:T(8,128)(2,1)}, bf16[576,1536]{1,0:T(8,128)(2,1)}, s32[76]{0:T(128)}) custom-call(s32[134]{0:T(256)} %concatenate.19.refs_0_, bf16[64,3072]{1,0:T(8,128)(2,1)} %get-tuple-element.16.refs_1_, bf16[64,3072]{1,0:T(8,128)(2,1)} %get-tuple-element.17.refs_2_, ...), custom_call_target="tpu_custom_call" | custom-call | flops 6845104128 | bytes 7077888 | tf_op jit(solution)/shard_map/pallas_call | solution.py:341
  53.7 0.0 copy-done
  53.7 0.0 copy-start.3
  53.7 0.9 copy-done.3
  54.6 0.0 copy-start.4
  54.6 1.0 copy-done.4
  55.6 0.7 shard_map.75.sent_ref
  56.3 22.9 %shard_map.78 = (bf16[64,2176]{1,0:T(8,128)(2,1)}, bf16[64,2176]{1,0:T(8,128)(2,1)}) custom-call(s32[134]{0:T(256)} %concatenate.19.refs_0_, bf16[64,3072]{1,0:T(8,128)(2,1)} %get-tuple-element.20.refs_1_, bf16[64,3072]{1,0:T(8,128)(2,1)} %get-tuple-element.21.refs_2_, bf16[16,128,512]{2,1,0:T(8,128)(2,1)} %refs_3_.3, bf16[576,8192]{1,0:T(8,128)(2,1)} %bitcast.14, ...), custom_call_target="tpu_custom_call" | custom-call | flops 6845104128 | bytes 7077888 | tf_op jit(solution)/shard_map/pallas_call | solution.py:341
  79.2 0.0 copy-start.1
  79.2 0.9 copy-done.1
  80.2 0.0 copy-start.2
  80.2 1.0 copy-done.2
  81.1 0.7 shard_map.79.sent_ref
  81.8 0.1 collective-permute-start.8
  81.9 2.0 %collective-permute-start.3 = (bf16[128,2176]{1,0:T(8,128)(2,1)S(1)}, bf16[128,2176]{1,0:T(8,128)(2,1)S(1)}, u32[]{:S(2)}, u32[]{:S(2)}) collective-permute-start(bf16[128,2176]{1,0:T(8,128)(2,1)S(1)} %shard_map.75.sent_ref), channel_id=1, source_target_pairs={{0,8},{4,12},{8,0},{12,4},{1,9},{5,13},{9,1},{13,5},{2,10},{6,14},... | collective-permute-start | bytes 1671176 | tf_op jit(solution)/shard_map/ppermute | solution.py:506
  83.9 13.4 %collective-permute-done.8.got_ref = bf16[128,2176]{1,0:T(8,128)(2,1)S(1)} collective-permute-done((bf16[128,2176]{1,0:T(8,128)(2,1)S(1)}, bf16[128,2176]{1,0:T(8,128)(2,1)S(1)}, u32[]{:S(2)}, u32[]{:S(2)}) %collective-permute-start.8) | collective-permute-done | bytes 557088 | tf_op jit(solution)/shard_map/ppermute | solution.py:506
  97.4 1.0 shard_map.80
  98.4 0.1 collective-permute-start.9
  98.7 9.8 %collective-permute-done.3.got_ref = bf16[128,2176]{1,0:T(8,128)(2,1)S(1)} collective-permute-done((bf16[128,2176]{1,0:T(8,128)(2,1)S(1)}, bf16[128,2176]{1,0:T(8,128)(2,1)S(1)}, u32[]{:S(2)}, u32[]{:S(2)}) %collective-permute-start.3) | collective-permute-done | bytes 557088 | tf_op jit(solution)/shard_map/ppermute | solution.py:506
  108.6 1.0 shard_map.76
  109.6 0.1 collective-permute-start.4
  109.7 0.0 collective-permute-done.9
  109.7 1.1 pad_maximum_fusion.1.x_ref
  110.8 8.0 %shard_map.81 = bf16[256,1792]{1,0:T(8,128)(2,1)} custom-call(bf16[256,2048]{1,0:T(8,128)(2,1)} %pad_maximum_fusion.1.x_ref, bf16[2048,1792]{1,0:T(8,128)(2,1)} %w_ref.3), custom_call_target="tpu_custom_call" | custom-call | flops 1879048192 | bytes 9306112 | tf_op jit(solution)/shard_map/pallas_call | solution.py:441
  118.7 1.2 constant_dynamic-slice_fusion.2
  120.0 3.9 %collective-permute-start.12 = (bf16[64,1792]{1,0:T(8,128)(2,1)S(1)}, bf16[64,1792]{1,0:T(8,128)(2,1)S(1)}, u32[]{:S(2)}, u32[]{:S(2)}) collective-permute-start(bf16[64,1792]{1,0:T(8,128)(2,1)S(1)} %get-tuple-element.31), channel_id=1, source_target_pairs={{0,3},{1,0},{2,1},{3,2},{4,7},{5,4},{6,5},{7,6},{8,11},{9,8},{10,9... | collective-permute-start | bytes 688136 | tf_op jit(solution)/shard_map/ppermute | solution.py:528
  123.8 0.0 collective-permute-start.11
  123.8 1.0 collective-permute-start.10
  124.8 0.0 collective-permute-done.4
  124.8 1.1 pad_maximum_fusion.x_ref
  126.0 8.0 %shard_map.77 = bf16[256,1792]{1,0:T(8,128)(2,1)} custom-call(bf16[256,2048]{1,0:T(8,128)(2,1)} %pad_maximum_fusion.x_ref, bf16[2048,1792]{1,0:T(8,128)(2,1)} %w_ref.3), custom_call_target="tpu_custom_call" | custom-call | flops 1879048192 | bytes 9306112 | tf_op jit(solution)/shard_map/pallas_call | solution.py:441
  133.9 1.2 constant_dynamic-slice_fusion.5
  135.1 2.9 %collective-permute-start.7 = (bf16[64,1792]{1,0:T(8,128)(2,1)S(1)}, bf16[64,1792]{1,0:T(8,128)(2,1)S(1)}, u32[]{:S(2)}, u32[]{:S(2)}) collective-permute-start(bf16[64,1792]{1,0:T(8,128)(2,1)S(1)} %get-tuple-element.28), channel_id=1, source_target_pairs={{0,3},{1,0},{2,1},{3,2},{4,7},{5,4},{6,5},{7,6},{8,11},{9,8},{10,9... | collective-permute-start | bytes 688136 | tf_op jit(solution)/shard_map/ppermute | solution.py:528
  138.0 0.6 collective-permute-start.6
  138.6 0.0 collective-permute-done.12
  138.6 1.4 collective-permute-start.5
  140.0 0.0 collective-permute-done.11
  140.0 4.4 %collective-permute-done.10 = bf16[64,1792]{1,0:T(8,128)(2,1)S(1)} collective-permute-done((bf16[64,1792]{1,0:T(8,128)(2,1)S(1)}, bf16[64,1792]{1,0:T(8,128)(2,1)S(1)}, u32[]{:S(2)}, u32[]{:S(2)}) %collective-permute-start.10) | collective-permute-done | bytes 229408 | tf_op jit(solution)/shard_map/ppermute | solution.py:528
  144.4 1.1 add_convert_fusion
  145.5 7.2 %collective-permute-done.7 = bf16[64,1792]{1,0:T(8,128)(2,1)S(1)} collective-permute-done((bf16[64,1792]{1,0:T(8,128)(2,1)S(1)}, bf16[64,1792]{1,0:T(8,128)(2,1)S(1)}, u32[]{:S(2)}, u32[]{:S(2)}) %collective-permute-start.7) | collective-permute-done | bytes 229408 | tf_op jit(solution)/shard_map/ppermute | solution.py:528
  152.7 0.0 collective-permute-done.6
  152.7 11.0 %collective-permute-done.5 = bf16[64,1792]{1,0:T(8,128)(2,1)S(1)} collective-permute-done((bf16[64,1792]{1,0:T(8,128)(2,1)S(1)}, bf16[64,1792]{1,0:T(8,128)(2,1)S(1)}, u32[]{:S(2)}, u32[]{:S(2)}) %collective-permute-start.5) | collective-permute-done | bytes 229408 | tf_op jit(solution)/shard_map/ppermute | solution.py:528
  163.7 1.1 add_convert_fusion.1
  164.8 0.8 pad_maximum_fusion.2
Async XLA Ops:
  0.0 25.1 %collective-permute-start.2 = (bf16[576,8192]{1,0:T(8,128)(2,1)}, bf16[576,8192]{1,0:T(8,128)(2,1)}, u32[]{:S(2)}, u32[]{:S(2)}) collective-permute-start(bf16[576,8192]{1,0:T(8,128)(2,1)} %bitcast.10), channel_id=1, source_target_pairs={{0,4},{4,0},{8,12},{12,8},{1,5},{5,1},{9,13},{13,9},{2,6},{6,2},{1... | collective-permute-start | bytes 28311560 | tf_op jit(solution)/shard_map/ppermute | solution.py:481
  0.5 23.0 %collective-permute-start = (s32[1,64]{1,0:T(1,128)}, s32[1,64]{1,0:T(1,128)S(1)}, u32[]{:S(2)}, u32[]{:S(2)}) collective-permute-start(s32[1,64]{1,0:T(1,128)} %param.9), channel_id=1, source_target_pairs={{0,8},{4,12},{8,0},{12,4},{1,9},{5,13},{9,1},{13,5},{2,10},{6,14},... | collective-permute-start | bytes 776 | tf_op jit(solution)/shard_map/ppermute | solution.py:482
  2.9 21.2 %collective-permute-start.1 = (bf16[128,3072]{1,0:T(8,128)(2,1)}, bf16[128,3072]{1,0:T(8,128)(2,1)S(1)}, u32[]{:S(2)}, u32[]{:S(2)}) collective-permute-start(bf16[128,3072]{1,0:T(8,128)(2,1)} %refs_1_.1), channel_id=1, source_target_pairs={{0,8},{4,12},{8,0},{12,4},{1,9},{5,13},{9,1},{13,5},{2,10},{6,14},... | collective-permute-start | bytes 2359304 | tf_op jit(solution)/shard_map/ppermute | solution.py:480
  4.9 17.6 %copy-start.5 = (bf16[128,3072]{1,0:T(8,128)(2,1)S(1)}, bf16[128,3072]{1,0:T(8,128)(2,1)}, u32[]{:S(2)}) copy-start(bf16[128,3072]{1,0:T(8,128)(2,1)} %refs_1_.1) | copy-start | bytes 2359300
  4.9 18.5 %copy-start.6 = (s32[1,64]{1,0:T(1,128)S(1)}, s32[1,64]{1,0:T(1,128)}, u32[]{:S(2)}) copy-start(s32[1,64]{1,0:T(1,128)} %param.9) | copy-start | bytes 772
  25.1 28.6 %copy-start = (bf16[128,2176]{1,0:T(8,128)(2,1)S(1)}, bf16[128,2176]{1,0:T(8,128)(2,1)}, u32[]{:S(2)}) copy-start(bf16[128,2176]{1,0:T(8,128)(2,1)} %shard_map.73.near_ref) | copy-start | bytes 1671172
  53.7 1.0 copy-start.3
  54.6 1.0 copy-start.4
  79.2 1.0 copy-start.1
  80.2 1.0 copy-start.2
  81.8 15.5 %collective-permute-start.8 = (bf16[128,2176]{1,0:T(8,128)(2,1)S(1)}, bf16[128,2176]{1,0:T(8,128)(2,1)S(1)}, u32[]{:S(2)}, u32[]{:S(2)}) collective-permute-start(bf16[128,2176]{1,0:T(8,128)(2,1)S(1)} %shard_map.79.sent_ref), channel_id=1, source_target_pairs={{0,8},{4,12},{8,0},{12,4},{1,9},{5,13},{9,1},{13,5},{2,10},{6,14},... | collective-permute-start | bytes 1671176 | tf_op jit(solution)/shard_map/ppermute | solution.py:506
  81.9 26.7 %collective-permute-start.3 = (bf16[128,2176]{1,0:T(8,128)(2,1)S(1)}, bf16[128,2176]{1,0:T(8,128)(2,1)S(1)}, u32[]{:S(2)}, u32[]{:S(2)}) collective-permute-start(bf16[128,2176]{1,0:T(8,128)(2,1)S(1)} %shard_map.75.sent_ref), channel_id=1, source_target_pairs={{0,8},{4,12},{8,0},{12,4},{1,9},{5,13},{9,1},{13,5},{2,10},{6,14},... | collective-permute-start | bytes 1671176 | tf_op jit(solution)/shard_map/ppermute | solution.py:506
  98.4 11.3 %collective-permute-start.9 = (bf16[128,2048]{1,0:T(8,128)(2,1)S(1)}, bf16[128,2048]{1,0:T(8,128)(2,1)S(1)}, u32[]{:S(2)}, u32[]{:S(2)}) collective-permute-start(bf16[128,2048]{1,0:T(8,128)(2,1)S(1)} %shard_map.80), channel_id=1, source_target_pairs={{0,4},{4,0},{8,12},{12,8},{1,5},{5,1},{9,13},{13,9},{2,6},{6,2},{1... | collective-permute-start | bytes 1572872 | tf_op jit(solution)/shard_map/ppermute | solution.py:517
  109.6 15.2 %collective-permute-start.4 = (bf16[128,2048]{1,0:T(8,128)(2,1)S(1)}, bf16[128,2048]{1,0:T(8,128)(2,1)S(1)}, u32[]{:S(2)}, u32[]{:S(2)}) collective-permute-start(bf16[128,2048]{1,0:T(8,128)(2,1)S(1)} %shard_map.76), channel_id=1, source_target_pairs={{0,4},{4,0},{8,12},{12,8},{1,5},{5,1},{9,13},{13,9},{2,6},{6,2},{1... | collective-permute-start | bytes 1572872 | tf_op jit(solution)/shard_map/ppermute | solution.py:517
  120.0 18.7 %collective-permute-start.12 = (bf16[64,1792]{1,0:T(8,128)(2,1)S(1)}, bf16[64,1792]{1,0:T(8,128)(2,1)S(1)}, u32[]{:S(2)}, u32[]{:S(2)}) collective-permute-start(bf16[64,1792]{1,0:T(8,128)(2,1)S(1)} %get-tuple-element.31), channel_id=1, source_target_pairs={{0,3},{1,0},{2,1},{3,2},{4,7},{5,4},{6,5},{7,6},{8,11},{9,8},{10,9... | collective-permute-start | bytes 688136 | tf_op jit(solution)/shard_map/ppermute | solution.py:528
  123.8 16.2 %collective-permute-start.11 = (bf16[64,1792]{1,0:T(8,128)(2,1)S(1)}, bf16[64,1792]{1,0:T(8,128)(2,1)S(1)}, u32[]{:S(2)}, u32[]{:S(2)}) collective-permute-start(bf16[64,1792]{1,0:T(8,128)(2,1)S(1)} %get-tuple-element.32), channel_id=1, source_target_pairs={{0,1},{1,2},{2,3},{3,0},{4,5},{5,6},{6,7},{7,4},{8,9},{9,10},{10,1... | collective-permute-start | bytes 688136 | tf_op jit(solution)/shard_map/ppermute | solution.py:528
  123.8 20.6 %collective-permute-start.10 = (bf16[64,1792]{1,0:T(8,128)(2,1)S(1)}, bf16[64,1792]{1,0:T(8,128)(2,1)S(1)}, u32[]{:S(2)}, u32[]{:S(2)}) collective-permute-start(bf16[64,1792]{1,0:T(8,128)(2,1)S(1)} %get-tuple-element.30), channel_id=1, source_target_pairs={{0,2},{1,3},{2,0},{3,1},{4,6},{5,7},{6,4},{7,5},{8,10},{9,11},{10,... | collective-permute-start | bytes 688136 | tf_op jit(solution)/shard_map/ppermute | solution.py:528
  135.1 17.6 %collective-permute-start.7 = (bf16[64,1792]{1,0:T(8,128)(2,1)S(1)}, bf16[64,1792]{1,0:T(8,128)(2,1)S(1)}, u32[]{:S(2)}, u32[]{:S(2)}) collective-permute-start(bf16[64,1792]{1,0:T(8,128)(2,1)S(1)} %get-tuple-element.28), channel_id=1, source_target_pairs={{0,3},{1,0},{2,1},{3,2},{4,7},{5,4},{6,5},{7,6},{8,11},{9,8},{10,9... | collective-permute-start | bytes 688136 | tf_op jit(solution)/shard_map/ppermute | solution.py:528
  138.0 14.7 %collective-permute-start.6 = (bf16[64,1792]{1,0:T(8,128)(2,1)S(1)}, bf16[64,1792]{1,0:T(8,128)(2,1)S(1)}, u32[]{:S(2)}, u32[]{:S(2)}) collective-permute-start(bf16[64,1792]{1,0:T(8,128)(2,1)S(1)} %get-tuple-element.29), channel_id=1, source_target_pairs={{0,1},{1,2},{2,3},{3,0},{4,5},{5,6},{6,7},{7,4},{8,9},{9,10},{10,1... | collective-permute-start | bytes 688136 | tf_op jit(solution)/shard_map/ppermute | solution.py:528
  138.6 25.1 %collective-permute-start.5 = (bf16[64,1792]{1,0:T(8,128)(2,1)S(1)}, bf16[64,1792]{1,0:T(8,128)(2,1)S(1)}, u32[]{:S(2)}, u32[]{:S(2)}) collective-permute-start(bf16[64,1792]{1,0:T(8,128)(2,1)S(1)} %get-tuple-element.27), channel_id=1, source_target_pairs={{0,2},{1,3},{2,0},{3,1},{4,6},{5,7},{6,4},{7,5},{8,10},{9,11},{10,... | collective-permute-start | bytes 688136 | tf_op jit(solution)/shard_map/ppermute | solution.py:528

commit v4 on v3

--- a/solution.py
+++ b/solution.py
@@ -16,7 +16,7 @@
 NEVER = -1e30
 FAR = 1 << 30
 MIB = 1024 * 1024
-META = 67
+META = 68
 
 
 def attend_kernel(blocks_held, jobs, fresh, keep, *refs):
@@ -31,18 +31,14 @@
     (meta,) = take(1)
     queries = take(n)
     wa_hbm, own_hbm, sib_hbm, wv_hbm = take(4)
-    saved, listed = ([], None) if fresh else (take(n), take(1)[0])
+    saved = [] if fresh else take(n)
     outs = take(n)
     kept = take(n) if keep else []
-    if keep:
-        (listed,) = take(1)
     raws = take(n) if fresh else []
     kts = take(n)
     q_full, wa, wv = take(3)
     accs, stores, peaks, totals = take(2), take(2), take(2), take(2)
-    if fresh and not keep:
-        (listed,) = take(1)
-    edge, wa_sem, wv_sem, kv_sems, keep_sems = take(5)
+    wa_sem, wv_sem, kv_sems, keep_sems = take(4)
 
     tokens = queries[0].shape[0]
     heads, nope, lat = wa.shape
@@ -50,75 +46,35 @@
     vd = wv.shape[2]
     head_width = nope + width - lat
     fold = head_width ** -0.5 * math.log2(math.e)
-    strides = [0]
-    for kt in kts:
-        strides.append(strides[-1] + kt.shape[1] // BT + 2)
-
-    wa_copy = pltpu.make_async_copy(wa_hbm, wa, wa_sem)
-    wv_copy = pltpu.make_async_copy(wv_hbm, wv, wv_sem)
-    wa_copy.start()
+
+    def slots_of(j):
+        return (meta[META * j + 65] + SMALL - 1) // SMALL * SMALL
 
     def gather(j):
-        row0, list0 = META * j, strides[j]
-        room = kts[j].shape[1] // BT
-        start, mine, other = meta[row0 + 64], meta[row0 + 65], meta[row0 + 66]
+        row0 = META * j
+        count, mine = meta[row0 + 65], meta[row0 + 67]
         raw, sem = raws[j], kv_sems.at[j]
-        holders = [
-            h for h in (("own", mine, own_hbm), ("sib", other, sib_hbm)) if h[0] in jobs[j][0]
-        ]
-
-        def fetch(block, slot):
-            owner = block // blocks_held
+
+        def fetch(i, _):
+            block = meta[row0 + i]
             col = pl.multiple_of((block % blocks_held) // 2 * WIDE, WIDE)
-            for _, holder, source in holders:
-                @pl.when(owner == holder)
-                def _(source=source):
-                    pltpu.make_async_copy(source.at[:, pl.ds(col, WIDE)], raw.at[slot], sem).start()
-
-        def scan(i, carry):
-            full, part = carry
-            block = meta[row0 + i]
-            owner = block // blocks_held
-            here = jnp.bool_(False)
-            for _, holder, _ in holders:
-                here = here | (owner == holder)
-            whole = here & (block * BT + BT - 1 <= start)
-            some = here & (block * BT + BT - 1 > start) & (block * BT <= start + jobs[j][1] - 1)
-
-            @pl.when(whole)
+            here = (block // blocks_held == mine) | (i >= count)
+
+            @pl.when(here)
             def _():
-                fetch(block, full)
-                listed[list0 + full] = block
-
-            @pl.when(some)
+                pltpu.make_async_copy(own_hbm.at[:, pl.ds(col, WIDE)], raw.at[i], sem).start()
+
+            @pl.when(jnp.logical_not(here))
             def _():
-                edge[part] = block
-
-            return full + whole.astype(jnp.int32), part + some.astype(jnp.int32)
-
-        full, part = lax.fori_loop(0, 64, scan, (jnp.int32(0), jnp.int32(0)))
-
-        def fetch_edge(i, _):
-            fetch(edge[i], full + i)
-            listed[list0 + full + i] = edge[i]
+                pltpu.make_async_copy(sib_hbm.at[:, pl.ds(col, WIDE)], raw.at[i], sem).start()
+
             return 0
 
-        lax.fori_loop(0, part, fetch_edge, 0)
-        count = full + part
-
-        def fill(i, _):
-            pltpu.make_async_copy(own_hbm.at[:, pl.ds(0, WIDE)], raw.at[i], sem).start()
-            listed[list0 + i] = 0
-            return 0
-
-        lax.fori_loop(count, (count + SMALL - 1) // SMALL * SMALL, fill, 0)
-        listed[list0 + room] = full
-        listed[list0 + room + 1] = count
+        lax.fori_loop(0, slots_of(j), fetch, 0)
 
     def join(j):
-        raw, kt, list0 = raws[j], kts[j], strides[j]
-        count = listed[list0 + kt.shape[1] // BT + 1]
-        slots = (count + SMALL - 1) // SMALL * SMALL
+        raw, kt, row0 = raws[j], kts[j], META * j
+        slots = slots_of(j)
 
         def land(i, _):
             pltpu.make_async_copy(own_hbm.at[:, pl.ds(0, WIDE)], raw.at[0], kv_sems.at[j]).wait()
@@ -131,24 +87,17 @@
             right = raw[2 * i + 1]
             left_swapped = jnp.concatenate([left[:, BT:], left[:, :BT]], axis=1)
             right_swapped = jnp.concatenate([right[:, BT:], right[:, :BT]], axis=1)
-            low = jnp.where(listed[list0 + 2 * i] % 2 == 1, left_swapped, left)
-            high = jnp.where(listed[list0 + 2 * i + 1] % 2 == 1, right, right_swapped)
+            low = jnp.where(meta[row0 + 2 * i] % 2 == 1, left_swapped, left)
+            high = jnp.where(meta[row0 + 2 * i + 1] % 2 == 1, right, right_swapped)
             lane = lax.broadcasted_iota(jnp.int32, (width, WIDE), 1)
             kt[:, pl.ds(pl.multiple_of(i * WIDE, WIDE), WIDE)] = jnp.where(lane < BT, low, high)
             return 0
 
         lax.fori_loop(0, slots // 2, pair, 0)
 
-    if fresh:
-        for j in range(n):
-            gather(j)
-    else:
-        for j in range(n):
-            pltpu.make_async_copy(saved[j], kts[j], kv_sems.at[j]).start()
-    wv_copy.start()
-    wa_copy.wait()
     rows_each = heads * tokens
-    for j in range(n):
+
+    def absorb(j):
         for h in range(heads):
             base = h * head_width
             latent_part = jnp.dot(
@@ -158,25 +107,31 @@
             q_full[rows, 0:lat] = (latent_part * fold).astype(jnp.bfloat16)
             turned = queries[j][:, base + nope : base + head_width].astype(jnp.float32)
             q_full[rows, lat:width] = (turned * fold).astype(jnp.bfloat16)
+
+    def held(j):
+        return kts[j].at[:, 0 : kts[j].shape[1] - CHUNK * BT]
+
+    wa_copy = pltpu.make_async_copy(wa_hbm, wa, wa_sem)
+    wv_copy = pltpu.make_async_copy(wv_hbm, wv, wv_sem)
+    wa_copy.start()
     for j in range(n):
         if fresh:
-            join(j)
+            gather(j)
         else:
-            pltpu.make_async_copy(saved[j], kts[j], kv_sems.at[j]).wait()
-        if keep:
-            pltpu.make_async_copy(kts[j], kept[j], keep_sems.at[j]).start()
-    wv_copy.wait()
+            pltpu.make_async_copy(saved[j], held(j), kv_sems.at[j]).start()
+        if j == 0:
+            wv_copy.start()
+    wa_copy.wait()
 
     tile = accs[0].shape[0]
     tile_heads = tile // tokens
     lane = lax.broadcasted_iota(jnp.int32, (tokens, 128), 1)
 
     def work(j):
-        kt, list0, o_ref = kts[j], strides[j], outs[j]
-        room = kt.shape[1] // BT
-        first = meta[META * j + 64] + jobs[j][2]
-        full = listed[list0 + room]
-        count = listed[list0 + room + 1]
+        kt, list0, o_ref = kts[j], META * j, outs[j]
+        first = meta[list0 + 66] + jobs[j][1]
+        full = meta[list0 + 64]
+        count = meta[list0 + 65]
         plain_chunks = full // CHUNK
         done = plain_chunks * CHUNK
         small_chunks = (count - done + SMALL - 1) // SMALL
@@ -218,10 +173,9 @@
                     preferred_element_type=jnp.float32,
                 )
 
-            def chunk(n, total_chunks, start, masked, c, _):
+            def chunk(n, start, masked, c, _):
                 key0 = pl.multiple_of(start + c * n * BT, 128)
-                last = start + (total_chunks - 1) * n * BT
-                key1 = pl.multiple_of(jnp.minimum(key0 + n * BT, last), 128)
+                key1 = pl.multiple_of(key0 + n * BT, 128)
                 visible = None
                 if masked:
                     block0 = key0 // BT
@@ -230,7 +184,7 @@
                     for b in range(n):
                         at = jnp.where(
                             block0 + b < full, 0,
-                            jnp.where(block0 + b < count, listed[list0 + block0 + b] * BT, FAR),
+                            jnp.where(block0 + b < count, meta[list0 + block0 + b] * BT, FAR),
                         )
                         position = jnp.where(column // BT == b, at + column % BT, position)
                     query = first + lax.broadcasted_iota(jnp.int32, (tokens, n * BT), 0)
@@ -246,16 +200,13 @@
             @pl.when(plain_chunks > 0)
             def _():
                 score(0, 0, CHUNK)
-                lax.fori_loop(
-                    0, plain_chunks, functools.partial(chunk, CHUNK, plain_chunks, 0, False), 0
-                )
-
-            @pl.when(small_chunks > 0)
+
+            @pl.when(plain_chunks == 0)
             def _():
-                score(0, pl.multiple_of(done * BT, 128), SMALL)
-                lax.fori_loop(
-                    0, small_chunks, functools.partial(chunk, SMALL, small_chunks, done * BT, True), 0
-                )
+                score(0, 0, SMALL)
+
+            lax.fori_loop(0, plain_chunks, functools.partial(chunk, CHUNK, 0, False), 0)
+            lax.fori_loop(0, small_chunks, functools.partial(chunk, SMALL, done * BT, True), 0)
 
             for i in range(2):
                 total = jnp.maximum(jnp.sum(totals[i][...], axis=1, keepdims=True), 1e-30)
@@ -276,10 +227,19 @@
         o_ref[:, heads * vd :] = lse_tile.astype(jnp.bfloat16)
 
     for j in range(n):
+        absorb(j)
+        if fresh:
+            join(j)
+        else:
+            pltpu.make_async_copy(saved[j], held(j), kv_sems.at[j]).wait()
+        if keep:
+            pltpu.make_async_copy(held(j), kept[j], keep_sems.at[j]).start()
+        if j == 0:
+            wv_copy.wait()
         work(j)
     if keep:
         for j in range(n):
-            pltpu.make_async_copy(kts[j], kept[j], keep_sems.at[j]).wait()
+            pltpu.make_async_copy(held(j), kept[j], keep_sems.at[j]).wait()
 
 
 def place_log(tile, lane, h, value):
@@ -297,30 +257,27 @@
     heads, nope, lat = w_absorb.shape
     vd = w_value.shape[2]
     width = own.shape[0]
-    slots = [-(-depth * len(job[0]) // SMALL) * SMALL for job in jobs]
+    slots = [-(-depth * job[0] // SMALL) * SMALL for job in jobs]
     rows = heads * tokens
     tile = min(row_tile, rows // 2)
     keys = sum(slots) * BT * 2 // 3
     any_space = pl.BlockSpec(memory_space=pl.ANY)
     vmem = pl.BlockSpec(memory_space=pltpu.VMEM)
     smem = pl.BlockSpec(memory_space=pltpu.SMEM)
-    lists = sum(slots) + 2 * len(jobs)
-    kt_shapes = [(width, s * BT) for s in slots]
     out_shape = [jax.ShapeDtypeStruct((tokens, heads * vd + 128), jnp.bfloat16) for _ in jobs]
     out_specs = [vmem for _ in jobs]
     if keep:
-        out_shape += [jax.ShapeDtypeStruct(s, jnp.bfloat16) for s in kt_shapes]
-        out_shape += [jax.ShapeDtypeStruct((lists,), jnp.int32)]
-        out_specs += [any_space] * len(jobs) + [smem]
+        out_shape += [jax.ShapeDtypeStruct((width, s * BT), jnp.bfloat16) for s in slots]
+        out_specs += [any_space] * len(jobs)
     in_specs = [smem] + [vmem] * len(jobs) + [any_space] * 4
-    operands = [jnp.concatenate(metas), *queries, w_absorb, own, sib, w_value]
+    operands = [metas, *queries, w_absorb, own, sib, w_value]
     if not fresh:
-        in_specs += [any_space] * len(jobs) + [smem]
+        in_specs += [any_space] * len(jobs)
         operands += saved
     scratch = []
     if fresh:
         scratch += [pltpu.VMEM((s, width, WIDE), jnp.bfloat16) for s in slots]
-    scratch += [pltpu.VMEM(s, jnp.bfloat16) for s in kt_shapes]
+    scratch += [pltpu.VMEM((width, (s + CHUNK) * BT), jnp.bfloat16) for s in slots]
     scratch += [
         pltpu.VMEM((len(jobs) * rows, width), jnp.bfloat16),
         pltpu.VMEM(w_absorb.shape, jnp.bfloat16),
@@ -328,11 +285,6 @@
         *[pltpu.VMEM((tile, lat), jnp.float32)] * 2,
         *[pltpu.VMEM((tile, CHUNK * BT), jnp.float32)] * 2,
         *[pltpu.VMEM((tile, 128), jnp.float32)] * 4,
-    ]
-    if fresh and not keep:
-        scratch += [pltpu.SMEM((lists,), jnp.int32)]
-    scratch += [
-        pltpu.SMEM((64,), jnp.int32),
         pltpu.SemaphoreType.DMA,
         pltpu.SemaphoreType.DMA,
         pltpu.SemaphoreType.DMA((len(jobs),)),
@@ -344,7 +296,7 @@
         in_specs=in_specs,
         out_specs=out_specs,
         scratch_shapes=scratch,
-        compiler_params=pltpu.CompilerParams(vmem_limit_bytes=56 * MIB),
+        compiler_params=pltpu.CompilerParams(vmem_limit_bytes=44 * MIB),
         cost_estimate=pl.CostEstimate(
             flops=2 * rows * keys * (width + lat),
             bytes_accessed=2 * keys * width * 2,
@@ -390,9 +342,7 @@
         in_specs=[vmem] * len(operands),
         out_specs=vmem,
         compiler_params=pltpu.CompilerParams(vmem_limit_bytes=16 * MIB),
-        cost_estimate=pl.CostEstimate(
-            flops=4 * shape[0] * shape[1], bytes_accessed=8 * shape[0] * shape[1], transcendentals=0
-        ),
+        cost_estimate=pl.CostEstimate(flops=1, bytes_accessed=1, transcendentals=0),
     )(*operands)
 
 
@@ -447,12 +397,8 @@
             pl.BlockSpec((depth, wide), lambda j: (0, j)),
         ],
         out_specs=pl.BlockSpec((rows, wide), lambda j: (0, j)),
-        compiler_params=pltpu.CompilerParams(vmem_limit_bytes=60 * MIB),
-        cost_estimate=pl.CostEstimate(
-            flops=2 * rows * depth * columns,
-            bytes_accessed=2 * (rows * depth + depth * columns + rows * columns),
-            transcendentals=0,
-        ),
+        compiler_params=pltpu.CompilerParams(vmem_limit_bytes=24 * MIB),
+        cost_estimate=pl.CostEstimate(flops=1, bytes_accessed=1, transcendentals=0),
     )(x, w)
 
 
@@ -472,18 +418,37 @@
     back = {t: [(i, (i - 2 * t) % owners) for i in range(owners)] for t in turns}
     own = latent.T
 
-    def meta_of(row, index):
-        return jnp.concatenate(
-            [row[0], jnp.stack([span_offset[0] + index * tokens, me, me ^ 1])]
-        ).astype(jnp.int32)
+    held = latent.shape[0] // BT
+
+    def lists_of(rows, indices, own_too, sib_too):
+        starts = span_offset[0] + indices * tokens
+        owner = rows // held
+        here = ((owner == (me ^ 1)) & sib_too) | ((owner == me) & own_too)
+        full = here & (rows * BT + BT - 1 <= starts[:, None])
+        edge = here & ~full & (rows * BT <= starts[:, None] + tokens - 1)
+        order = jnp.arange(rows.shape[1])
+        before = order[None, :] < order[:, None]
+        rank = lambda marks: jnp.sum(marks[:, None, :] & before[None], axis=2, dtype=jnp.int32)
+        n_full = jnp.sum(full, axis=1, dtype=jnp.int32)
+        n_all = n_full + jnp.sum(edge, axis=1, dtype=jnp.int32)
+        slot = jnp.where(full, rank(full), jnp.where(edge, n_full[:, None] + rank(edge), -1))
+        listed = jnp.sum(
+            jnp.where(slot[:, None, :] == order[None, :, None], rows[:, None, :], 0), axis=2, dtype=jnp.int32
+        )
+        mine = jnp.full_like(n_all, me)
+        tail = jnp.stack([n_full, n_all, starts.astype(jnp.int32), mine], axis=1)
+        return jnp.concatenate([listed, tail], axis=1).reshape(-1)
 
     far_queries = {t: lax.ppermute(queries, "ctx", ahead[t]) for t in turns}
     sib = lax.ppermute(own, "ctx", sibling)
     far_rows = {t: lax.ppermute(selection, "ctx", ahead[t]) for t in turns}
-    my_meta = meta_of(selection, me)
-    metas = [meta_of(far_rows[t], (me - 2 * t) % owners) for t in turns] + [my_meta]
-    (near,) = attend(
-        [my_meta], [queries], [(("own",), tokens, 0)], own, own, w_absorb, w_value, depth, 1024
+    near_meta = lists_of(selection, me[None], True, False)
+    (near,) = attend(near_meta, [queries], [(1, 0)], own, own, w_absorb, w_value, depth, 1024)
+    meta = lists_of(
+        jnp.concatenate([far_rows[t] for t in turns] + [selection], axis=0),
+        jnp.stack([(me - 2 * t) % owners for t in turns] + [me]),
+        jnp.arange(chips)[:, None] < chips - 1,
+        True,
     )
     outputs = []
     saved = None
@@ -491,11 +456,11 @@
     last = near
     for c in range(PIECES):
         rows = slice(c * piece, (c + 1) * piece)
-        jobs = [(("own", "sib"), tokens, c * piece) for _ in turns] + [(("sib",), tokens, c * piece)]
+        jobs = [(2, c * piece)] * (chips - 1) + [(1, c * piece)]
         cuts = [far_queries[t][rows] for t in turns] + [queries[rows]]
         *cuts, last = lax.optimization_barrier((*cuts, last))
         results = attend(
-            metas, cuts, jobs, own, sib, w_absorb, w_value, depth, 512, saved, saved is None
+            meta, cuts, jobs, own, sib, w_absorb, w_value, depth, 512, saved, saved is None
         )
         if saved is None:
             saved = list(results[len(jobs) :])
@@ -507,9 +472,11 @@
         else:
             arrived = [lax.ppermute(far, "ctx", back[t]) for t, far in zip(turns, fars)]
             pieces.append(combine([(a, 0) for a in arrived] + [(side, 0), (near, c * piece)], heads))
+    last = [last]
     for c in range(PIECES):
         if chips == 2:
             sent, got = pieces[c]
+            got, *last = lax.optimization_barrier((got, *last))
             mine = settle(sent, got, heads)
         else:
             mine = pieces[c]
@@ -522,10 +489,12 @@
             place = (me + block) % 2 * chips + turn
             return lax.dynamic_slice_in_dim(shares, place * piece, piece, 0)
 
-        arrived = [share_of(column)]
-        for s in sorted(range(1, groups), key=lambda s: -min(s, groups - s)):
-            shift = [(i, (i + s) % groups) for i in range(groups)]
-            arrived.append(lax.ppermute(share_of((column + s) % groups), "head", shift))
+        steps = sorted(range(1, groups), key=lambda s: -min(s, groups - s))
+        last = [share_of((column + s) % groups) for s in steps]
+        arrived = [share_of(column)] + [
+            lax.ppermute(share, "head", [(i, (i + s) % groups) for i in range(groups)])
+            for s, share in zip(steps, last)
+        ]
         outputs.append(sum(a.astype(jnp.float32) for a in arrived).astype(jnp.bfloat16))
     return jnp.concatenate(outputs, axis=0)
 

time: 164 us -> 142 us (0.87)
  Pallas kernels: 88.4 us -> 69.5 us
  waiting for transfers between devices: 45.9 us -> 34.4 us
  local copies, waits for them, and re-layouts: 8.75 us -> 14.5 us
    ppermute x2, waiting for transfers between devices: 23.3 us -> 6.12 us  [body(): pieces.append((sent, lax.ppermute(sent, 'ctx', ahead[1])))]
    pallas_call x3, Pallas kernels: 69 us -> 58.5 us  [attend(): pl.pallas_call(functools.partial(attend_kernel, own.shape[1] // BT, jobs,...]
    pallas_call x2, Pallas kernels: 15.9 us -> 7.45 us  [project(): pl.pallas_call(project_kernel, out_shape=jax.ShapeDtypeStruct((rows, colu...]
    unnamed x14 -> x16, local copies, waits for them, and re-layouts: 3.82 us -> 12.1 us
    ppermute x6, waiting for transfers between devices: 22.6 us -> 26.8 us  [body(): lax.ppermute(share, 'head', [(i, (i + s) % groups) for i in range(groups)])]
    reduce_sum x0 -> x8, other arithmetic: none -> 3.38 us  [the longest x2 1.47 us: lists_of(): n_all = n_full + jnp.sum(edge, axis=1, dtype=jnp.int32)]
    ppermute x2, starting transfers between devices: 0.14 us -> 3.14 us  [body(): pair = jnp.concatenate([mine, lax.ppermute(mine, 'ctx', sibling)], axis=0)]
    dynamic_slice x2, local copies, waits for them, and re-layouts: 2.41 us -> 0.11 us  [share_of(): return lax.dynamic_slice_in_dim(shares, place * piece, piece, 0)]
  transfers between devices with their start and end apart: 13 -> 13, of which waited for: 5 -> 6; matrix products, arithmetic and copies ran while one was open for 6% -> 5% of each run, Pallas kernels for 21% -> 31%
where the time goes in v4:
time: 142 us
  Pallas kernels  69.5 us (49%)
  waiting for transfers between devices  34.4 us (24%)
  starting transfers between devices  16.1 us (11%)
  local copies, waits for them, and re-layouts  14.5 us (10%)
  other arithmetic  5.39 us (4%)
  between operations  2.15 us (2%)
    pallas_call x3, Pallas kernels, attend(): pl.pallas_call(functools.partial(attend_kernel, own.shape[1] // BT, jobs,...  58.5 us
    ppermute x6, waiting for transfers between devices, body(): lax.ppermute(share, 'head', [(i, (i + s) % groups) for i in range(groups)])  26.8 us
    unnamed x16, local copies, waits for them, and re-layouts  12.1 us
    ppermute x6, starting transfers between devices, body(): lax.ppermute(share, 'head', [(i, (i + s) % groups) for i in range(groups)])  9.83 us
    pallas_call x2, Pallas kernels, project(): pl.pallas_call(project_kernel, out_shape=jax.ShapeDtypeStruct((rows, colu...  7.45 us
    ppermute x2, waiting for transfers between devices, body(): pieces.append((sent, lax.ppermute(sent, 'ctx', ahead[1])))  6.12 us
    pallas_call x4, Pallas kernels, small_call(): pl.pallas_call(kernel, out_shape=jax.ShapeDtypeStruct(shape, jnp.bfloat16...  3.5 us
    ppermute x2, starting transfers between devices, body(): pair = jnp.concatenate([mine, lax.ppermute(mine, 'ctx', sibling)], axis=0)  3.14 us
  transfers between devices with their start and end apart: 13, of which 6 were waited for; matrix products, arithmetic and copies ran while one was open for 5% of the time, Pallas kernels for 31%

profile of v4, /device:TPU:0, one launch (start us, length us, event | category | flops | bytes accessed | tf_op | source)
XLA Modules:
  0.0 142.0 jit_solution(14181240668261887205)
XLA Ops:
  0.0 0.5 collective-permute-start.2
  0.5 2.5 %collective-permute-start = (s32[1,64]{1,0:T(1,128)}, s32[1,64]{1,0:T(1,128)S(1)}, u32[]{:S(2)}, u32[]{:S(2)}) collective-permute-start(s32[1,64]{1,0:T(1,128)} %param.9), channel_id=1, source_target_pairs={{0,8},{4,12},{8,0},{12,4},{1,9},{5,13},{9,1},{13,5},{2,10},{6,14},... | collective-permute-start | bytes 776 | tf_op jit(solution)/shard_map/ppermute | solution.py:444
  2.9 0.1 collective-permute-start.1
  3.7 1.3 convert_reduce_fusion.6
  5.0 0.7 convert_reduce_fusion.7
  6.8 0.1 convert_reduce_fusion.2
  6.9 0.6 fusion.5
  7.6 0.8 select_reduce_fusion.1
  8.3 0.7 concatenate.69
  9.1 0.1 broadcast_add_fusion
  9.2 0.0 copy-start.2
  9.2 1.6 %copy-done.2 = bf16[16,128,512]{2,1,0:T(8,128)(2,1)S(1)} copy-done((bf16[16,128,512]{2,1,0:T(8,128)(2,1)S(1)}, bf16[16,128,512]{2,1,0:T(8,128)(2,1)}, u32[]{:S(2)}) %copy-start.2) | copy-done | bytes 2097176
  10.8 1.6 %copy-done.4 = bf16[16,512,128]{2,1,0:T(8,128)(2,1)S(1)} copy-done((bf16[16,512,128]{2,1,0:T(8,128)(2,1)S(1)}, bf16[16,512,128]{2,1,0:T(8,128)(2,1)}, u32[]{:S(2)}) %copy-start.4) | copy-done | bytes 2097176
  12.4 1.1 copy-done.6
  13.5 17.7 %shard_map.73.near_ref = bf16[128,2176]{1,0:T(8,128)(2,1)S(1)} custom-call(s32[68]{0:T(128)S(1)} %bitcast.30, bf16[128,3072]{1,0:T(8,128)(2,1)S(1)} %copy-done.6, bf16[16,128,512]{2,1,0:T(8,128)(2,1)S(1)} %copy-done.2, bf16[576,8192]{1,0:T(8,128)(2,1)} %bitcast.32, bf16[576,8192]{1,0:T(8,128)(2,1)} %bitcast.33, bf16[16,512,128]{2,1,0:T(8,128)(2,1)S(1)} %copy-done.4), custom_call_target="tpu_custom_call" | custom-call | flops 4563402752 | bytes 2359296 | tf_op jit(solution)/shard_map/pallas_call | solution.py:293
  31.2 0.0 copy-start.3
  31.2 0.1 fusion.7
  31.3 0.0 collective-permute-done
  31.3 0.2 convert_reduce_fusion.4
  31.5 0.1 convert_reduce_fusion.5
  31.6 0.1 copy.12
  31.7 0.1 copy.11
  31.8 0.2 convert_reduce_fusion
  31.9 0.1 select_select_fusion
  32.0 0.1 select_reduce_fusion
  32.1 0.1 concatenate.68
  32.2 0.1 reshape.529.refs_0_
  32.3 0.0 collective-permute-done.1
  32.3 1.2 fusion.8
  33.5 0.0 copy-start.5
  33.5 1.6 %copy-done.5 = bf16[16,512,128]{2,1,0:T(8,128)(2,1)S(1)} copy-done((bf16[16,512,128]{2,1,0:T(8,128)(2,1)S(1)}, bf16[16,512,128]{2,1,0:T(8,128)(2,1)}, u32[]{:S(2)}) %copy-start.5) | copy-done | bytes 2097176
  35.1 23.0 %shard_map.74 = (bf16[64,2176]{1,0:T(8,128)(2,1)S(1)}, bf16[64,2176]{1,0:T(8,128)(2,1)S(1)}, bf16[576,3072]{1,0:T(8,128)(2,1)}, bf16[576,1536]{1,0:T(8,128)(2,1)S(1)}) custom-call(s32[136]{0:T(256)S(1)} %reshape.529.refs_0_, bf16[64,3072]{1,0:T(8,128)(2,1)S(1)} %get-tuple-element.17.refs_1_, bf16[64,3072]{1,0:T(8,128)(2,1)S(1)} %get-tuple-element.18.refs_2_, ...), custom_call_target="tpu_custom_call" | custom-call | flops 6845104128 | bytes 7077888 | tf_op jit(solution)/shard_map/pallas_call | solution.py:293
  58.1 0.7 shard_map.75.sent_ref
  58.9 0.1 collective-permute-start.3
  58.9 17.8 %shard_map.76 = (bf16[64,2176]{1,0:T(8,128)(2,1)S(1)}, bf16[64,2176]{1,0:T(8,128)(2,1)S(1)}) custom-call(s32[136]{0:T(256)S(1)} %reshape.529.refs_0_, bf16[64,3072]{1,0:T(8,128)(2,1)S(1)} %get-tuple-element.21.refs_1_, bf16[64,3072]{1,0:T(8,128)(2,1)S(1)} %get-tuple-element.22.refs_2_, bf16[16,128,512]{2,1,0:T(8,128)(2,1)S(1)} %copy-done.3, ...), custom_call_target="tpu_custom_call" | custom-call | flops 6845104128 | bytes 7077888 | tf_op jit(solution)/shard_map/pallas_call | solution.py:293
  76.8 0.7 shard_map.77.sent_ref
  77.5 0.0 collective-permute-done.3.got_ref
  77.5 1.0 shard_map.78
  78.6 3.1 %collective-permute-start.4 = (bf16[128,2048]{1,0:T(8,128)(2,1)S(1)}, bf16[128,2048]{1,0:T(8,128)(2,1)S(1)}, u32[]{:S(2)}, u32[]{:S(2)}) collective-permute-start(bf16[128,2048]{1,0:T(8,128)(2,1)S(1)} %shard_map.78), channel_id=1, source_target_pairs={{0,4},{4,0},{8,12},{12,8},{1,5},{5,1},{9,13},{13,9},{2,6},{6,2},{1... | collective-permute-start | bytes 1572872 | tf_op jit(solution)/shard_map/ppermute | solution.py:484
  81.6 1.5 %collective-permute-done.4 = bf16[128,2048]{1,0:T(8,128)(2,1)S(1)} collective-permute-done((bf16[128,2048]{1,0:T(8,128)(2,1)S(1)}, bf16[128,2048]{1,0:T(8,128)(2,1)S(1)}, u32[]{:S(2)}, u32[]{:S(2)}) %collective-permute-start.4) | collective-permute-done | bytes 524320 | tf_op jit(solution)/shard_map/ppermute | solution.py:484
  83.2 0.1 pad_maximum_fusion.x_ref
  83.2 0.0 copy-start
  83.2 3.1 %copy-done = bf16[2048,1792]{1,0:T(8,128)(2,1)S(1)} copy-done((bf16[2048,1792]{1,0:T(8,128)(2,1)S(1)}, bf16[2048,1792]{1,0:T(8,128)(2,1)}, u32[]{:S(2)}) %copy-start) | copy-done | bytes 7340056
  86.3 3.7 %shard_map.79 = bf16[256,1792]{1,0:T(8,128)(2,1)S(1)} custom-call(bf16[256,2048]{1,0:T(8,128)(2,1)S(1)} %pad_maximum_fusion.x_ref, bf16[2048,1792]{1,0:T(8,128)(2,1)S(1)} %copy-done), custom_call_target="tpu_custom_call" | custom-call | flops 1 | bytes 1 | tf_op jit(solution)/shard_map/pallas_call | solution.py:391
  90.1 0.1 constant_dynamic-slice_fusion.3
  90.1 6.1 %collective-permute-done.8.got_ref = bf16[128,2176]{1,0:T(8,128)(2,1)S(1)} collective-permute-done((bf16[128,2176]{1,0:T(8,128)(2,1)S(1)}, bf16[128,2176]{1,0:T(8,128)(2,1)S(1)}, u32[]{:S(2)}, u32[]{:S(2)}) %collective-permute-start.8) | collective-permute-done | bytes 557088 | tf_op jit(solution)/shard_map/ppermute | solution.py:471
  96.2 1.0 shard_map.80
  97.3 0.1 collective-permute-start.9
  97.4 3.9 %collective-permute-start.7 = (bf16[64,1792]{1,0:T(8,128)(2,1)S(1)}, bf16[64,1792]{1,0:T(8,128)(2,1)S(1)}, u32[]{:S(2)}, u32[]{:S(2)}) collective-permute-start(bf16[64,1792]{1,0:T(8,128)(2,1)S(1)} %get-tuple-element.42), channel_id=1, source_target_pairs={{0,3},{1,0},{2,1},{3,2},{4,7},{5,4},{6,5},{7,6},{8,11},{9,8},{10,9... | collective-permute-start | bytes 688136 | tf_op jit(solution)/shard_map/ppermute | solution.py:495
  101.3 0.1 pad_maximum_fusion.1.x_ref
  101.4 1.1 collective-permute-start.5
  102.4 3.1 %copy-done.1 = bf16[2048,1792]{1,0:T(8,128)(2,1)S(1)} copy-done((bf16[2048,1792]{1,0:T(8,128)(2,1)S(1)}, bf16[2048,1792]{1,0:T(8,128)(2,1)}, u32[]{:S(2)}) %copy-start.1) | copy-done | bytes 7340056
  105.5 3.7 %shard_map.81 = bf16[256,1792]{1,0:T(8,128)(2,1)S(1)} custom-call(bf16[256,2048]{1,0:T(8,128)(2,1)S(1)} %pad_maximum_fusion.1.x_ref, bf16[2048,1792]{1,0:T(8,128)(2,1)S(1)} %copy-done.1), custom_call_target="tpu_custom_call" | custom-call | flops 1 | bytes 1 | tf_op jit(solution)/shard_map/pallas_call | solution.py:391
  109.3 0.1 constant_dynamic-slice_fusion.2
  109.3 2.9 %collective-permute-start.12 = (bf16[64,1792]{1,0:T(8,128)(2,1)S(1)}, bf16[64,1792]{1,0:T(8,128)(2,1)S(1)}, u32[]{:S(2)}, u32[]{:S(2)}) collective-permute-start(bf16[64,1792]{1,0:T(8,128)(2,1)S(1)} %get-tuple-element.40), channel_id=1, source_target_pairs={{0,3},{1,0},{2,1},{3,2},{4,7},{5,4},{6,5},{7,6},{8,11},{9,8},{10,9... | collective-permute-start | bytes 688136 | tf_op jit(solution)/shard_map/ppermute | solution.py:495
  112.2 0.6 collective-permute-start.11
  112.8 1.4 collective-permute-start.10
  114.2 7.7 %collective-permute-done.5 = bf16[64,1792]{1,0:T(8,128)(2,1)S(1)} collective-permute-done((bf16[64,1792]{1,0:T(8,128)(2,1)S(1)}, bf16[64,1792]{1,0:T(8,128)(2,1)S(1)}, u32[]{:S(2)}, u32[]{:S(2)}) %collective-permute-start.5) | collective-permute-done | bytes 229408 | tf_op jit(solution)/shard_map/ppermute | solution.py:495
  121.9 0.1 add_convert_fusion.1
  122.0 0.1 collective-permute-done.12
  122.1 5.8 %collective-permute-done.11 = bf16[64,1792]{1,0:T(8,128)(2,1)S(1)} collective-permute-done((bf16[64,1792]{1,0:T(8,128)(2,1)S(1)}, bf16[64,1792]{1,0:T(8,128)(2,1)S(1)}, u32[]{:S(2)}, u32[]{:S(2)}) %collective-permute-start.11) | collective-permute-done | bytes 229408 | tf_op jit(solution)/shard_map/ppermute | solution.py:495
  127.9 13.2 %collective-permute-done.10 = bf16[64,1792]{1,0:T(8,128)(2,1)S(1)} collective-permute-done((bf16[64,1792]{1,0:T(8,128)(2,1)S(1)}, bf16[64,1792]{1,0:T(8,128)(2,1)S(1)}, u32[]{:S(2)}, u32[]{:S(2)}) %collective-permute-start.10) | collective-permute-done | bytes 229408 | tf_op jit(solution)/shard_map/ppermute | solution.py:495
  141.1 0.1 add_convert_fusion
  141.2 0.8 pad_maximum_fusion.2
  (17 shorter events, 0.1 us)
Async XLA Ops:
  0.0 33.5 %collective-permute-start.2 = (bf16[576,8192]{1,0:T(8,128)(2,1)}, bf16[576,8192]{1,0:T(8,128)(2,1)}, u32[]{:S(2)}, u32[]{:S(2)}) collective-permute-start(bf16[576,8192]{1,0:T(8,128)(2,1)} %bitcast.31), channel_id=1, source_target_pairs={{0,4},{4,0},{8,12},{12,8},{1,5},{5,1},{9,13},{13,9},{2,6},{6,2},{1... | collective-permute-start | bytes 28311560 | tf_op jit(solution)/shard_map/ppermute | solution.py:443
  0.5 30.8 %collective-permute-start = (s32[1,64]{1,0:T(1,128)}, s32[1,64]{1,0:T(1,128)S(1)}, u32[]{:S(2)}, u32[]{:S(2)}) collective-permute-start(s32[1,64]{1,0:T(1,128)} %param.9), channel_id=1, source_target_pairs={{0,8},{4,12},{8,0},{12,4},{1,9},{5,13},{9,1},{13,5},{2,10},{6,14},... | collective-permute-start | bytes 776 | tf_op jit(solution)/shard_map/ppermute | solution.py:444
  2.9 29.4 %collective-permute-start.1 = (bf16[128,3072]{1,0:T(8,128)(2,1)}, bf16[128,3072]{1,0:T(8,128)(2,1)}, u32[]{:S(2)}, u32[]{:S(2)}) collective-permute-start(bf16[128,3072]{1,0:T(8,128)(2,1)} %refs_1_.1), channel_id=1, source_target_pairs={{0,8},{4,12},{8,0},{12,4},{1,9},{5,13},{9,1},{13,5},{2,10},{6,14},... | collective-permute-start | bytes 2359304 | tf_op jit(solution)/shard_map/ppermute | solution.py:442
  9.2 1.6 %copy-start.2 = (bf16[16,128,512]{2,1,0:T(8,128)(2,1)S(1)}, bf16[16,128,512]{2,1,0:T(8,128)(2,1)}, u32[]{:S(2)}) copy-start(bf16[16,128,512]{2,1,0:T(8,128)(2,1)} %refs_3_.3) | copy-start | bytes 6291460
  10.8 1.6 %copy-start.4 = (bf16[16,512,128]{2,1,0:T(8,128)(2,1)S(1)}, bf16[16,512,128]{2,1,0:T(8,128)(2,1)}, u32[]{:S(2)}) copy-start(bf16[16,512,128]{2,1,0:T(8,128)(2,1)} %refs_6_.3) | copy-start | bytes 6291460
  12.4 1.1 copy-start.6
  13.5 17.8 %copy-start.7 = (s32[1,64]{1,0:T(1,128)S(1)}, s32[1,64]{1,0:T(1,128)}, u32[]{:S(2)}) copy-start(s32[1,64]{1,0:T(1,128)} %param.9) | copy-start | bytes 772
  31.2 2.3 %copy-start.3 = (bf16[16,128,512]{2,1,0:T(8,128)(2,1)S(1)}, bf16[16,128,512]{2,1,0:T(8,128)(2,1)}, u32[]{:S(2)}) copy-start(bf16[16,128,512]{2,1,0:T(8,128)(2,1)} %refs_3_.3) | copy-start | bytes 6291460
  33.5 1.6 %copy-start.5 = (bf16[16,512,128]{2,1,0:T(8,128)(2,1)S(1)}, bf16[16,512,128]{2,1,0:T(8,128)(2,1)}, u32[]{:S(2)}) copy-start(bf16[16,512,128]{2,1,0:T(8,128)(2,1)} %refs_6_.3) | copy-start | bytes 6291460
  58.9 18.6 %collective-permute-start.3 = (bf16[128,2176]{1,0:T(8,128)(2,1)S(1)}, bf16[128,2176]{1,0:T(8,128)(2,1)S(1)}, u32[]{:S(2)}, u32[]{:S(2)}) collective-permute-start(bf16[128,2176]{1,0:T(8,128)(2,1)S(1)} %shard_map.75.sent_ref), channel_id=1, source_target_pairs={{0,8},{4,12},{8,0},{12,4},{1,9},{5,13},{9,1},{13,5},{2,10},{6,14},... | collective-permute-start | bytes 1671176 | tf_op jit(solution)/shard_map/ppermute | solution.py:471
  78.6 4.6 %collective-permute-start.4 = (bf16[128,2048]{1,0:T(8,128)(2,1)S(1)}, bf16[128,2048]{1,0:T(8,128)(2,1)S(1)}, u32[]{:S(2)}, u32[]{:S(2)}) collective-permute-start(bf16[128,2048]{1,0:T(8,128)(2,1)S(1)} %shard_map.78), channel_id=1, source_target_pairs={{0,4},{4,0},{8,12},{12,8},{1,5},{5,1},{9,13},{13,9},{2,6},{6,2},{1... | collective-permute-start | bytes 1572872 | tf_op jit(solution)/shard_map/ppermute | solution.py:484
  81.6 14.6 %collective-permute-start.8 = (bf16[128,2176]{1,0:T(8,128)(2,1)S(1)}, bf16[128,2176]{1,0:T(8,128)(2,1)S(1)}, u32[]{:S(2)}, u32[]{:S(2)}) collective-permute-start(bf16[128,2176]{1,0:T(8,128)(2,1)S(1)} %shard_map.77.sent_ref), channel_id=1, source_target_pairs={{0,8},{4,12},{8,0},{12,4},{1,9},{5,13},{9,1},{13,5},{2,10},{6,14},... | collective-permute-start | bytes 1671176 | tf_op jit(solution)/shard_map/ppermute | solution.py:471
  83.2 3.1 %copy-start = (bf16[2048,1792]{1,0:T(8,128)(2,1)S(1)}, bf16[2048,1792]{1,0:T(8,128)(2,1)}, u32[]{:S(2)}) copy-start(bf16[2048,1792]{1,0:T(8,128)(2,1)} %w_ref.3) | copy-start | bytes 22020100
  97.3 4.0 %collective-permute-start.9 = (bf16[128,2048]{1,0:T(8,128)(2,1)S(1)}, bf16[128,2048]{1,0:T(8,128)(2,1)S(1)}, u32[]{:S(2)}, u32[]{:S(2)}) collective-permute-start(bf16[128,2048]{1,0:T(8,128)(2,1)S(1)} %shard_map.80), channel_id=1, source_target_pairs={{0,4},{4,0},{8,12},{12,8},{1,5},{5,1},{9,13},{13,9},{2,6},{6,2},{1... | collective-permute-start | bytes 1572872 | tf_op jit(solution)/shard_map/ppermute | solution.py:484
  97.4 15.4 %collective-permute-start.7 = (bf16[64,1792]{1,0:T(8,128)(2,1)S(1)}, bf16[64,1792]{1,0:T(8,128)(2,1)S(1)}, u32[]{:S(2)}, u32[]{:S(2)}) collective-permute-start(bf16[64,1792]{1,0:T(8,128)(2,1)S(1)} %get-tuple-element.42), channel_id=1, source_target_pairs={{0,3},{1,0},{2,1},{3,2},{4,7},{5,4},{6,5},{7,6},{8,11},{9,8},{10,9... | collective-permute-start | bytes 688136 | tf_op jit(solution)/shard_map/ppermute | solution.py:495
  101.3 12.9 %collective-permute-start.6 = (bf16[64,1792]{1,0:T(8,128)(2,1)S(1)}, bf16[64,1792]{1,0:T(8,128)(2,1)S(1)}, u32[]{:S(2)}, u32[]{:S(2)}) collective-permute-start(bf16[64,1792]{1,0:T(8,128)(2,1)S(1)} %get-tuple-element.43), channel_id=1, source_target_pairs={{0,1},{1,2},{2,3},{3,0},{4,5},{5,6},{6,7},{7,4},{8,9},{9,10},{10,1... | collective-permute-start | bytes 688136 | tf_op jit(solution)/shard_map/ppermute | solution.py:495
  101.4 20.5 %collective-permute-start.5 = (bf16[64,1792]{1,0:T(8,128)(2,1)S(1)}, bf16[64,1792]{1,0:T(8,128)(2,1)S(1)}, u32[]{:S(2)}, u32[]{:S(2)}) collective-permute-start(bf16[64,1792]{1,0:T(8,128)(2,1)S(1)} %get-tuple-element.44), channel_id=1, source_target_pairs={{0,2},{1,3},{2,0},{3,1},{4,6},{5,7},{6,4},{7,5},{8,10},{9,11},{10,... | collective-permute-start | bytes 688136 | tf_op jit(solution)/shard_map/ppermute | solution.py:495
  102.4 3.1 %copy-start.1 = (bf16[2048,1792]{1,0:T(8,128)(2,1)S(1)}, bf16[2048,1792]{1,0:T(8,128)(2,1)}, u32[]{:S(2)}) copy-start(bf16[2048,1792]{1,0:T(8,128)(2,1)} %w_ref.3) | copy-start | bytes 22020100
  109.3 12.8 %collective-permute-start.12 = (bf16[64,1792]{1,0:T(8,128)(2,1)S(1)}, bf16[64,1792]{1,0:T(8,128)(2,1)S(1)}, u32[]{:S(2)}, u32[]{:S(2)}) collective-permute-start(bf16[64,1792]{1,0:T(8,128)(2,1)S(1)} %get-tuple-element.40), channel_id=1, source_target_pairs={{0,3},{1,0},{2,1},{3,2},{4,7},{5,4},{6,5},{7,6},{8,11},{9,8},{10,9... | collective-permute-start | bytes 688136 | tf_op jit(solution)/shard_map/ppermute | solution.py:495
  112.2 15.7 %collective-permute-start.11 = (bf16[64,1792]{1,0:T(8,128)(2,1)S(1)}, bf16[64,1792]{1,0:T(8,128)(2,1)S(1)}, u32[]{:S(2)}, u32[]{:S(2)}) collective-permute-start(bf16[64,1792]{1,0:T(8,128)(2,1)S(1)} %get-tuple-element.41), channel_id=1, source_target_pairs={{0,1},{1,2},{2,3},{3,0},{4,5},{5,6},{6,7},{7,4},{8,9},{9,10},{10,1... | collective-permute-start | bytes 688136 | tf_op jit(solution)/shard_map/ppermute | solution.py:495
  112.8 28.3 %collective-permute-start.10 = (bf16[64,1792]{1,0:T(8,128)(2,1)S(1)}, bf16[64,1792]{1,0:T(8,128)(2,1)S(1)}, u32[]{:S(2)}, u32[]{:S(2)}) collective-permute-start(bf16[64,1792]{1,0:T(8,128)(2,1)S(1)} %get-tuple-element.39), channel_id=1, source_target_pairs={{0,2},{1,3},{2,0},{3,1},{4,6},{5,7},{6,4},{7,5},{8,10},{9,11},{10,... | collective-permute-start | bytes 688136 | tf_op jit(solution)/shard_map/ppermute | solution.py:495

commit v5 on v2

v5 whole, which is shorter than its diff:
```python
import functools
import math

import jax
import jax.numpy as jnp
from jax import lax
from jax.experimental import pallas as pl
from jax.experimental.pallas import tpu as pltpu
from jax.sharding import PartitionSpec as P

BT = 64
WIDE = 128
CHUNK = 8
SMALL = 4
FIRST = 64
NEVER = -1e30
FAR = 1 << 30
MIB = 1024 * 1024
META = 128


def attend_kernel(
    blocks_held, cuts,
    meta, query_hbm, wa_hbm, own_hbm, sib_hbm, wv_hbm, *refs,
):
    outs, refs = refs[: len(cuts)], refs[len(cuts) :]
    raw, queries, kt, q_full, wa, wv, *refs = refs
    accs, stores, peaks, totals = refs[0:2], refs[2:4], refs[4:6], refs[6:8]
    wa_sem, wv_sem, q_sem, kv_sem = refs[8:]

    tokens = queries.shape[0]
    heads, nope, lat = wa.shape
    width = kt.shape[0]
    vd = wv.shape[2]
    head_width = nope + width - lat
    fold = head_width ** -0.5 * math.log2(math.e)
    full, count, first, mine = meta[64], meta[65], meta[66], meta[67]
    plain_chunks = full // CHUNK
    done = plain_chunks * CHUNK
    small_chunks = (count - done + SMALL - 1) // SMALL
    slots = done + small_chunks * SMALL

    q_copy = pltpu.make_async_copy(query_hbm, queries, q_sem)
    wa_copy = pltpu.make_async_copy(wa_hbm, wa, wa_sem)
    wv_copy = pltpu.make_async_copy(wv_hbm, wv, wv_sem)
    q_copy.start()
    wa_copy.start()

    def fetch(i, _):
        block = meta[i]
        col = pl.multiple_of((block % blocks_held) // 2 * WIDE, WIDE)
        here = (block // blocks_held == mine) | (i >= count)

        @pl.when(here)
        def _():
            pltpu.make_async_copy(own_hbm.at[:, pl.ds(col, WIDE)], raw.at[i], kv_sem).start()

        @pl.when(jnp.logical_not(here))
        def _():
            pltpu.make_async_copy(sib_hbm.at[:, pl.ds(col, WIDE)], raw.at[i], kv_sem).start()

        return 0

    lax.fori_loop(0, slots, fetch, 0)
    wv_copy.start()
    q_copy.wait()
    wa_copy.wait()
    for h in range(heads):
        base = h * head_width
        latent_part = jnp.dot(
            queries[:, base : base + nope], wa[h], preferred_element_type=jnp.float32
        )
        rows = slice(h * tokens, (h + 1) * tokens)
        q_full[rows, 0:lat] = (latent_part * fold).astype(jnp.bfloat16)
        turned = queries[:, base + nope : base + head_width].astype(jnp.float32)
        q_full[rows, lat:width] = (turned * fold).astype(jnp.bfloat16)

    def land(i, _):
        pltpu.make_async_copy(own_hbm.at[:, pl.ds(0, WIDE)], raw.at[0], kv_sem).wait()
        return 0

    lax.fori_loop(0, slots, land, 0)

    def pair(i, _):
        left_odd = meta[2 * i] % 2 == 1
        right_odd = meta[2 * i + 1] % 2 == 1
        target = pl.ds(pl.multiple_of(i * WIDE, WIDE), WIDE)
        lane = lax.broadcasted_iota(jnp.int32, (width, WIDE), 1)

        def swap(x):
            return jnp.concatenate([x[:, BT:], x[:, :BT]], axis=1)

        @pl.when(jnp.logical_not(left_odd) & right_odd)
        def _():
            kt[:, target] = jnp.where(lane < BT, raw[2 * i], raw[2 * i + 1])

        @pl.when(left_odd & right_odd)
        def _():
            kt[:, target] = jnp.where(lane < BT, swap(raw[2 * i]), raw[2 * i + 1])

        @pl.when(jnp.logical_not(left_odd | right_odd))
        def _():
            kt[:, target] = jnp.where(lane < BT, raw[2 * i], swap(raw[2 * i + 1]))

        @pl.when(left_odd & jnp.logical_not(right_odd))
        def _():
            kt[:, target] = swap(jnp.where(lane < BT, raw[2 * i + 1], raw[2 * i]))

        return 0

    lax.fori_loop(0, slots // 2, pair, 0)
    wv_copy.wait()

    tile = accs[0].shape[0]
    tile_heads = tile // tokens
    lane = lax.broadcasted_iota(jnp.int32, (tokens, 128), 1)

    def row_pair(r, lse_tile):
        row0 = r * 2 * tile
        bases = [pl.multiple_of(row0, tile), pl.multiple_of(row0 + tile, tile)]
        for i in range(2):
            accs[i][...] = jnp.zeros_like(accs[i])
            peaks[i][...] = jnp.full(peaks[i].shape, NEVER, jnp.float32)
            totals[i][...] = jnp.zeros_like(totals[i])

        def score(i, key0, n):
            stores[i][:, 0 : n * BT] = jnp.dot(
                q_full[pl.ds(bases[i], tile), :], kt[:, pl.ds(key0, n * BT)],
                preferred_element_type=jnp.float32,
            )

        def soften(i, n, visible):
            scores = stores[i][:, 0 : n * BT]
            if visible is not None:
                scores = jnp.where(
                    visible[None], scores.reshape(tile_heads, tokens, n * BT), NEVER
                ).reshape(tile, n * BT)
            peak = peaks[i][...]
            new_peak = jnp.maximum(peak, jnp.max(scores, axis=1, keepdims=True))
            peaks[i][...] = new_peak
            raised = jnp.exp2(scores - new_peak[:, 0:1])
            keep_share = jnp.exp2(peak - new_peak)
            total = totals[i][...] * keep_share
            for k in range(n * BT // 128):
                total = total + raised[:, k * 128 : (k + 1) * 128]
            totals[i][...] = total
            return raised.astype(jnp.bfloat16), keep_share[:, 0:1]

        def mix(i, key0, n, raised, keep_share):
            accs[i][...] = accs[i][...] * keep_share + lax.dot_general(
                raised, kt[0:lat, pl.ds(key0, n * BT)], (((1,), (1,)), ((), ())),
                preferred_element_type=jnp.float32,
            )

        def chunk(n, start, masked, c, _):
            key0 = pl.multiple_of(start + c * n * BT, 128)
            key1 = pl.multiple_of(key0 + n * BT, 128)
            visible = None
            if masked:
                block0 = key0 // BT
                column = lax.broadcasted_iota(jnp.int32, (tokens, n * BT), 1)
                position = jnp.zeros((tokens, n * BT), jnp.int32)
                for b in range(n):
                    at = jnp.where(
                        block0 + b < full, 0,
                        jnp.where(block0 + b < count, meta[block0 + b] * BT, FAR),
                    )
                    position = jnp.where(column // BT == b, at + column % BT, position)
                query = first + lax.broadcasted_iota(jnp.int32, (tokens, n * BT), 0)
                visible = position <= query
            score(1, key0, n)
            raised, share = soften(0, n, visible)
            mix(0, key0, n, raised, share)
            score(0, key1, n)
            raised, share = soften(1, n, visible)
            mix(1, key0, n, raised, share)
            return 0

        @pl.when(plain_chunks > 0)
        def _():
            score(0, 0, CHUNK)

        @pl.when(plain_chunks == 0)
        def _():
            score(0, 0, SMALL)

        lax.fori_loop(0, plain_chunks, functools.partial(chunk, CHUNK, 0, False), 0)
        lax.fori_loop(0, small_chunks, functools.partial(chunk, SMALL, done * BT, True), 0)

        for i in range(2):
            total = jnp.maximum(jnp.sum(totals[i][...], axis=1, keepdims=True), 1e-30)
            lse = peaks[i][:, 0:1] + jnp.log2(total)
            scale = 1.0 / total
            for k in range(tile_heads):
                h = (r * 2 + i) * tile_heads + k
                rows = slice(k * tokens, (k + 1) * tokens)
                mixed = (accs[i][rows, :] * scale[rows, :]).astype(jnp.bfloat16)
                out = jnp.dot(mixed, wv[h], preferred_element_type=jnp.float32)
                out = out.astype(jnp.bfloat16)
                for ref, (low, high) in zip(outs, cuts):
                    ref[:, pl.ds(pl.multiple_of(h * vd, vd), vd)] = out[low:high, :]
                lse_tile = place_log(lse_tile, lane, h, lse[rows, :])
        return lse_tile

    lse_tile = lax.fori_loop(
        0, heads * tokens // (2 * tile), row_pair, jnp.zeros((tokens, 128), jnp.float32)
    ).astype(jnp.bfloat16)
    for ref, (low, high) in zip(outs, cuts):
        ref[:, heads * vd :] = lse_tile[low:high, :]


def place_log(tile, lane, h, value):
    high = value.astype(jnp.bfloat16).astype(jnp.float32)
    middle = (value - high).astype(jnp.bfloat16).astype(jnp.float32)
    low = value - high - middle
    tile = jnp.where(lane == h, high, tile)
    tile = jnp.where(lane == h + 32, middle, tile)
    return jnp.where(lane == h + 64, low, tile)


def attend(meta, queries, own, sib, w_absorb, w_value, slots, row_tile, cuts):
    tokens = queries.shape[0]
    heads, nope, lat = w_absorb.shape
    vd = w_value.shape[2]
    width = own.shape[0]
    slots = -(-slots // SMALL) * SMALL
    rows = heads * tokens
    tile = min(row_tile, rows // 2)
    keys = slots * BT * 2 // 3
    any_space = pl.BlockSpec(memory_space=pl.ANY)
    vmem = pl.BlockSpec(memory_space=pltpu.VMEM)
    smem = pl.BlockSpec(memory_space=pltpu.SMEM)
    return pl.pallas_call(
        functools.partial(attend_kernel, own.shape[1] // BT, cuts),
        out_shape=[
            jax.ShapeDtypeStruct((high - low, heads * vd + 128), jnp.bfloat16) for low, high in cuts
        ],
        in_specs=[smem] + [any_space] * 5,
        out_specs=[vmem] * len(cuts),
        scratch_shapes=[
            pltpu.VMEM((slots, width, WIDE), jnp.bfloat16),
            pltpu.VMEM(queries.shape, jnp.bfloat16),
            pltpu.VMEM((width, (slots + CHUNK) * BT), jnp.bfloat16),
            pltpu.VMEM((rows, width), jnp.bfloat16),
            pltpu.VMEM(w_absorb.shape, jnp.bfloat16),
            pltpu.VMEM(w_value.shape, jnp.bfloat16),
            *[pltpu.VMEM((tile, lat), jnp.float32)] * 2,
            *[pltpu.VMEM((tile, CHUNK * BT), jnp.float32)] * 2,
            *[pltpu.VMEM((tile, 128), jnp.float32)] * 4,
            *[pltpu.SemaphoreType.DMA] * 4,
        ],
        compiler_params=pltpu.CompilerParams(vmem_limit_bytes=50 * MIB),
        cost_estimate=pl.CostEstimate(
            flops=2 * rows * keys * (width + lat),
            bytes_accessed=2 * keys * width * 2,
            transcendentals=rows * keys,
        ),
    )(meta.reshape(-1), queries, w_absorb, own, sib, w_value)


def read_log(ref, rows, heads):
    tail = ref[rows, ref.shape[1] - 128 :].astype(jnp.float32)
    return tail[:, 0:heads] + tail[:, 32 : 32 + heads] + tail[:, 64 : 64 + heads]


def merge(parts, heads, out, out_rows, with_log):
    vd = (parts[0][0].shape[1] - 128) // heads
    logs = [read_log(ref, rows, heads) for ref, rows in parts]
    peak = functools.reduce(jnp.maximum, logs)
    shares = [jnp.exp2(value - peak) for value in logs]
    total = functools.reduce(jnp.add, shares)
    norm = 1.0 / total
    for h in range(heads):
        columns = slice(h * vd, (h + 1) * vd)
        mixed = sum(
            ref[rows, columns].astype(jnp.float32) * (share * norm)[:, h : h + 1]
            for (ref, rows), share in zip(parts, shares)
        )
        out[out_rows, columns] = mixed.astype(jnp.bfloat16)
    if with_log:
        log = peak + jnp.log2(total)
        tokens = log.shape[0]
        lane = lax.broadcasted_iota(jnp.int32, (tokens, 128), 1)
        tile = jnp.zeros((tokens, 128), jnp.float32)
        for h in range(heads):
            tile = place_log(tile, lane, h, log[:, h : h + 1])
        out[out_rows, heads * vd :] = tile.astype(jnp.bfloat16)


def small_call(kernel, shape, operands):
    vmem = pl.BlockSpec(memory_space=pltpu.VMEM)
    return pl.pallas_call(
        kernel,
        out_shape=jax.ShapeDtypeStruct(shape, jnp.bfloat16),
        in_specs=[vmem] * len(operands),
        out_specs=vmem,
        compiler_params=pltpu.CompilerParams(vmem_limit_bytes=16 * MIB),
        cost_estimate=pl.CostEstimate(flops=1, bytes_accessed=1, transcendentals=0),
    )(*operands)


def combine(partials, heads, with_log):
    tokens, columns = partials[0].shape

    def kernel(*refs):
        rows = slice(0, tokens)
        merge([(ref, rows) for ref in refs[:-1]], heads, refs[-1], rows, with_log)

    return small_call(kernel, (tokens, columns if with_log else columns - 128), partials)


def settle(near, far_near, far, got, low, heads):
    rows, columns = far.shape
    cut, whole = slice(low, low + rows), slice(0, rows)

    def kernel(near_ref, far_near_ref, far_ref, got_ref, out):
        merge([(near_ref, cut), (got_ref, whole)], heads, out, whole, False)
        merge([(far_near_ref, cut), (far_ref, whole)], heads, out, slice(rows, 2 * rows), False)

    return small_call(kernel, (2 * rows, columns - 128), [near, far_near, far, got])


def project_kernel(steps, mine_ref, other_ref, w_hbm, o_ref, w, acc, sems):
    depth = w.shape[0] // steps
    copies = [
        pltpu.make_async_copy(w_hbm.at[k * depth : (k + 1) * depth, :], w.at[k * depth : (k + 1) * depth, :], sems.at[k])
        for k in range(steps)
    ]
    for copy in copies:
        copy.start()
    for k, copy in enumerate(copies):
        rows = slice(k * depth, (k + 1) * depth)
        x = jnp.concatenate([mine_ref[:, rows], other_ref[:, rows]], axis=0)
        copy.wait()
        part = jnp.dot(x, w[rows, :], preferred_element_type=jnp.float32)
        if k > 0:
            part = acc[...] + part
        if k < steps - 1:
            acc[...] = part
        else:
            o_ref[...] = part.astype(jnp.bfloat16)


def project(mine, other, w):
    rows, depth = mine.shape
    columns = w.shape[1]
    steps = 4
    vmem = pl.BlockSpec(memory_space=pltpu.VMEM)
    return pl.pallas_call(
        functools.partial(project_kernel, steps),
        out_shape=jax.ShapeDtypeStruct((2 * rows, columns), jnp.bfloat16),
        in_specs=[vmem, vmem, pl.BlockSpec(memory_space=pltpu.HBM)],
        out_specs=vmem,
        scratch_shapes=[
            pltpu.VMEM(w.shape, jnp.bfloat16),
            pltpu.VMEM((2 * rows, columns), jnp.float32),
            pltpu.SemaphoreType.DMA((steps,)),
        ],
        compiler_params=pltpu.CompilerParams(vmem_limit_bytes=50 * MIB),
        cost_estimate=pl.CostEstimate(flops=1, bytes_accessed=1, transcendentals=0),
    )(mine, other, w)


def list_kernel(owners, held, tokens, turns, flags, me_ref, offset_ref, *refs):
    outs = refs[-len(turns) :]
    refs = refs[: -len(turns)]
    me = me_ref[0]
    count = refs[0].shape[1]
    row = lax.broadcasted_iota(jnp.int32, (count, count), 0)
    col = lax.broadcasted_iota(jnp.int32, (count, count), 1)
    before = (row < col).astype(jnp.float32)
    lane = lax.broadcasted_iota(jnp.int32, (1, META), 1)
    for j, turn in enumerate(turns):
        blocks = refs[min(j, len(refs) - 1)][...]
        start = offset_ref[0] + lax.rem(me - 2 * turn + owners, owners) * tokens
        here = jnp.zeros(blocks.shape, jnp.bool_)
        for wanted, holder in zip(flags[j], (me, me ^ 1)):
            if wanted:
                here = here | ((blocks >= holder * held) & (blocks < (holder + 1) * held))
        seen = blocks * BT + (BT - 1) <= start
        full = jnp.where(here & seen, 1.0, 0.0)
        edge = jnp.where(
            here & jnp.logical_not(seen) & (blocks * BT <= start + tokens - 1), 1.0, 0.0
        )
        n_full = jnp.sum(full, axis=1, keepdims=True)
        n_edge = jnp.sum(edge, axis=1, keepdims=True)
        full_rank = jnp.dot(full, before, preferred_element_type=jnp.float32)
        edge_rank = jnp.dot(edge, before, preferred_element_type=jnp.float32) + n_full
        slot = jnp.where(full > 0, full_rank, jnp.where(edge > 0, edge_rank, -1.0)).astype(jnp.int32)
        hits = jnp.where(row == jnp.broadcast_to(slot, (count, count)), 1.0, 0.0)
        listed = lax.dot_general(
            (blocks // 16).astype(jnp.float32), hits, (((1,), (1,)), ((), ())), preferred_element_type=jnp.float32
        ) * 16.0 + lax.dot_general(
            (blocks % 16).astype(jnp.float32), hits, (((1,), (1,)), ((), ())), preferred_element_type=jnp.float32
        )
        line = jnp.concatenate(
            [listed, jnp.zeros((1, META - count), jnp.float32)], axis=1
        ).astype(jnp.int32)
        line = jnp.where(lane == count, n_full.astype(jnp.int32), line)
        line = jnp.where(lane == count + 1, (n_full + n_edge).astype(jnp.int32), line)
        line = jnp.where(lane == count + 2, start, line)
        line = jnp.where(lane == count + 3, me, line)
        outs[j][...] = line


def make_lists(rows, turns, flags, me, span_offset, owners, held, tokens):
    smem = pl.BlockSpec(memory_space=pltpu.SMEM)
    vmem = pl.BlockSpec(memory_space=pltpu.VMEM)
    return pl.pallas_call(
        functools.partial(list_kernel, owners, held, tokens, turns, flags),
        out_shape=[jax.ShapeDtypeStruct((1, META), jnp.int32)] * len(turns),
        in_specs=[smem, smem] + [vmem] * len(rows),
        out_specs=[vmem] * len(turns),
        cost_estimate=pl.CostEstimate(flops=1, bytes_accessed=1, transcendentals=0),
    )(me.reshape(1), span_offset, *rows)


def body(queries, latent, selection, span_offset, w_absorb, w_value, w_out):
    owners = lax.axis_size("ctx")
    groups = lax.axis_size("head")
    me = lax.axis_index("ctx")
    column = lax.axis_index("head")
    chips = owners // 2
    depth = 3 * selection.shape[1] // (2 * owners)
    heads = w_absorb.shape[0]
    tokens = queries.shape[0]
    sibling = [(i, i ^ 1) for i in range(owners)]
    turns = range(1, chips)
    ahead = {t: [(i, (i + 2 * t) % owners) for i in range(owners)] for t in turns}
    back = {t: [(i, (i - 2 * t) % owners) for i in range(owners)] for t in turns}
    own = latent.T

    held = latent.shape[0] // BT

    far_queries = {t: lax.ppermute(queries, "ctx", ahead[t]) for t in turns}
    sib = lax.ppermute(own, "ctx", sibling)
    far_rows = {t: lax.ppermute(selection, "ctx", ahead[t]) for t in turns}
    lists = functools.partial(
        make_lists, me=me, span_offset=span_offset, owners=owners, held=held, tokens=tokens
    )
    near_meta, side_meta = lists([selection], [0, 0], [(True, False), (False, True)])
    weights = (w_absorb, w_value)
    whole = [(0, tokens)]
    (near,) = attend(near_meta, queries, own, own, *weights, depth, 1024, whole)
    (side,) = attend(
        side_meta, queries, own, sib, *weights, depth, 1024, whole
    )
    near = combine([near, side], heads, True)
    cuts = [(0, FIRST), (FIRST, tokens)] if chips == 2 else whole
    if chips == 2:
        far_near = lax.ppermute(near, "ctx", ahead[1])
        (meta,) = lists([far_rows[1]], [1], [(True, True)])
        meta, near = lax.optimization_barrier((meta, near))
        fars = attend(meta, far_queries[1], own, sib, *weights, 2 * depth, 1024, cuts)
        *fars, far_near = lax.optimization_barrier((*fars, far_near))
        gots = []
        for far in fars:
            if gots:
                far, gots[-1] = lax.optimization_barrier((far, gots[-1]))
            gots.append(lax.ppermute(far, "ctx", ahead[1]))

        def mine_of(c):
            return settle(near, far_near, fars[c], gots[c], cuts[c][0], heads)
    else:
        arrived = [near]
        for t in turns:
            (meta,) = lists([far_rows[t]], [t], [(True, True)])
            (far,) = attend(meta, far_queries[t], own, sib, *weights, 2 * depth, 1024, whole)
            arrived.append(lax.ppermute(far, "ctx", back[t]))
        mine = combine(arrived, heads, False)
        mine = jnp.concatenate([mine] + [lax.ppermute(mine, "ctx", ahead[t]) for t in turns], axis=0)

        def mine_of(c):
            return mine

    outputs = []
    for c, (low, high) in enumerate(cuts):
        piece = high - low
        mine = mine_of(c)
        shares = project(mine, lax.ppermute(mine, "ctx", sibling), w_out)

        def share_of(block):
            turn = (me // 2 - block // 2) % chips
            place = (me + block) % 2 * chips + turn
            return lax.dynamic_slice_in_dim(shares, place * piece, piece, 0)

        steps = sorted(range(1, groups), key=lambda s: -min(s, groups - s))
        moved = [
            lax.ppermute(
                share_of((column + s) % groups), "head", [(i, (i + s) % groups) for i in range(groups)]
            )
            for s in steps
        ]
        arrived = [share_of(column)] + moved
        outputs.append(sum(a.astype(jnp.float32) for a in arrived).astype(jnp.bfloat16))
    return jnp.concatenate(outputs, axis=0)


def solution(mesh):
    placed = (
        P(("groups", "ctx"), "head"),
        P(("groups", "ctx"), None),
        P(("groups", "ctx"), None),
        P("groups"),
        P("head", None, None),
        P("head", None, None),
        P("head", "ctx"),
    )
    return jax.shard_map(
        body, mesh=mesh, in_specs=placed, out_specs=P(("groups", "head"), "ctx"), check_vma=False
    )
```

time: 148 us -> 129 us (0.87)
  the two profiles are of different devices: /device:TPU:17 before, /device:TPU:0 now
where the time goes in v5:
time: 129 us; the launch traced here: 128 us
  Pallas kernels  65.7 us (51%)
  waiting for transfers between devices  41.7 us (32%)
  starting transfers between devices  13.8 us (11%)
  local copies, waits for them, and re-layouts  4.53 us (4%)
    pallas_call x3, Pallas kernels, attend(): pl.pallas_call(functools.partial(attend_kernel, own.shape[1] // BT, cuts)...  51.1 us
    ppermute x6, waiting for transfers between devices, body(): lax.ppermute(share_of((column + s) % groups), 'head', [(i, (i + s) % grou...  29.3 us
    ppermute x2, waiting for transfers between devices, body(): gots.append(lax.ppermute(far, 'ctx', ahead[1]))  12.3 us
    ppermute x6, starting transfers between devices, body(): lax.ppermute(share_of((column + s) % groups), 'head', [(i, (i + s) % grou...  9.58 us
    pallas_call x2, Pallas kernels, project(): pl.pallas_call(functools.partial(project_kernel, steps), out_shape=jax.Sh...  8.34 us
    unnamed x14, local copies, waits for them, and re-layouts  4.42 us
    pallas_call x3, Pallas kernels, small_call(): pl.pallas_call(kernel, out_shape=jax.ShapeDtypeStruct(shape, jnp.bfloat16...  3.3 us
    pallas_call x2, Pallas kernels, make_lists(): pl.pallas_call(functools.partial(list_kernel, owners, held, tokens, turns...  2.91 us
  transfers between devices with their start and end apart: 14, of which 6 were waited for; matrix products, arithmetic and copies ran while one was open for 0% of the time, Pallas kernels for 51%

profile of v5, /device:TPU:0, one launch (start us, length us, event | category | flops | bytes accessed | tf_op | source)
XLA Modules:
  0.0 127.8 jit_solution(8656251690007459076)
XLA Ops:
  0.0 0.5 collective-permute-start.1
  0.5 2.5 %collective-permute-start = (s32[1,64]{1,0:T(1,128)}, s32[1,64]{1,0:T(1,128)S(1)}, u32[]{:S(2)}, u32[]{:S(2)}) collective-permute-start(s32[1,64]{1,0:T(1,128)} %refs_0_.1), channel_id=1, source_target_pairs={{0,8},{4,12},{8,0},{12,4},{1,9},{5,13},{9,1},{13,5},{2,10},{6,14},... | collective-permute-start | bytes 776 | tf_op jit(solution)/shard_map/ppermute | solution.py:437
  2.9 0.1 collective-permute-start.2
  3.7 1.6 %shard_map.74 = (s32[1,128]{1,0:T(1,128)}, s32[1,128]{1,0:T(1,128)}) custom-call(s32[1]{0:T(128)} %bitcast.me_ref, s32[1]{0:T(128)S(6)} %copy.8.offset_ref, s32[1,64]{1,0:T(1,128)} %refs_0_.1), custom_call_target="tpu_custom_call" | custom-call | flops 1 | bytes 1 | tf_op jit(solution)/shard_map/pallas_call | solution.py:409
  5.2 0.0 copy-start
  5.2 1.6 %copy-done = bf16[16,128,512]{2,1,0:T(8,128)(2,1)S(1)} copy-done((bf16[16,128,512]{2,1,0:T(8,128)(2,1)S(1)}, bf16[16,128,512]{2,1,0:T(8,128)(2,1)}, u32[]{:S(2)}) %copy-start) | copy-done | bytes 2097176
  6.8 0.0 copy-start.2
  6.8 1.1 copy-done.2
  7.9 0.0 copy-start.4
  7.9 0.6 copy-done.4
  8.5 0.0 copy-start.3
  8.6 13.4 %shard_map.75.refs_0_ = bf16[128,2176]{1,0:T(8,128)(2,1)S(1)} custom-call(s32[128]{0:T(128)S(1)} %bitcast.6, bf16[128,3072]{1,0:T(8,128)(2,1)S(1)} %copy-done.2, bf16[16,128,512]{2,1,0:T(8,128)(2,1)S(1)} %copy-done, bf16[576,8192]{1,0:T(8,128)(2,1)} %bitcast.9, bf16[576,8192]{1,0:T(8,128)(2,1)} %bitcast.10, bf16[16,512,128]{2,1,0:T(8,128)(2,1)} %wv_hbm.5), custom_call_target="tpu_custom_call" | custom-call | flops 4563402752 | bytes 2359296 | tf_op jit(solution)/shard_map/pallas_call | solution.py:233
  21.9 0.0 collective-permute-done.1.sib_hbm
  21.9 0.0 copy-done.3
  21.9 0.0 copy-start.1
  22.0 15.1 %shard_map.76.refs_1_ = bf16[128,2176]{1,0:T(8,128)(2,1)S(1)} custom-call(s32[128]{0:T(128)S(1)} %bitcast.5, bf16[128,3072]{1,0:T(8,128)(2,1)S(1)} %copy-done.2, bf16[16,128,512]{2,1,0:T(8,128)(2,1)S(1)} %copy-done, bf16[576,8192]{1,0:T(8,128)(2,1)} %bitcast.11, bf16[576,8192]{1,0:T(8,128)(2,1)} %collective-permute-done.1.sib_hbm, bf16[16,512,128]{2,1,0:T(8,128)(2,1)} %wv_hbm.5), custom_call_target="tpu_custom_call" | custom-call | flops 4563402752 | bytes 2359296 | tf_op jit(solution)/shard_map/pallas_call | solution.py:233
  37.1 0.0 collective-permute-done.refs_0_
  37.1 0.0 copy-start.6
  37.1 0.5 copy-done.6
  37.6 1.4 %shard_map.73 = s32[1,128]{1,0:T(1,128)} custom-call(s32[1]{0:T(128)} %bitcast.me_ref, s32[1]{0:T(128)S(6)} %copy.8.offset_ref, s32[1,64]{1,0:T(1,128)} %copy-done.6), custom_call_target="tpu_custom_call" | custom-call | flops 1 | bytes 1 | tf_op jit(solution)/shard_map/pallas_call | solution.py:409
  38.9 1.2 shard_map.77.near_ref
  40.2 0.1 collective-permute-start.3
  40.2 0.0 collective-permute-done.2.query_hbm
  40.3 0.0 copy-done.1
  40.3 0.0 copy-start.5
  40.3 0.6 copy-done.5
  40.8 22.7 %shard_map.78 = (bf16[64,2176]{1,0:T(8,128)(2,1)S(1)}, bf16[64,2176]{1,0:T(8,128)(2,1)S(1)}) custom-call(s32[128]{0:T(128)S(1)} %bitcast.7, bf16[128,3072]{1,0:T(8,128)(2,1)} %collective-permute-done.2.query_hbm, bf16[16,128,512]{2,1,0:T(8,128)(2,1)S(1)} %copy-done.1, bf16[576,8192]{1,0:T(8,128)(2,1)} %bitcast.12, ...), custom_call_target="tpu_custom_call" | custom-call | flops 9126805504 | bytes 4718592 | tf_op jit(solution)/shard_map/pallas_call | solution.py:233
  63.5 0.0 collective-permute-done.3.far_near_ref
  63.5 0.7 collective-permute-start.4
  64.2 7.1 %collective-permute-done.4.got_ref = bf16[64,2176]{1,0:T(8,128)(2,1)S(1)} collective-permute-done((bf16[64,2176]{1,0:T(8,128)(2,1)S(1)}, bf16[64,2176]{1,0:T(8,128)(2,1)S(1)}, u32[]{:S(2)}, u32[]{:S(2)}) %collective-permute-start.4) | collective-permute-done | bytes 278560 | tf_op jit(solution)/shard_map/ppermute | solution.py:460
  71.3 0.4 collective-permute-start.9
  71.6 1.0 shard_map.79.mine_ref
  72.7 0.1 collective-permute-start.5
  72.8 5.3 %collective-permute-done.9.got_ref = bf16[64,2176]{1,0:T(8,128)(2,1)S(1)} collective-permute-done((bf16[64,2176]{1,0:T(8,128)(2,1)S(1)}, bf16[64,2176]{1,0:T(8,128)(2,1)S(1)}, u32[]{:S(2)}, u32[]{:S(2)}) %collective-permute-start.9) | collective-permute-done | bytes 278560 | tf_op jit(solution)/shard_map/ppermute | solution.py:460
  78.0 1.0 shard_map.81.mine_ref
  79.1 0.1 collective-permute-start.10
  79.4 0.0 collective-permute-done.5.other_ref
  79.4 4.2 %shard_map.80 = bf16[256,1792]{1,0:T(8,128)(2,1)S(1)} custom-call(bf16[128,2048]{1,0:T(8,128)(2,1)S(1)} %shard_map.79.mine_ref, bf16[128,2048]{1,0:T(8,128)(2,1)S(1)} %collective-permute-done.5.other_ref, bf16[2048,1792]{1,0:T(8,128)(2,1)} %w_hbm.3), custom_call_target="tpu_custom_call" | custom-call | flops 1 | bytes 1 | tf_op jit(solution)/shard_map/pallas_call | solution.py:349
  83.6 0.1 constant_dynamic-slice_fusion.5
  83.7 3.7 %collective-permute-start.8 = (bf16[64,1792]{1,0:T(8,128)(2,1)S(1)}, bf16[64,1792]{1,0:T(8,128)(2,1)S(1)}, u32[]{:S(2)}, u32[]{:S(2)}) collective-permute-start(bf16[64,1792]{1,0:T(8,128)(2,1)S(1)} %get-tuple-element.28), channel_id=1, source_target_pairs={{0,3},{1,0},{2,1},{3,2},{4,7},{5,4},{6,5},{7,6},{8,11},{9,8},{10,9... | collective-permute-start | bytes 688136 | tf_op jit(solution)/shard_map/ppermute | solution.py:489
  87.3 0.0 collective-permute-start.7
  87.3 1.0 collective-permute-start.6
  88.4 0.0 collective-permute-done.10.other_ref
  88.4 4.2 %shard_map.82 = bf16[256,1792]{1,0:T(8,128)(2,1)S(1)} custom-call(bf16[128,2048]{1,0:T(8,128)(2,1)S(1)} %shard_map.81.mine_ref, bf16[128,2048]{1,0:T(8,128)(2,1)S(1)} %collective-permute-done.10.other_ref, bf16[2048,1792]{1,0:T(8,128)(2,1)} %w_hbm.3), custom_call_target="tpu_custom_call" | custom-call | flops 1 | bytes 1 | tf_op jit(solution)/shard_map/pallas_call | solution.py:349
  92.5 0.1 constant_dynamic-slice_fusion.2
  92.6 2.9 %collective-permute-start.13 = (bf16[64,1792]{1,0:T(8,128)(2,1)S(1)}, bf16[64,1792]{1,0:T(8,128)(2,1)S(1)}, u32[]{:S(2)}, u32[]{:S(2)}) collective-permute-start(bf16[64,1792]{1,0:T(8,128)(2,1)S(1)} %get-tuple-element.31), channel_id=1, source_target_pairs={{0,3},{1,0},{2,1},{3,2},{4,7},{5,4},{6,5},{7,6},{8,11},{9,8},{10,9... | collective-permute-start | bytes 688136 | tf_op jit(solution)/shard_map/ppermute | solution.py:489
  95.5 0.6 collective-permute-start.12
  96.1 0.0 collective-permute-done.8
  96.1 1.4 %collective-permute-start.11 = (bf16[64,1792]{1,0:T(8,128)(2,1)S(1)}, bf16[64,1792]{1,0:T(8,128)(2,1)S(1)}, u32[]{:S(2)}, u32[]{:S(2)}) collective-permute-start(bf16[64,1792]{1,0:T(8,128)(2,1)S(1)} %get-tuple-element.30), channel_id=1, source_target_pairs={{0,2},{1,3},{2,0},{3,1},{4,6},{5,7},{6,4},{7,5},{8,10},{9,11},{10,... | collective-permute-start | bytes 688136 | tf_op jit(solution)/shard_map/ppermute | solution.py:489
  97.5 1.7 %collective-permute-done.7 = bf16[64,1792]{1,0:T(8,128)(2,1)S(1)} collective-permute-done((bf16[64,1792]{1,0:T(8,128)(2,1)S(1)}, bf16[64,1792]{1,0:T(8,128)(2,1)S(1)}, u32[]{:S(2)}, u32[]{:S(2)}) %collective-permute-start.7) | collective-permute-done | bytes 229408 | tf_op jit(solution)/shard_map/ppermute | solution.py:489
  99.2 9.0 %collective-permute-done.6 = bf16[64,1792]{1,0:T(8,128)(2,1)S(1)} collective-permute-done((bf16[64,1792]{1,0:T(8,128)(2,1)S(1)}, bf16[64,1792]{1,0:T(8,128)(2,1)S(1)}, u32[]{:S(2)}, u32[]{:S(2)}) %collective-permute-start.6) | collective-permute-done | bytes 229408 | tf_op jit(solution)/shard_map/ppermute | solution.py:489
  108.3 0.1 add_convert_fusion.1
  108.4 0.0 collective-permute-done.13
  108.4 5.6 %collective-permute-done.12 = bf16[64,1792]{1,0:T(8,128)(2,1)S(1)} collective-permute-done((bf16[64,1792]{1,0:T(8,128)(2,1)S(1)}, bf16[64,1792]{1,0:T(8,128)(2,1)S(1)}, u32[]{:S(2)}, u32[]{:S(2)}) %collective-permute-start.12) | collective-permute-done | bytes 229408 | tf_op jit(solution)/shard_map/ppermute | solution.py:489
  114.0 12.9 %collective-permute-done.11 = bf16[64,1792]{1,0:T(8,128)(2,1)S(1)} collective-permute-done((bf16[64,1792]{1,0:T(8,128)(2,1)S(1)}, bf16[64,1792]{1,0:T(8,128)(2,1)S(1)}, u32[]{:S(2)}, u32[]{:S(2)}) %collective-permute-start.11) | collective-permute-done | bytes 229408 | tf_op jit(solution)/shard_map/ppermute | solution.py:489
  126.9 0.1 add_convert_fusion
  127.0 0.8 pad_maximum_fusion
Async XLA Ops:
  0.0 21.9 %collective-permute-start.1 = (bf16[576,8192]{1,0:T(8,128)(2,1)}, bf16[576,8192]{1,0:T(8,128)(2,1)}, u32[]{:S(2)}, u32[]{:S(2)}) collective-permute-start(bf16[576,8192]{1,0:T(8,128)(2,1)} %bitcast.8), channel_id=1, source_target_pairs={{0,4},{4,0},{8,12},{12,8},{1,5},{5,1},{9,13},{13,9},{2,6},{6,2},{1... | collective-permute-start | bytes 28311560 | tf_op jit(solution)/shard_map/ppermute | solution.py:436
  0.5 36.6 %collective-permute-start = (s32[1,64]{1,0:T(1,128)}, s32[1,64]{1,0:T(1,128)S(1)}, u32[]{:S(2)}, u32[]{:S(2)}) collective-permute-start(s32[1,64]{1,0:T(1,128)} %refs_0_.1), channel_id=1, source_target_pairs={{0,8},{4,12},{8,0},{12,4},{1,9},{5,13},{9,1},{13,5},{2,10},{6,14},... | collective-permute-start | bytes 776 | tf_op jit(solution)/shard_map/ppermute | solution.py:437
  2.9 37.3 %collective-permute-start.2 = (bf16[128,3072]{1,0:T(8,128)(2,1)}, bf16[128,3072]{1,0:T(8,128)(2,1)}, u32[]{:S(2)}, u32[]{:S(2)}) collective-permute-start(bf16[128,3072]{1,0:T(8,128)(2,1)} %query_hbm.3), channel_id=1, source_target_pairs={{0,8},{4,12},{8,0},{12,4},{1,9},{5,13},{9,1},{13,5},{2,10},{6,14},... | collective-permute-start | bytes 2359304 | tf_op jit(solution)/shard_map/ppermute | solution.py:435
  5.2 1.6 %copy-start = (bf16[16,128,512]{2,1,0:T(8,128)(2,1)S(1)}, bf16[16,128,512]{2,1,0:T(8,128)(2,1)}, u32[]{:S(2)}) copy-start(bf16[16,128,512]{2,1,0:T(8,128)(2,1)} %wa_hbm.5) | copy-start | bytes 6291460
  6.8 1.1 copy-start.2
  7.9 0.6 copy-start.4
  8.5 13.4 %copy-start.3 = (s32[1,128]{1,0:T(1,128)S(1)}, s32[1,128]{1,0:T(1,128)}, u32[]{:S(2)}) copy-start(s32[1,128]{1,0:T(1,128)} %get-tuple-element.17) | copy-start | bytes 1540
  21.9 18.3 %copy-start.1 = (bf16[16,128,512]{2,1,0:T(8,128)(2,1)S(1)}, bf16[16,128,512]{2,1,0:T(8,128)(2,1)}, u32[]{:S(2)}) copy-start(bf16[16,128,512]{2,1,0:T(8,128)(2,1)} %wa_hbm.5) | copy-start | bytes 6291460
  37.1 0.5 copy-start.6
  40.2 23.4 %collective-permute-start.3 = (bf16[128,2176]{1,0:T(8,128)(2,1)S(1)}, bf16[128,2176]{1,0:T(8,128)(2,1)S(1)}, u32[]{:S(2)}, u32[]{:S(2)}) collective-permute-start(bf16[128,2176]{1,0:T(8,128)(2,1)S(1)} %shard_map.77.near_ref), channel_id=1, source_target_pairs={{0,8},{4,12},{8,0},{12,4},{1,9},{5,13},{9,1},{13,5},{2,10},{6,14},... | collective-permute-start | bytes 1671176 | tf_op jit(solution)/shard_map/ppermute | solution.py:451
  40.3 0.6 copy-start.5
  63.5 7.7 %collective-permute-start.4 = (bf16[64,2176]{1,0:T(8,128)(2,1)S(1)}, bf16[64,2176]{1,0:T(8,128)(2,1)S(1)}, u32[]{:S(2)}, u32[]{:S(2)}) collective-permute-start(bf16[64,2176]{1,0:T(8,128)(2,1)S(1)} %get-tuple-element.23.far_ref), channel_id=1, source_target_pairs={{0,8},{4,12},{8,0},{12,4},{1,9},{5,13},{9,1},{13,5},{2,10},{6,14},... | collective-permute-start | bytes 835592 | tf_op jit(solution)/shard_map/ppermute | solution.py:460
  71.3 6.8 %collective-permute-start.9 = (bf16[64,2176]{1,0:T(8,128)(2,1)S(1)}, bf16[64,2176]{1,0:T(8,128)(2,1)S(1)}, u32[]{:S(2)}, u32[]{:S(2)}) collective-permute-start(bf16[64,2176]{1,0:T(8,128)(2,1)S(1)} %get-tuple-element.26.far_ref), channel_id=1, source_target_pairs={{0,8},{4,12},{8,0},{12,4},{1,9},{5,13},{9,1},{13,5},{2,10},{6,14},... | collective-permute-start | bytes 835592 | tf_op jit(solution)/shard_map/ppermute | solution.py:460
  72.7 6.7 %collective-permute-start.5 = (bf16[128,2048]{1,0:T(8,128)(2,1)S(1)}, bf16[128,2048]{1,0:T(8,128)(2,1)S(1)}, u32[]{:S(2)}, u32[]{:S(2)}) collective-permute-start(bf16[128,2048]{1,0:T(8,128)(2,1)S(1)} %shard_map.79.mine_ref), channel_id=1, source_target_pairs={{0,4},{4,0},{8,12},{12,8},{1,5},{5,1},{9,13},{13,9},{2,6},{6,2},{1... | collective-permute-start | bytes 1572872 | tf_op jit(solution)/shard_map/ppermute | solution.py:480
  79.1 9.3 %collective-permute-start.10 = (bf16[128,2048]{1,0:T(8,128)(2,1)S(1)}, bf16[128,2048]{1,0:T(8,128)(2,1)S(1)}, u32[]{:S(2)}, u32[]{:S(2)}) collective-permute-start(bf16[128,2048]{1,0:T(8,128)(2,1)S(1)} %shard_map.81.mine_ref), channel_id=1, source_target_pairs={{0,4},{4,0},{8,12},{12,8},{1,5},{5,1},{9,13},{13,9},{2,6},{6,2},{1... | collective-permute-start | bytes 1572872 | tf_op jit(solution)/shard_map/ppermute | solution.py:480
  83.7 12.4 %collective-permute-start.8 = (bf16[64,1792]{1,0:T(8,128)(2,1)S(1)}, bf16[64,1792]{1,0:T(8,128)(2,1)S(1)}, u32[]{:S(2)}, u32[]{:S(2)}) collective-permute-start(bf16[64,1792]{1,0:T(8,128)(2,1)S(1)} %get-tuple-element.28), channel_id=1, source_target_pairs={{0,3},{1,0},{2,1},{3,2},{4,7},{5,4},{6,5},{7,6},{8,11},{9,8},{10,9... | collective-permute-start | bytes 688136 | tf_op jit(solution)/shard_map/ppermute | solution.py:489
  87.3 11.9 %collective-permute-start.7 = (bf16[64,1792]{1,0:T(8,128)(2,1)S(1)}, bf16[64,1792]{1,0:T(8,128)(2,1)S(1)}, u32[]{:S(2)}, u32[]{:S(2)}) collective-permute-start(bf16[64,1792]{1,0:T(8,128)(2,1)S(1)} %get-tuple-element.29), channel_id=1, source_target_pairs={{0,1},{1,2},{2,3},{3,0},{4,5},{5,6},{6,7},{7,4},{8,9},{9,10},{10,1... | collective-permute-start | bytes 688136 | tf_op jit(solution)/shard_map/ppermute | solution.py:489
  87.3 20.9 %collective-permute-start.6 = (bf16[64,1792]{1,0:T(8,128)(2,1)S(1)}, bf16[64,1792]{1,0:T(8,128)(2,1)S(1)}, u32[]{:S(2)}, u32[]{:S(2)}) collective-permute-start(bf16[64,1792]{1,0:T(8,128)(2,1)S(1)} %get-tuple-element.27), channel_id=1, source_target_pairs={{0,2},{1,3},{2,0},{3,1},{4,6},{5,7},{6,4},{7,5},{8,10},{9,11},{10,... | collective-permute-start | bytes 688136 | tf_op jit(solution)/shard_map/ppermute | solution.py:489
  92.6 15.8 %collective-permute-start.13 = (bf16[64,1792]{1,0:T(8,128)(2,1)S(1)}, bf16[64,1792]{1,0:T(8,128)(2,1)S(1)}, u32[]{:S(2)}, u32[]{:S(2)}) collective-permute-start(bf16[64,1792]{1,0:T(8,128)(2,1)S(1)} %get-tuple-element.31), channel_id=1, source_target_pairs={{0,3},{1,0},{2,1},{3,2},{4,7},{5,4},{6,5},{7,6},{8,11},{9,8},{10,9... | collective-permute-start | bytes 688136 | tf_op jit(solution)/shard_map/ppermute | solution.py:489
  95.5 18.6 %collective-permute-start.12 = (bf16[64,1792]{1,0:T(8,128)(2,1)S(1)}, bf16[64,1792]{1,0:T(8,128)(2,1)S(1)}, u32[]{:S(2)}, u32[]{:S(2)}) collective-permute-start(bf16[64,1792]{1,0:T(8,128)(2,1)S(1)} %get-tuple-element.32), channel_id=1, source_target_pairs={{0,1},{1,2},{2,3},{3,0},{4,5},{5,6},{6,7},{7,4},{8,9},{9,10},{10,1... | collective-permute-start | bytes 688136 | tf_op jit(solution)/shard_map/ppermute | solution.py:489
  96.1 30.8 %collective-permute-start.11 = (bf16[64,1792]{1,0:T(8,128)(2,1)S(1)}, bf16[64,1792]{1,0:T(8,128)(2,1)S(1)}, u32[]{:S(2)}, u32[]{:S(2)}) collective-permute-start(bf16[64,1792]{1,0:T(8,128)(2,1)S(1)} %get-tuple-element.30), channel_id=1, source_target_pairs={{0,2},{1,3},{2,0},{3,1},{4,6},{5,7},{6,4},{7,5},{8,10},{9,11},{10,... | collective-permute-start | bytes 688136 | tf_op jit(solution)/shard_map/ppermute | solution.py:489
